TPU v7x, 128 devices: a whole 4x4x4 slice. The times are simulated.
128 devices in a mesh: dp: 8 (over x, core), wide: 16 (over z, y).
Axes of the slice: x: 4, y: 4, z: 4, core: 2. Of those that a mesh axis runs over, the one named last changes fastest.
Arguments:
- volume: bfloat16 [8, 32, 16, 16, 128], P('dp', 'wide'), may hold values from -6 to 6
- kernel_five: bfloat16 [3, 3, 3, 128, 256], replicated, may hold values from -0.109375 to 0.109375
- kernel_six: bfloat16 [3, 3, 3, 256, 256], replicated, may hold values from -0.078125 to 0.078125
- cotangent: bfloat16 [8, 8, 4, 4, 256], P('dp', None, None, None, 'wide'), may hold values from -6 to 6
Outputs:
- next_input: bfloat16 [8, 8, 4, 4, 256], P('dp', None, None, None, 'wide')
- kernel_five_grad: float32 [3, 3, 3, 128, 256], P(None, None, None, None, 'wide')
- kernel_six_grad: float32 [3, 3, 3, 256, 256], P(None, None, None, None, 'wide')
All inputs are finite; a program needn't handle non-finite values.
Results may differ from a plain program's by a relative error of at most 0.01.
Values may be sent and summed in bfloat16 or wider, within the bound.
No kernel may reach another device: no remote copies, remote signals or barrier semaphores. Data moves between devices by JAX's collectives and lax.ppermute only.
A program may use at most 128 MiB of HBM per device.

v0:
```python
import jax
import jax.numpy as jnp
from jax import lax
from jax.sharding import PartitionSpec as P

SLOPE = 0.3


def padded_2(block, sides, width):
    for axis, dim in sides:
        count = lax.axis_size(axis)
        forward = [(i, i + 1) for i in range(count - 1)]
        backward = [(target, source) for source, target in forward]
        low = lax.ppermute(
            lax.slice_in_dim(block, block.shape[dim] - width, None, axis=dim), axis, forward
        )
        high = lax.ppermute(lax.slice_in_dim(block, 0, width, axis=dim), axis, backward)
        block = jnp.concatenate([low, block, high], axis=dim)
    return block


def activate(value):
    return SLOPE * value + (1.0 - SLOPE) * value * jax.nn.sigmoid(value)


def slope_of(value):
    sigma = jax.nn.sigmoid(value)
    return SLOPE + (1.0 - SLOPE) * (sigma + value * sigma * (1.0 - sigma))


def tap_window(padded, depth_tap, row_tap, planes, side):
    columns = [
        padded[
            depth_tap : depth_tap + planes, row_tap : row_tap + side, col_tap : col_tap + side, :
        ]
        for col_tap in range(3)
    ]
    return jnp.concatenate(columns, axis=-1).reshape(planes * side * side, -1)


def convolve(padded, kernel, planes, side):
    channels = kernel.shape[3]
    filters = kernel.shape[4]
    result = jnp.zeros((planes * side * side, filters), jnp.float32)
    for depth_tap in range(3):
        for row_tap in range(3):
            window = tap_window(padded, depth_tap, row_tap, planes, side)
            taps = kernel[depth_tap, row_tap].reshape(3 * channels, filters)
            result = result + jnp.dot(window, taps, preferred_element_type=jnp.float32)
    return result


def convolve_flipped(padded, kernel, planes, side):
    channels = kernel.shape[3]
    filters = kernel.shape[4]
    result = jnp.zeros((filters, planes * side * side), jnp.float32)
    for depth_tap in range(3):
        for row_tap in range(3):
            window = tap_window(padded, depth_tap, row_tap, planes, side)
            taps = kernel[depth_tap, row_tap].reshape(3 * channels, filters)
            result = result + lax.dot_general(
                taps, window, (((0,), (1,)), ((), ())), preferred_element_type=jnp.float32
            )
    return result


def kernel_grad(padded, grad, planes, side):
    channels = padded.shape[3]
    pieces = []
    for depth_tap in range(3):
        for row_tap in range(3):
            window = tap_window(padded, depth_tap, row_tap, planes, side)
            pieces.append(
                lax.dot_general(
                    window, grad, (((0,), (0,)), ((), ())), preferred_element_type=jnp.float32
                )
            )
    return jnp.stack(pieces).reshape(3, 3, 3, channels, grad.shape[1])


def kernel_grad_flipped(padded, grad_rows, planes, side):
    channels = padded.shape[3]
    pieces = []
    for depth_tap in range(3):
        for row_tap in range(3):
            window = tap_window(padded, depth_tap, row_tap, planes, side)
            pieces.append(
                lax.dot_general(
                    window, grad_rows, (((0,), (1,)), ((), ())), preferred_element_type=jnp.float32
                )
            )
    return jnp.stack(pieces).reshape(3, 3, 3, channels, grad_rows.shape[0])


def shrink(values, planes, side):
    channels = values.shape[-1]
    return values.reshape(planes // 2, 2, side // 2, 2, side // 2, 2, channels).mean(axis=(1, 3, 5))


def shrink_rows(values, planes, side):
    filters = values.shape[0]
    return values.reshape(filters, planes // 2, 2, side // 2, 2, side // 2, 2).mean(axis=(2, 4, 6))


def expand(values):
    grown = jnp.broadcast_to(
        values[:, None, :, None, :, None, :],
        (values.shape[0], 2, values.shape[1], 2, values.shape[2], 2, values.shape[3]),
    )
    return grown.reshape(-1, values.shape[3])


def expand_rows(values):
    filters, planes, rows, cols = values.shape
    grown = jnp.broadcast_to(
        values[:, :, None, :, None, :, None], (filters, planes, 2, rows, 2, cols, 2)
    )
    return grown.reshape(filters, -1)


def pad_grid(values):
    return jnp.pad(values, ((1, 1), (1, 1), (1, 1), (0, 0)))


def shards(volume, kernel_five, kernel_six, cotangent):
    planes = volume.shape[1]
    side = volume.shape[2]
    half = side // 2
    mid_channels = kernel_five.shape[4]
    share = cotangent.shape[4]
    position = lax.axis_index("wide")
    slab = volume[0]
    rimmed = padded_2(slab, (("wide", 0),), 1)
    padded_five = jnp.pad(rimmed, ((0, 0), (1, 1), (1, 1), (0, 0)))
    pre_five = convolve(padded_five, kernel_five, planes, side)
    pooled_own = shrink(activate(pre_five), planes, side).astype(jnp.bfloat16)
    pooled = lax.all_gather(pooled_own, "wide", axis=0, tiled=True)
    depth_half = pooled.shape[0]
    kernel_own = lax.dynamic_slice_in_dim(kernel_six, position * share, share, 4)
    padded_six = pad_grid(pooled)
    pre_six = convolve_flipped(padded_six, kernel_own, depth_half, half)
    next_rows = shrink_rows(activate(pre_six), depth_half, half)
    next_input = next_rows.transpose(1, 2, 3, 0).astype(jnp.bfloat16)
    upstream = cotangent[0].transpose(3, 0, 1, 2).astype(jnp.float32)
    grad_rows = (expand_rows(upstream) * 0.125 * slope_of(pre_six)).astype(jnp.bfloat16)
    weight_six = kernel_grad_flipped(padded_six, grad_rows, depth_half, half)
    grad_box = jnp.pad(
        grad_rows.reshape(share, depth_half, half, half), ((0, 0), (1, 1), (1, 1), (1, 1))
    )
    partial_grad = jnp.zeros((depth_half * half * half, mid_channels), jnp.float32)
    for depth_tap in range(3):
        for row_tap in range(3):
            for col_tap in range(3):
                piece = grad_box[
                    :,
                    2 - depth_tap : 2 - depth_tap + depth_half,
                    2 - row_tap : 2 - row_tap + half,
                    2 - col_tap : 2 - col_tap + half,
                ].reshape(share, -1)
                partial_grad = partial_grad + lax.dot_general(
                    piece,
                    kernel_own[depth_tap, row_tap, col_tap],
                    (((0,), (1,)), ((), ())),
                    preferred_element_type=jnp.float32,
                )
    partial_grad = partial_grad.reshape(depth_half, half, half, mid_channels)
    grad_pooled = lax.psum_scatter(partial_grad, "wide", scatter_dimension=0, tiled=True)
    grad_five = (expand(grad_pooled) * 0.125 * slope_of(pre_five)).astype(jnp.bfloat16)
    weight_five = kernel_grad(padded_five, grad_five, planes, side)
    summed_five, summed_six = lax.psum((weight_five, weight_six), "dp")
    share_five = lax.psum_scatter(summed_five, "wide", scatter_dimension=4, tiled=True)
    return (next_input.reshape((1,) + next_input.shape), share_five, summed_six)


def solution(mesh):
    in_specs = (P("dp", "wide", None, None, None), P(), P(), P("dp", None, None, None, "wide"))
    out_specs = (
        P("dp", None, None, None, "wide"),
        P(None, None, None, None, "wide"),
        P(None, None, None, None, "wide"),
    )
    return jax.shard_map(shards, mesh=mesh, in_specs=in_specs, out_specs=out_specs, check_vma=False)
```

profile of v0, /device:TPU:1, one launch (start us, length us, event | category | flops | bytes accessed | tf_op | source)
XLA Modules:
  0.0 315.6 jit_solution(5492530422099596012)
XLA Ops:
  8.1 4.0 %collective-permute-start = (bf16[1,16,16,128]{3,2,1,0:T(8,128)(2,1)S(1)}, bf16[1,16,16,128]{3,2,1,0:T(8,128)(2,1)S(1)}, u32[]{:S(2)}, u32[]{:S(2)}) collective-permute-start(bf16[1,16,16,128]{3,2,1,0:T(8,128)(2,1)S(1)} %get-tuple-element.107), channel_id=1, source_target_pairs={{0,1},{1,2},{2,3},{3,4},{4,5},{5,6},{6,7},{7,8},{8,9},{9,10},{10,1... | collective-permute-start | bytes 196616 | tf_op jit(solution)/shard_map/ppermute | solution.py:14
  12.1 1.3 collective-permute-start.1
  13.5 2.6 fusion.71
  16.1 3.3 %constant_dynamic-slice_fusion = (bf16[1,1,3,256,16]{4,3,2,1,0:T(8,128)(2,1)}, bf16[1,1,3,256,16]{4,3,2,1,0:T(8,128)(2,1)S(1)}, bf16[1,1,3,256,16]{4,3,2,1,0:T(8...) fusion(bf16[3,3,3,256,256]{4,3,2,1,0:T(8,128)(2,1)} %param.6, ...), kind=kLoop, calls=%fused_computation.227 | loop fusion | bytes 442380 | tf_op jit(solution)/shard_map/slice | solution.py:60
  24.7 1.1 multiply_add_fusion
  26.4 22.6 %all-gather = bf16[128,8,256]{2,1,0:T(8,128)(2,1)S(1)} all-gather(bf16[8,8,256]{2,1,0:T(8,128)(2,1)S(1)} %multiply_convert_fusion.3), channel_id=2, replica_groups=mesh['dp'=8,'wide'=16] {'wide'}, dimensions={0}, use_global_device_ids=true | all-gather | bytes 557056 | tf_op jit(solution)/shard_map/all_gather | solution.py:137
  49.1 2.4 pad_slice_fusion.2
  60.0 1.2 pad_slice_fusion.26
  72.3 1.4 convolution_add_fusion.1
  74.0 75.6 %reduce-scatter.7.cloned.1.call-done = f32[1,8,8,256]{3,2,1,0:T(8,128)} async-done(((f32[16,8,8,256]{3,2,1,0:T(8,128)}), f32[1,8,8,256]{3,2,1,0:T(8,128)}) %reduce-scatter.7.cloned.1.call-update) | async-done | bytes 65552
  150.4 1.1 broadcast_in_dim.5
  151.5 2.2 mul.93
  153.8 1.5 multiply_convert_fusion
  155.3 1.4 fusion.14
  156.6 1.4 fusion.13
  160.3 1.7 copy-done.13
  162.1 5.2 %copy.18 = f32[3,3,3,128,256]{3,4,2,1,0:T(8,128)} copy(f32[3,3,3,128,256]{4,3,2,1,0:T(8,128)} %bitcast.360) | data formatting | bytes 7077888 | tf_op jit(solution)/shard_map/reshape | solution.py:78
  167.3 2.5 fusion.23
  169.8 2.5 fusion.22
  178.9 2.1 reshape.264
  180.9 62.0 %reduce-scatter.5.cloned.1.call-done = f32[3,3,3,128,16]{3,4,2,1,0:T(8,128)} async-done(((f32[3,3,3,128,256]{3,4,2,1,0:T(8,128)}), f32[3,3,3,128,16]{3,4,2,1,0:T(8,128)}) %reduce-scatter.5.cloned.1.call-update) | async-done | bytes 221200 | tf_op jit(solution)/shard_map/reduce_scatter | solution.py:171
  244.2 61.3 %all-reduce.7.cloned.1.call-done = (f32[3,3,3,128,16]{3,4,2,1,0:T(8,128)}, f32[3,3,3,256,16]{3,2,4,1,0:T(4,128)}) async-done(((f32[3,3,3,128,16]{3,4,2,1,0:T(8,128)}, f32[3,3,3,256,16]{3,2,4,1,0:T(4,128)}), (f32[3,3,3,128,16]{3,4,2,1,0:T(8,128)}, f32[3,3,3,256,16]{3,2,4,1,0:T(4,128)})) %all-reduce.7.cloned.1.call-update) | async-done | bytes 663568 | tf_op jit(solution)/shard_map/psum | solution.py:170
  305.6 1.9 copy.19
  307.5 1.6 copy.38
  (194 shorter events, 36.9 us)
Async XLA Ops:
  7.2 8.9 %copy-start.49 = (bf16[1,8,4,4,16]{4,3,2,1,0:T(4,128)(2,1)S(1)}, bf16[1,8,4,4,16]{4,3,2,1,0:T(4,128)(2,1)}, u32[]{:S(2)}) copy-start(bf16[1,8,4,4,16]{4,3,2,1,0:T(4,128)(2,1)} %param.7) | copy-start | bytes 12292
  7.2 142.4 %reduce-scatter.7.cloned.1.call-start = ((), (), s32[]{:S(2)}) async-start(), calls=%async_computation.3 | async-start | bytes 1114112
  8.1 12.2 %collective-permute-start = (bf16[1,16,16,128]{3,2,1,0:T(8,128)(2,1)S(1)}, bf16[1,16,16,128]{3,2,1,0:T(8,128)(2,1)S(1)}, u32[]{:S(2)}, u32[]{:S(2)}) collective-permute-start(bf16[1,16,16,128]{3,2,1,0:T(8,128)(2,1)S(1)} %get-tuple-element.107), channel_id=1, source_target_pairs={{0,1},{1,2},{2,3},{3,4},{4,5},{5,6},{6,7},{7,8},{8,9},{9,10},{10,1... | collective-permute-start | bytes 196616 | tf_op jit(solution)/shard_map/ppermute | solution.py:14
  12.1 8.2 %collective-permute-start.1 = (bf16[1,16,16,128]{3,2,1,0:T(8,128)(2,1)S(1)}, bf16[1,16,16,128]{3,2,1,0:T(8,128)(2,1)S(1)}, u32[]{:S(2)}, u32[]{:S(2)}) collective-permute-start(bf16[1,16,16,128]{3,2,1,0:T(8,128)(2,1)S(1)} %get-tuple-element.108), channel_id=1, source_target_pairs={{1,0},{2,1},{3,2},{4,3},{5,4},{6,5},{7,6},{8,7},{9,8},{10,9},{11,1... | collective-permute-start | bytes 196616 | tf_op jit(solution)/shard_map/ppermute | solution.py:17
  16.1 4.3 %copy-start.25 = (bf16[1,2,16,16,128]{4,3,2,1,0:T(8,128)(2,1)S(1)}, bf16[1,2,16,16,128]{4,3,2,1,0:T(8,128)(2,1)}, u32[]{:S(2)}) copy-start(bf16[1,2,16,16,128]{4,3,2,1,0:T(8,128)(2,1)} %param.4) | copy-start | bytes 393220
  21.2 3.0 copy-start.14
  53.8 4.8 %copy-start = (bf16[16,8,8,768]{3,2,1,0:T(8,128)(2,1)}, bf16[16,8,8,768]{3,2,1,0:T(8,128)(2,1)S(1)}, u32[]{:S(2)}) copy-start(bf16[16,8,8,768]{3,2,1,0:T(8,128)(2,1)S(1)} %pad_maximum_fusion.7) | copy-start | bytes 4718596
  54.0 4.1 %copy-start.2 = (bf16[16,8,8,768]{3,2,1,0:T(8,128)(2,1)}, bf16[16,8,8,768]{3,2,1,0:T(8,128)(2,1)S(1)}, u32[]{:S(2)}) copy-start(bf16[16,8,8,768]{3,2,1,0:T(8,128)(2,1)S(1)} %pad_maximum_fusion.6) | copy-start | bytes 4718596
  54.1 3.4 %copy-start.5 = (bf16[16,8,8,768]{3,2,1,0:T(8,128)(2,1)}, bf16[16,8,8,768]{3,2,1,0:T(8,128)(2,1)S(1)}, u32[]{:S(2)}) copy-start(bf16[16,8,8,768]{3,2,1,0:T(8,128)(2,1)S(1)} %pad_maximum_fusion.5) | copy-start | bytes 4718596
  54.5 2.9 copy-start.11
  73.7 169.3 %reduce-scatter.5.cloned.1.call-start = ((), (), s32[]{:S(2)}) async-start(), calls=%async_computation.2 | async-start | bytes 3760128 | tf_op jit(solution)/shard_map/reduce_scatter | solution.py:171
  151.5 7.2 %copy-start.26 = (bf16[1,2,16,16,128]{4,3,2,1,0:T(8,128)(2,1)S(1)}, bf16[1,2,16,16,128]{4,3,2,1,0:T(8,128)(2,1)}, u32[]{:S(2)}) copy-start(bf16[1,2,16,16,128]{4,3,2,1,0:T(8,128)(2,1)} %param.4) | copy-start | bytes 393220
  151.5 7.2 %copy-start.44 = (bf16[2,16,16,128]{3,2,1,0:T(8,128)(2,1)S(1)}, bf16[2,16,16,128]{3,2,1,0:T(8,128)(2,1)}, u32[]{:S(2)}) copy-start(bf16[2,16,16,128]{3,2,1,0:T(8,128)(2,1)} %copy-done.43) | copy-start | bytes 393220
  153.7 4.2 %copy-start.20 = (bf16[2,16,16,384]{3,2,1,0:T(8,128)(2,1)S(1)}, bf16[2,16,16,384]{3,2,1,0:T(8,128)(2,1)}, u32[]{:S(2)}) copy-start(bf16[2,16,16,384]{3,2,1,0:T(8,128)(2,1)} %copy-done.19) | copy-start | bytes 1179652
  153.7 4.6 %copy-start.18 = (bf16[2,16,16,384]{3,2,1,0:T(8,128)(2,1)S(1)}, bf16[2,16,16,384]{3,2,1,0:T(8,128)(2,1)}, u32[]{:S(2)}) copy-start(bf16[2,16,16,384]{3,2,1,0:T(8,128)(2,1)} %copy-done.17) | copy-start | bytes 1179652
  153.8 4.9 %copy-start.46 = (bf16[2,16,16,128]{3,2,1,0:T(8,128)(2,1)S(1)}, bf16[2,16,16,128]{3,2,1,0:T(8,128)(2,1)}, u32[]{:S(2)}) copy-start(bf16[2,16,16,128]{3,2,1,0:T(8,128)(2,1)} %copy-done.45) | copy-start | bytes 393220
  155.2 3.8 %copy-start.24 = (bf16[2,16,16,384]{3,2,1,0:T(8,128)(2,1)S(1)}, bf16[2,16,16,384]{3,2,1,0:T(8,128)(2,1)}, u32[]{:S(2)}) copy-start(bf16[2,16,16,384]{3,2,1,0:T(8,128)(2,1)} %copy-done.23) | copy-start | bytes 1179652
  156.6 2.7 copy-start.22
  167.3 138.3 %all-reduce.7.cloned.1.call-start = ((), (), s32[]{:S(2)}) async-start(), calls=%async_computation.4 | async-start | bytes 1622016 | tf_op jit(solution)/shard_map/psum | solution.py:170
  167.3 5.0 %copy-start.10 = (bf16[16,8,8,768]{3,2,1,0:T(8,128)(2,1)S(1)}, bf16[16,8,8,768]{3,2,1,0:T(8,128)(2,1)}, u32[]{:S(2)}) copy-start(bf16[16,8,8,768]{3,2,1,0:T(8,128)(2,1)} %copy-done.9) | copy-start | bytes 4718596
  167.3 5.9 %copy-start.8 = (bf16[16,8,8,768]{3,2,1,0:T(8,128)(2,1)S(1)}, bf16[16,8,8,768]{3,2,1,0:T(8,128)(2,1)}, u32[]{:S(2)}) copy-start(bf16[16,8,8,768]{3,2,1,0:T(8,128)(2,1)} %copy-done.7) | copy-start | bytes 4718596
  169.8 5.3 %copy-start.6 = (bf16[16,8,8,768]{3,2,1,0:T(8,128)(2,1)S(1)}, bf16[16,8,8,768]{3,2,1,0:T(8,128)(2,1)}, u32[]{:S(2)}) copy-start(bf16[16,8,8,768]{3,2,1,0:T(8,128)(2,1)} %copy-done.5) | copy-start | bytes 4718596
  172.3 3.8 %copy-start.3 = (bf16[16,8,8,768]{3,2,1,0:T(8,128)(2,1)S(1)}, bf16[16,8,8,768]{3,2,1,0:T(8,128)(2,1)}, u32[]{:S(2)}) copy-start(bf16[16,8,8,768]{3,2,1,0:T(8,128)(2,1)} %copy-done.2) | copy-start | bytes 4718596
  173.2 3.8 %copy-start.1 = (bf16[16,8,8,768]{3,2,1,0:T(8,128)(2,1)S(1)}, bf16[16,8,8,768]{3,2,1,0:T(8,128)(2,1)}, u32[]{:S(2)}) copy-start(bf16[16,8,8,768]{3,2,1,0:T(8,128)(2,1)} %copy-done) | copy-start | bytes 4718596
  (31 other events, 49.3 us)
Sparse Core Ops, SparseCore 0:
  73.8 75.7 reduce-scatter.6
  167.4 75.5 reduce-scatter.4
  245.6 59.9 all-reduce.6
where the time goes:
time: 318 us; the launch traced here: 316 us
  waiting for transfers between devices  199 us (63%)
  matrix products  36.1 us (11%)
  local copies, waits for them, and re-layouts  31.9 us (10%)
  blocking collectives  22.6 us (7%)
  between operations  14.8 us (5%)
  starting transfers between devices  5.67 us (2%)
  other arithmetic  5.44 us (2%)
    unnamed x4, waiting for transfers between devices  75.7 us
    reduce_scatter x1, waiting for transfers between devices, shards(): lax.psum_scatter(summed_five, 'wide', scatter_dimension=4, tiled=True)  62 us
    psum x1, waiting for transfers between devices, shards(): summed_five, summed_six = lax.psum((weight_five, weight_six), 'dp')  61.3 us
    all_gather x1, blocking collectives, shards(): pooled = lax.all_gather(pooled_own, 'wide', axis=0, tiled=True)  22.6 us
    dot_general x27, matrix products, shards(): lax.dot_general(piece, kernel_own[depth_tap, row_tap, col_tap], (((0,), (...  11.5 us
    dot_general x9, matrix products, kernel_grad_flipped(): lax.dot_general(window, grad_rows, (((0,), (1,)), ((), ())), preferred_el...  11.5 us
    unnamed x102, local copies, waits for them, and re-layouts  7.82 us
  transfers between devices with their start and end apart: 5, of which 3 were waited for; matrix products, arithmetic and copies ran while one was open for 7% of the time, Pallas kernels for 0%

commit v1 on v0

v1 whole, which is shorter than its diff:
```python
import jax
import jax.numpy as jnp
from jax import lax
from jax.sharding import PartitionSpec as P

SLOPE = 0.3
HALF_TAPS = 14


def activate(value):
    return SLOPE * value + (1.0 - SLOPE) * value * jax.nn.sigmoid(value)


def slope_of(value):
    sigma = jax.nn.sigmoid(value)
    return SLOPE + (1.0 - SLOPE) * (sigma + value * sigma * (1.0 - sigma))


def shrink(values):
    planes, rows, cols, channels = values.shape
    return values.reshape(planes // 2, 2, rows // 2, 2, cols // 2, 2, channels).mean(
        axis=(1, 3, 5)
    )


def expand(values):
    planes, rows, cols, channels = values.shape
    grown = jnp.broadcast_to(
        values[:, None, :, None, :, None, :], (planes, 2, rows, 2, cols, 2, channels)
    )
    return grown.reshape(2 * planes, 2 * rows, 2 * cols, channels)


def pad_sides(values):
    return jnp.pad(values, ((0, 0), (1, 1), (1, 1), (0, 0)))


def window(padded, tap, planes, side):
    depth_tap, row_tap, col_tap = tap // 9, (tap // 3) % 3, tap % 3
    return padded[
        depth_tap : depth_tap + planes, row_tap : row_tap + side, col_tap : col_tap + side, :
    ].reshape(planes * side * side, -1)


def convolve(padded, kernel, planes, side):
    wide = jnp.concatenate([window(padded, tap, planes, side) for tap in range(27)], axis=-1)
    return jnp.dot(wide, kernel.reshape(-1, kernel.shape[-1]), preferred_element_type=jnp.float32)


def shift_perm(axis, step):
    count = lax.axis_size(axis)
    return [(i, i + step) for i in range(count) if 0 <= i + step < count]


def forward_five(slab, low, high, kernel, cot_rows):
    planes, side = slab.shape[0], slab.shape[1]
    padded = pad_sides(jnp.concatenate([low, slab, high], axis=0))
    pre = convolve(padded, kernel, planes, side)
    pooled = shrink(activate(pre).reshape(planes, side, side, -1)).astype(jnp.bfloat16)
    cells = pooled.reshape(-1, pooled.shape[-1])
    message = jnp.concatenate([cells[:, :128], cells[:, 128:], cot_rows], axis=0)
    return pre, message, padded


def to_all(message, axis):
    count = lax.axis_size(axis)
    copies = jnp.broadcast_to(message[None], (count,) + message.shape)
    return lax.all_to_all(copies, axis, split_axis=0, concat_axis=0, tiled=True)


def back_five(pooled, cot, kernel, pre_five, position):
    filters = pooled.shape[-1]
    ring = jnp.pad(pooled, ((2, 2), (0, 0), (0, 0), (0, 0)))
    near = lax.dynamic_slice_in_dim(ring, position, 5, 0)
    pre_six = convolve(pad_sides(near), kernel, 3, 8).reshape(3, 8, 8, filters)
    up = jnp.pad(expand(cot), ((1, 1), (0, 0), (0, 0), (0, 0)))
    upstream = lax.dynamic_slice_in_dim(up, position, 3, 0).astype(jnp.float32)
    grad_six = (upstream * 0.125 * slope_of(pre_six)).astype(jnp.bfloat16)
    flipped = jnp.flip(kernel, (0, 1, 2)).transpose(0, 1, 2, 4, 3)
    grad_pooled = convolve(pad_sides(grad_six), flipped, 1, 8).reshape(1, 8, 8, filters)
    grown = expand(grad_pooled).reshape(-1, filters)
    grad_five = (grown * 0.125 * slope_of(pre_five)).astype(jnp.bfloat16)
    return grad_five


def weight_five(padded, grad_five, half):
    planes = padded.shape[0] - 2
    side = padded.shape[1] - 2
    rows = grad_five.T
    pieces = [
        jnp.dot(rows, window(padded, tap, planes, side), preferred_element_type=jnp.float32)
        for tap in range(27)
    ]
    pieces.append(jnp.zeros_like(pieces[0]))
    full = jnp.stack(pieces).astype(jnp.bfloat16)
    mine = lax.dynamic_slice_in_dim(full, half * HALF_TAPS, HALF_TAPS, 0)
    theirs = lax.dynamic_slice_in_dim(full, (1 - half) * HALF_TAPS, HALF_TAPS, 0)

    def by_target(values):
        return values.reshape(HALF_TAPS, 16, 16, 128).transpose(1, 0, 2, 3)

    return by_target(mine), by_target(theirs)


def six_own(pooled, kernel, cot_own, position, half):
    depth, side = pooled.shape[0], pooled.shape[1]
    share = cot_own.shape[-1]
    own = lax.dynamic_slice_in_dim(kernel, position * share, share, 4)
    padded = jnp.pad(pooled, ((1, 1), (1, 1), (1, 1), (0, 0)))
    pre = convolve(padded, own, depth, side).reshape(depth, side, side, share)
    next_input = shrink(activate(pre)).astype(jnp.bfloat16)
    upstream = expand(cot_own).astype(jnp.float32)
    grad = (upstream * 0.125 * slope_of(pre)).astype(jnp.bfloat16).reshape(-1, share)
    rows = grad.T
    pieces = [
        jnp.dot(rows, window(padded, tap, depth, side), preferred_element_type=jnp.float32)
        for tap in range(27)
    ]
    pieces.append(jnp.zeros_like(pieces[0]))
    full = jnp.stack(pieces).astype(jnp.bfloat16)
    mine = lax.dynamic_slice_in_dim(full, half * HALF_TAPS, HALF_TAPS, 0)
    theirs = lax.dynamic_slice_in_dim(full, (1 - half) * HALF_TAPS, HALF_TAPS, 0)
    return next_input, mine, theirs


def core_swap(values):
    count = lax.axis_size("dp")
    return lax.ppermute(values, "dp", [(i, i ^ 1) for i in range(count)])


def sum_over_chips(values):
    count = lax.axis_size("dp")
    total = values.astype(jnp.float32)
    for step in range(1, count // 2):
        pairs = [(i, (i + 2 * step) % count) for i in range(count)]
        total = total + lax.ppermute(values, "dp", pairs).astype(jnp.float32)
    return total


def shards(volume, kernel_five, kernel_six, cotangent):
    position = lax.axis_index("wide")
    half = lax.axis_index("dp") % 2
    slab = volume[0]
    low = lax.ppermute(slab[-1:], "wide", shift_perm("wide", 1))
    high = lax.ppermute(slab[:1], "wide", shift_perm("wide", -1))
    cot_own = cotangent[0]
    cot_rows = cot_own.reshape(128, 16).T
    pre_five, message, padded = forward_five(slab, low, high, kernel_five, cot_rows)
    gathered = to_all(message, "wide")
    pooled = jnp.concatenate([gathered[:, :64], gathered[:, 64:128]], axis=-1)
    pooled = pooled.reshape(16, 8, 8, 256)
    cot = gathered[:, 128:].reshape(256, 128).T.reshape(8, 4, 4, 256)
    grad_five = back_five(pooled, cot, kernel_six, pre_five, position)
    mine_five, theirs_five = weight_five(padded, grad_five, half)
    next_input, mine_six, theirs_six = six_own(pooled, kernel_six, cot_own, position, half)
    got_five = core_swap(theirs_five)
    got_six = core_swap(theirs_six)
    pair_five = mine_five + got_five
    pair_six = mine_six + got_six
    spread = lax.all_to_all(pair_five, "wide", split_axis=0, concat_axis=0, tiled=True)
    depth_five = spread.astype(jnp.float32).sum(0).astype(jnp.bfloat16)
    both = jnp.concatenate([depth_five, pair_six], axis=-1)
    total = sum_over_chips(both).astype(jnp.bfloat16)
    other = core_swap(total)
    first = jnp.where(half == 0, total, other)
    second = jnp.where(half == 0, other, total)
    whole = jnp.concatenate([first, second], axis=0)[:27].astype(jnp.float32)
    out_five = whole[:, :, :128].transpose(0, 2, 1).reshape(3, 3, 3, 128, 16)
    out_six = whole[:, :, 128:].transpose(0, 2, 1).reshape(3, 3, 3, 256, 16)
    return (next_input[None], out_five, out_six)


def solution(mesh):
    in_specs = (P("dp", "wide", None, None, None), P(), P(), P("dp", None, None, None, "wide"))
    out_specs = (
        P("dp", None, None, None, "wide"),
        P(None, None, None, None, "wide"),
        P(None, None, None, None, "wide"),
    )
    return jax.shard_map(shards, mesh=mesh, in_specs=in_specs, out_specs=out_specs, check_vma=False)
```

time: 318 us -> 167 us (0.53)
  waiting for transfers between devices: 199 us -> 18.2 us
  local copies, waits for them, and re-layouts: 31.9 us -> 70.1 us
  starting transfers between devices: 5.67 us -> 32.1 us
  blocking collectives: 22.6 us -> 0 us
  between operations: 14.8 us -> 2.31 us
  other arithmetic: 5.44 us -> 10.2 us
  matrix products: 36.1 us -> 32.9 us
    unnamed x4 -> x0, waiting for transfers between devices: 75.7 us -> none
    reduce_scatter x1 -> x0, waiting for transfers between devices: 62 us -> none  [shards(): lax.psum_scatter(summed_five, 'wide', scatter_dimension=4, tiled=True)]
    psum x1 -> x0, waiting for transfers between devices: 61.3 us -> none  [shards(): summed_five, summed_six = lax.psum((weight_five, weight_six), 'dp')]
    unnamed x102 -> x218, local copies, waits for them, and re-layouts: 7.82 us -> 49 us
    all_gather x1 -> x0, blocking collectives: 22.6 us -> none  [shards(): pooled = lax.all_gather(pooled_own, 'wide', axis=0, tiled=True)]
    all_to_all x0 -> x2, starting transfers between devices: none -> 16.2 us  [the longest x1 9.25 us: to_all(): return lax.all_to_all(copies, axis, split_axis=0, concat_axis=0, tiled=True)]
    ppermute x2 -> x8, starting transfers between devices: 5.33 us -> 16 us  [the longest x3 5.78 us: core_swap(): return lax.ppermute(values, 'dp', [(i, i ^ 1) for i in range(count)])]
    all_to_all x0 -> x2, waiting for transfers between devices: none -> 10.1 us  [the longest x1 10.1 us: shards(): lax.all_to_all(pair_five, 'wide', split_axis=0, concat_axis=0, tiled=True)]
  transfers between devices with their start and end apart: 5 -> 10, of which waited for: 3 -> 5; matrix products, arithmetic and copies ran while one was open for 7% -> 36% of each run, Pallas kernels for 0% -> 0%
where the time goes in v1:
time: 167 us; the launch traced here: 166 us
  local copies, waits for them, and re-layouts  70.1 us (42%)
  matrix products  32.9 us (20%)
  starting transfers between devices  32.1 us (19%)
  waiting for transfers between devices  18.2 us (11%)
  other arithmetic  10.2 us (6%)
  between operations  2.31 us (1%)
    unnamed x218, local copies, waits for them, and re-layouts  49 us
    dot_general x4, matrix products, convolve(): jnp.dot(wide, kernel.reshape(-1, kernel.shape[-1]), preferred_element_typ...  14.7 us
    dot_general x27, matrix products, weight_five(): jnp.dot(rows, window(padded, tap, planes, side), preferred_element_type=j...  10.5 us
    all_to_all x1, waiting for transfers between devices, shards(): lax.all_to_all(pair_five, 'wide', split_axis=0, concat_axis=0, tiled=True)  10.1 us
    all_to_all x1, starting transfers between devices, to_all(): return lax.all_to_all(copies, axis, split_axis=0, concat_axis=0, tiled=True)  9.25 us
    dot_general x27, matrix products, six_own(): jnp.dot(rows, window(padded, tap, depth, side), preferred_element_type=jn...  7.79 us
    all_to_all x1, starting transfers between devices, shards(): lax.all_to_all(pair_five, 'wide', split_axis=0, concat_axis=0, tiled=True)  6.9 us
    ppermute x3, starting transfers between devices, core_swap(): return lax.ppermute(values, 'dp', [(i, i ^ 1) for i in range(count)])  5.78 us
  transfers between devices with their start and end apart: 10, of which 5 were waited for; matrix products, arithmetic and copies ran while one was open for 36% of the time, Pallas kernels for 0%

profile of v1, /device:TPU:1, one launch (start us, length us, event | category | flops | bytes accessed | tf_op | source)
XLA Modules:
  0.0 165.9 jit_solution(14195404579780980814)
XLA Ops:
  1.7 4.0 %collective-permute-start = (bf16[1,16,16,128]{3,2,1,0:T(8,128)(2,1)S(1)}, bf16[1,16,16,128]{3,2,1,0:T(8,128)(2,1)S(1)}, u32[]{:S(2)}, u32[]{:S(2)}) collective-permute-start(bf16[1,16,16,128]{3,2,1,0:T(8,128)(2,1)S(1)} %get-tuple-element.39), channel_id=1, source_target_pairs={{0,1},{1,2},{2,3},{3,4},{4,5},{5,6},{6,7},{7,8},{8,9},{9,10},{10,1... | collective-permute-start | bytes 196616 | tf_op jit(solution)/shard_map/ppermute | solution.py:144
  5.7 1.3 collective-permute-start.1
  7.8 2.9 %collective-permute-done.1 = bf16[1,16,16,128]{3,2,1,0:T(8,128)(2,1)S(1)} collective-permute-done((bf16[1,16,16,128]{3,2,1,0:T(8,128)(2,1)S(1)}, bf16[1,16,16,128]{3,2,1,0:T(8,128)(2,1)S(1)}, u32[]{:S(2)}, u32[]{:S(2)}) %collective-permute-start.1) | collective-permute-done | bytes 65568 | tf_op jit(solution)/shard_map/ppermute | solution.py:145
  14.2 1.9 %multiply_add_fusion.1 = (f32[512,256]{1,0:T(8,128)S(1)}, f32[512,256]{1,0:T(8,128)}) fusion(bf16[512,3456]{1,0:T(8,128)(2,1)S(1)} %constant_dynamic-update-slice_fusion, bf16[3456,256]{1,0:T(8,128)(2,1)S(1)} %bitcast.752), kind=kOutput, calls=%fused_computation.281 | convolution fusion | flops 906887168 | bytes 6356992 | tf_op jit(solution)/shard_map/dot_general | solution.py:47
  17.7 9.2 %all-to-all-start = ((bf16[16,144,128]{2,1,0:T(8,128)(2,1)}), bf16[16,144,128]{2,1,0:T(8,128)(2,1)S(1)}, u32[]{:S(2)}, u32[]{:S(2)}) async-start(bf16[16,144,128]{2,1,0:T(8,128)(2,1)} %broadcast_in_dim.10), calls=%async_computation | async-start | bytes 1179648 | tf_op jit(solution)/shard_map/all_to_all | solution.py:68
  27.0 6.1 %copy.129 = bf16[3,3,3,256,256]{3,4,2,1,0:T(8,128)(2,1)} copy(bf16[3,3,3,256,256]{4,3,2,1,0:T(8,128)(2,1)} %param.6) | data formatting | bytes 7077888 | tf_op args[2]
  33.1 4.2 %rev.4 = bf16[3,3,3,256,256]{3,4,2,1,0:T(8,128)(2,1)} reverse(bf16[3,3,3,256,256]{3,4,2,1,0:T(8,128)(2,1)} %copy.129), dimensions={0,1,2} | reverse | bytes 7077888 | tf_op jit(solution)/shard_map/jit(_flip)/rev | solution.py:79
  37.2 3.3 %constant_dynamic-slice_fusion.3 = bf16[3,3,3,256,16]{4,3,2,1,0:T(8,128)(2,1)} fusion(bf16[3,3,3,256,256]{4,3,2,1,0:T(8,128)(2,1)} %param.6, s32[]{:T(128)S(6)} %select_n.36), kind=kLoop, calls=%fused_computation.447 | loop fusion | bytes 442372 | tf_op jit(solution)/shard_map/dynamic_slice | solution.py:108
  64.1 3.9 %multiply_convert_fusion.2 = bf16[3,8,8,256]{3,2,1,0:T(8,128)(2,1)S(1)} fusion(bf16[3,8,8,6912]{3,2,1,0:T(8,128)(2,1)} %constant_dynamic-update-slice_fusion.54, bf16[6912,256,1,1]{1,0,3,2:T(8,128)(2,1)} %bitcast.755, s32[]{:T(128)S(6)} %select_n.39, bf16[16,8,8,256]{3,2,1,0:T(8,128)(2,1)} %reshape.512), kind=kOutput, calls=%fused_computation.401 | convolution fusion | flops 680116224 | bytes 6815748 | tf_op jit(solution)/shard_map/dot_general | solution.py:47
  70.2 1.4 mul.110
  71.7 1.4 multiply_convert_fusion.1
  73.1 1.2 fusion.1
  74.3 1.2 fusion.3
  75.6 1.2 fusion.5
  84.3 2.7 %collective-permute-start.2 = (bf16[16,14,16,128]{3,2,0,1:T(8,128)(2,1)S(1)}, bf16[16,14,16,128]{3,2,0,1:T(8,128)(2,1)S(1)}, u32[]{:S(2)}, u32[]{:S(2)}) collective-permute-start(bf16[16,14,16,128]{3,2,0,1:T(8,128)(2,1)S(1)} %bitcast.815), channel_id=1, source_target_pairs={{0,16},{16,0},{32,48},{48,32},{64,80},{80,64},{96,112},{112,96},{1... | collective-permute-start | bytes 2752520 | tf_op jit(solution)/shard_map/ppermute | solution.py:128
  111.7 8.1 %multiply_convert_fusion = (bf16[16,8,8,16]{3,2,1,0:T(8,128)(2,1)S(1)}, f32[16,8,8,16]{3,2,1,0:T(8,128)}) fusion(f32[16,8,8,16]{3,2,1,0:T(8,128)S(1)} %bitcast.816, bf16[16,8,8,6912]{3,2,1,0:T(8,128)(2,1)} %constant_dynamic-update-slice_fusion.27, bf16[6912,16,1,1]{1,0,3,2:T(8,128)(2,1)S(1)} %bitcast.762), kind=kOutput, calls=%fused_computation.277 | convolution fusion | flops 226738176 | bytes 14540800 | tf_op jit(solution)/shard_map/dot_general | solution.py:47
  126.7 1.2 copy.130
  127.8 6.9 %all-to-all-start.1 = ((bf16[16,14,16,128]{3,2,1,0:T(8,128)(2,1)}), bf16[16,14,16,128]{3,2,1,0:T(8,128)(2,1)S(1)}, u32[]{:S(2)}, u32[]{:S(2)}) async-start(bf16[16,14,16,128]{3,2,1,0:T(8,128)(2,1)} %copy.130), calls=%async_computation.1 | async-start | bytes 1835008 | tf_op jit(solution)/shard_map/all_to_all | solution.py:160
  140.1 10.1 %all-to-all-done.1 = bf16[16,14,16,128]{3,2,1,0:T(8,128)(2,1)S(1)} async-done(((bf16[16,14,16,128]{3,2,1,0:T(8,128)(2,1)}), bf16[16,14,16,128]{3,2,1,0:T(8,128)(2,1)S(1)}, u32[]{:S(2)}, u32[]{:S(2)}) %all-to-all-start.1) | async-done | bytes 917536 | tf_op jit(solution)/shard_map/all_to_all | solution.py:160
  150.4 1.3 collective-permute-start.4
  151.7 2.5 %collective-permute-start.5 = (bf16[14,16,384]{2,1,0:T(8,128)(2,1)S(1)}, bf16[14,16,384]{2,1,0:T(8,128)(2,1)S(1)}, u32[]{:S(2)}, u32[]{:S(2)}) collective-permute-start(bf16[14,16,384]{2,1,0:T(8,128)(2,1)S(1)} %pad_maximum_fusion.2), channel_id=1, source_target_pairs={{0,64},{16,80},{32,96},{48,112},{64,0},{80,16},{96,32},{112,48},{1... | collective-permute-start | bytes 516104 | tf_op jit(solution)/shard_map/ppermute | solution.py:136
  155.3 1.4 reduce_sum.31
  156.6 3.7 %collective-permute-done.5 = bf16[14,16,384]{2,1,0:T(8,128)(2,1)S(1)} collective-permute-done((bf16[14,16,384]{2,1,0:T(8,128)(2,1)S(1)}, bf16[14,16,384]{2,1,0:T(8,128)(2,1)S(1)}, u32[]{:S(2)}, u32[]{:S(2)}) %collective-permute-start.5) | collective-permute-done | bytes 172064 | tf_op jit(solution)/shard_map/ppermute | solution.py:136
  160.5 2.8 %collective-permute-start.7 = (bf16[14,16,384]{2,1,0:T(8,128)(2,1)S(1)}, bf16[14,16,384]{2,1,0:T(8,128)(2,1)S(1)}, u32[]{:S(2)}, u32[]{:S(2)}) collective-permute-start(bf16[14,16,384]{2,1,0:T(8,128)(2,1)S(1)} %add_convert_fusion), channel_id=1, source_target_pairs={{0,16},{16,0},{32,48},{48,32},{64,80},{80,64},{96,112},{112,96},{1... | collective-permute-start | bytes 516104 | tf_op jit(solution)/shard_map/ppermute | solution.py:128
  (319 shorter events, 79.8 us)
Async XLA Ops:
  0.6 13.6 %copy-start = (bf16[3,3,3,128,256]{4,3,2,1,0:T(8,128)(2,1)S(1)}, bf16[3,3,3,128,256]{4,3,2,1,0:T(8,128)(2,1)}, u32[]{:S(2)}) copy-start(bf16[3,3,3,128,256]{4,3,2,1,0:T(8,128)(2,1)} %param.5) | copy-start | bytes 5308420
  1.7 6.2 %collective-permute-start = (bf16[1,16,16,128]{3,2,1,0:T(8,128)(2,1)S(1)}, bf16[1,16,16,128]{3,2,1,0:T(8,128)(2,1)S(1)}, u32[]{:S(2)}, u32[]{:S(2)}) collective-permute-start(bf16[1,16,16,128]{3,2,1,0:T(8,128)(2,1)S(1)} %get-tuple-element.39), channel_id=1, source_target_pairs={{0,1},{1,2},{2,3},{3,4},{4,5},{5,6},{6,7},{7,8},{8,9},{9,10},{10,1... | collective-permute-start | bytes 196616 | tf_op jit(solution)/shard_map/ppermute | solution.py:144
  5.7 5.0 %collective-permute-start.1 = (bf16[1,16,16,128]{3,2,1,0:T(8,128)(2,1)S(1)}, bf16[1,16,16,128]{3,2,1,0:T(8,128)(2,1)S(1)}, u32[]{:S(2)}, u32[]{:S(2)}) collective-permute-start(bf16[1,16,16,128]{3,2,1,0:T(8,128)(2,1)S(1)} %get-tuple-element.40), channel_id=1, source_target_pairs={{1,0},{2,1},{3,2},{4,3},{5,4},{6,5},{7,6},{8,7},{9,8},{10,9},{11,1... | collective-permute-start | bytes 196616 | tf_op jit(solution)/shard_map/ppermute | solution.py:145
  17.7 23.4 %all-to-all-start = ((bf16[16,144,128]{2,1,0:T(8,128)(2,1)}), bf16[16,144,128]{2,1,0:T(8,128)(2,1)S(1)}, u32[]{:S(2)}, u32[]{:S(2)}) async-start(bf16[16,144,128]{2,1,0:T(8,128)(2,1)} %broadcast_in_dim.10), calls=%async_computation | async-start | bytes 1179648 | tf_op jit(solution)/shard_map/all_to_all | solution.py:68
  64.1 4.3 %copy-start.1 = (bf16[3,3,3,256,256]{3,4,2,1,0:T(8,128)(2,1)S(1)}, bf16[3,3,3,256,256]{3,4,2,1,0:T(8,128)(2,1)}, u32[]{:S(2)}) copy-start(bf16[3,3,3,256,256]{3,4,2,1,0:T(8,128)(2,1)} %rev.4) | copy-start | bytes 10616836
  71.7 5.1 %copy-start.46 = (bf16[2,16,16,128]{3,2,1,0:T(8,128)(2,1)S(1)}, bf16[2,16,16,128]{3,2,1,0:T(8,128)(2,1)}, u32[]{:S(2)}) copy-start(bf16[2,16,16,128]{3,2,1,0:T(8,128)(2,1)} %copy-done.45) | copy-start | bytes 393220
  71.7 5.4 %copy-start.53 = (bf16[2,16,16,128]{3,2,1,0:T(8,128)(2,1)S(1)}, bf16[2,16,16,128]{3,2,1,0:T(8,128)(2,1)}, u32[]{:S(2)}) copy-start(bf16[2,16,16,128]{3,2,1,0:T(8,128)(2,1)} %copy-done.52) | copy-start | bytes 393220
  71.7 5.7 %copy-start.44 = (bf16[2,16,16,128]{3,2,1,0:T(8,128)(2,1)S(1)}, bf16[2,16,16,128]{3,2,1,0:T(8,128)(2,1)}, u32[]{:S(2)}) copy-start(bf16[2,16,16,128]{3,2,1,0:T(8,128)(2,1)} %copy-done.43) | copy-start | bytes 393220
  71.7 6.0 %copy-start.42 = (bf16[2,16,16,128]{3,2,1,0:T(8,128)(2,1)S(1)}, bf16[2,16,16,128]{3,2,1,0:T(8,128)(2,1)}, u32[]{:S(2)}) copy-start(bf16[2,16,16,128]{3,2,1,0:T(8,128)(2,1)} %copy-done.41) | copy-start | bytes 393220
  71.7 6.3 %copy-start.40 = (bf16[2,16,16,128]{3,2,1,0:T(8,128)(2,1)S(1)}, bf16[2,16,16,128]{3,2,1,0:T(8,128)(2,1)}, u32[]{:S(2)}) copy-start(bf16[2,16,16,128]{3,2,1,0:T(8,128)(2,1)} %copy-done.39) | copy-start | bytes 393220
  71.7 6.6 %copy-start.38 = (bf16[2,16,16,128]{3,2,1,0:T(8,128)(2,1)S(1)}, bf16[2,16,16,128]{3,2,1,0:T(8,128)(2,1)}, u32[]{:S(2)}) copy-start(bf16[2,16,16,128]{3,2,1,0:T(8,128)(2,1)} %copy-done.37) | copy-start | bytes 393220
  71.7 6.9 %copy-start.36 = (bf16[2,16,16,128]{3,2,1,0:T(8,128)(2,1)S(1)}, bf16[2,16,16,128]{3,2,1,0:T(8,128)(2,1)}, u32[]{:S(2)}) copy-start(bf16[2,16,16,128]{3,2,1,0:T(8,128)(2,1)} %copy-done.35) | copy-start | bytes 393220
  71.7 7.2 %copy-start.34 = (bf16[2,16,16,128]{3,2,1,0:T(8,128)(2,1)S(1)}, bf16[2,16,16,128]{3,2,1,0:T(8,128)(2,1)}, u32[]{:S(2)}) copy-start(bf16[2,16,16,128]{3,2,1,0:T(8,128)(2,1)} %copy-done.33) | copy-start | bytes 393220
  73.1 6.2 %copy-start.32 = (bf16[2,16,16,128]{3,2,1,0:T(8,128)(2,1)S(1)}, bf16[2,16,16,128]{3,2,1,0:T(8,128)(2,1)}, u32[]{:S(2)}) copy-start(bf16[2,16,16,128]{3,2,1,0:T(8,128)(2,1)} %copy-done.31) | copy-start | bytes 393220
  73.1 6.5 %copy-start.30 = (bf16[2,16,16,128]{3,2,1,0:T(8,128)(2,1)S(1)}, bf16[2,16,16,128]{3,2,1,0:T(8,128)(2,1)}, u32[]{:S(2)}) copy-start(bf16[2,16,16,128]{3,2,1,0:T(8,128)(2,1)} %copy-done.29) | copy-start | bytes 393220
  75.5 4.7 %copy-start.28 = (bf16[2,16,16,128]{3,2,1,0:T(8,128)(2,1)S(1)}, bf16[2,16,16,128]{3,2,1,0:T(8,128)(2,1)}, u32[]{:S(2)}) copy-start(bf16[2,16,16,128]{3,2,1,0:T(8,128)(2,1)} %copy-done.27) | copy-start | bytes 393220
  84.3 41.7 %collective-permute-start.2 = (bf16[16,14,16,128]{3,2,0,1:T(8,128)(2,1)S(1)}, bf16[16,14,16,128]{3,2,0,1:T(8,128)(2,1)S(1)}, u32[]{:S(2)}, u32[]{:S(2)}) collective-permute-start(bf16[16,14,16,128]{3,2,0,1:T(8,128)(2,1)S(1)} %bitcast.815), channel_id=1, source_target_pairs={{0,16},{16,0},{32,48},{48,32},{64,80},{80,64},{96,112},{112,96},{1... | collective-permute-start | bytes 2752520 | tf_op jit(solution)/shard_map/ppermute | solution.py:128
  106.9 4.6 %copy-start.54 = (f32[8,4,4,16]{3,2,1,0:T(4,128)S(1)}, f32[8,4,4,16]{3,2,1,0:T(4,128)}, u32[]{:S(2)}) copy-start(f32[8,4,4,16]{3,2,1,0:T(4,128)} %multiply_bitcast_fusion) | copy-start | bytes 24580
  127.8 22.4 %all-to-all-start.1 = ((bf16[16,14,16,128]{3,2,1,0:T(8,128)(2,1)}), bf16[16,14,16,128]{3,2,1,0:T(8,128)(2,1)S(1)}, u32[]{:S(2)}, u32[]{:S(2)}) async-start(bf16[16,14,16,128]{3,2,1,0:T(8,128)(2,1)} %copy.130), calls=%async_computation.1 | async-start | bytes 1835008 | tf_op jit(solution)/shard_map/all_to_all | solution.py:160
  137.9 1.3 collective-permute-start.3
  150.4 6.3 %collective-permute-start.4 = (bf16[14,16,384]{2,1,0:T(8,128)(2,1)S(1)}, bf16[14,16,384]{2,1,0:T(8,128)(2,1)S(1)}, u32[]{:S(2)}, u32[]{:S(2)}) collective-permute-start(bf16[14,16,384]{2,1,0:T(8,128)(2,1)S(1)} %pad_maximum_fusion.2), channel_id=1, source_target_pairs={{0,32},{16,48},{32,64},{48,80},{64,96},{80,112},{96,0},{112,16},{1... | collective-permute-start | bytes 516104 | tf_op jit(solution)/shard_map/ppermute | solution.py:136
  151.7 8.7 %collective-permute-start.5 = (bf16[14,16,384]{2,1,0:T(8,128)(2,1)S(1)}, bf16[14,16,384]{2,1,0:T(8,128)(2,1)S(1)}, u32[]{:S(2)}, u32[]{:S(2)}) collective-permute-start(bf16[14,16,384]{2,1,0:T(8,128)(2,1)S(1)} %pad_maximum_fusion.2), channel_id=1, source_target_pairs={{0,64},{16,80},{32,96},{48,112},{64,0},{80,16},{96,32},{112,48},{1... | collective-permute-start | bytes 516104 | tf_op jit(solution)/shard_map/ppermute | solution.py:136
  154.1 6.3 %collective-permute-start.6 = (bf16[14,16,384]{2,1,0:T(8,128)(2,1)S(1)}, bf16[14,16,384]{2,1,0:T(8,128)(2,1)S(1)}, u32[]{:S(2)}, u32[]{:S(2)}) collective-permute-start(bf16[14,16,384]{2,1,0:T(8,128)(2,1)S(1)} %pad_maximum_fusion.2), channel_id=1, source_target_pairs={{0,96},{16,112},{32,0},{48,16},{64,32},{80,48},{96,64},{112,80},{1... | collective-permute-start | bytes 516104 | tf_op jit(solution)/shard_map/ppermute | solution.py:136
  160.5 3.8 %collective-permute-start.7 = (bf16[14,16,384]{2,1,0:T(8,128)(2,1)S(1)}, bf16[14,16,384]{2,1,0:T(8,128)(2,1)S(1)}, u32[]{:S(2)}, u32[]{:S(2)}) collective-permute-start(bf16[14,16,384]{2,1,0:T(8,128)(2,1)S(1)} %add_convert_fusion), channel_id=1, source_target_pairs={{0,16},{16,0},{32,48},{48,32},{64,80},{80,64},{96,112},{112,96},{1... | collective-permute-start | bytes 516104 | tf_op jit(solution)/shard_map/ppermute | solution.py:128
  (43 other events, 86.4 us)

commit v2 on v1

v2 whole, which is shorter than its diff:
```python
import jax
import jax.numpy as jnp
from jax import lax
from jax.experimental import pallas as pl
from jax.experimental.pallas import tpu as pltpu
from jax.sharding import PartitionSpec as P

SLOPE = 0.3
HALF_TAPS = 14
VMEM = pltpu.VMEM
NT = (((1,), (1,)), ((), ()))


def both_of(value):
    sigma = 1.0 / (1.0 + jnp.exp(-value))
    act = value * (SLOPE + (1.0 - SLOPE) * sigma)
    slope = 0.125 * SLOPE + (0.125 * (1.0 - SLOPE)) * (sigma + value * sigma * (1.0 - sigma))
    return act, slope


def call(body, out_shape, scratch, operands, scalars=(), flops=0, limit=32):
    specs = [pl.BlockSpec(memory_space=pltpu.SMEM)] * len(scalars)
    specs += [pl.BlockSpec(memory_space=VMEM)] * len(operands)
    outs = jax.tree.map(lambda _: pl.BlockSpec(memory_space=VMEM), out_shape)
    return pl.pallas_call(
        body,
        out_shape=out_shape,
        in_specs=specs,
        out_specs=outs,
        scratch_shapes=scratch,
        compiler_params=pltpu.CompilerParams(vmem_limit_bytes=limit * 1024 * 1024),
        cost_estimate=pl.CostEstimate(flops=flops, bytes_accessed=4_000_000, transcendentals=0),
    )(*scalars, *operands)


def shape(dims, kind):
    return jax.ShapeDtypeStruct(dims, kind)


def shifted_rows(values, step, period):
    if step == 0:
        return values
    count = values.shape[0]
    column = lax.broadcasted_iota(jnp.int32, values.shape, 0) % period
    rolled = pltpu.roll(values, (-step) % count, 0)
    inside = (column + step >= 0) & (column + step < period)
    return jnp.where(inside, rolled, 0.0)


def forward_five_kernel(slab, low, high, kernel, cot, message, slope, padded, tall):
    for plane in range(4):
        if plane == 0:
            source = low[...]
        elif plane == 3:
            source = high[...]
        else:
            source = slab[plane - 1]
        values = source.astype(jnp.float32)
        padded[plane, 0:16, :] = jnp.zeros((16, 384), jnp.bfloat16)
        padded[plane, 272:288, :] = jnp.zeros((16, 384), jnp.bfloat16)
        padded[plane, 16:272, 0:128] = shifted_rows(values, -1, 16).astype(jnp.bfloat16)
        padded[plane, 16:272, 128:256] = source
        padded[plane, 16:272, 256:384] = shifted_rows(values, 1, 16).astype(jnp.bfloat16)
    acts = []
    for plane in range(2):
        total = jnp.zeros((256, 256), jnp.float32)
        for depth_tap in range(3):
            for row_tap in range(3):
                start = (depth_tap * 3 + row_tap) * 384
                total += jnp.dot(
                    padded[plane + depth_tap, 16 * row_tap : 16 * row_tap + 256, :],
                    kernel[start : start + 384, :],
                    preferred_element_type=jnp.float32,
                )
        act, slant = both_of(total)
        slope[plane * 256 : (plane + 1) * 256, :] = slant
        acts.append(act)
    two = (acts[0] + acts[1]).reshape(8, 2, 16, 256)
    pairs = (two[:, 0] + two[:, 1]).reshape(128, 256)
    pooled = []
    for side in range(2):
        tall[side] = pairs[:, side * 128 : (side + 1) * 128]
        even = tall[side, pl.ds(0, 64, stride=2), :]
        odd = tall[side, pl.ds(1, 64, stride=2), :]
        pooled.append(((even + odd) * 0.125).astype(jnp.bfloat16))
    marks = cot[...]
    for target in range(16):
        message[target, 0:64, :] = pooled[0]
        message[target, 64:128, :] = pooled[1]
        message[target, 128:144, :] = marks


def forward_five(slab, low, high, kernel, cot_rows):
    return call(
        forward_five_kernel,
        (
            shape((16, 144, 128), jnp.bfloat16),
            shape((512, 256), jnp.float32),
            shape((4, 288, 384), jnp.bfloat16),
        ),
        [VMEM((2, 128, 128), jnp.float32)],
        (
            slab.reshape(2, 256, 128),
            low.reshape(256, 128),
            high.reshape(256, 128),
            kernel.reshape(3456, 256),
            cot_rows,
        ),
        flops=900_000_000,
    )


def own_taps_kernel(position, kernel, own):
    rows = lax.broadcasted_iota(jnp.int32, (16, 256), 0) + position[0] * 16
    lanes = lax.broadcasted_iota(jnp.int32, (16, 256), 1)
    pick = jnp.where(rows == lanes, 1.0, 0.0).astype(jnp.bfloat16)
    for tap in range(27):
        chosen = lax.dot_general(pick, kernel[tap], NT, preferred_element_type=jnp.float32)
        own[tap] = chosen.astype(jnp.bfloat16)


def own_taps(kernel, position):
    return call(
        own_taps_kernel,
        shape((27, 16, 256), jnp.bfloat16),
        [],
        (kernel.reshape(27, 256, 256),),
        (position,),
        flops=900_000_000,
    )


def six_to_five(position, gathered, kernel, slope, rows_out, near, tall):
    for plane in range(5):
        where = position[0] + (plane - 2)
        inside = (where >= 0) & (where < 16)
        index = jnp.clip(where, 0, 15)
        left = gathered[index, 0:64, :]
        right = gathered[index, 64:128, :]
        values = jnp.concatenate([left, right], axis=1).astype(jnp.float32)
        values = jnp.where(inside, values, 0.0)
        blank = jnp.zeros((8, 256), jnp.float32)
        for col_tap in range(3):
            moved = shifted_rows(values, col_tap - 1, 8)
            for row_tap in range(3):
                if row_tap == 0:
                    cells = jnp.concatenate([blank, moved[:56]], axis=0)
                elif row_tap == 1:
                    cells = moved
                else:
                    cells = jnp.concatenate([moved[8:], blank], axis=0)
                lane = (row_tap * 3 + col_tap) * 256
                near[plane, :, lane : lane + 256] = cells.astype(jnp.bfloat16)
    pre_six = jnp.zeros((192, 256), jnp.float32)
    for depth_tap in range(3):
        taps = kernel[depth_tap * 9 : depth_tap * 9 + 9].reshape(2304, 256)
        cells = near[depth_tap : depth_tap + 3].reshape(192, 2304)
        pre_six += jnp.dot(cells, taps, preferred_element_type=jnp.float32)
    _, slant = both_of(pre_six)
    cell = lax.broadcasted_iota(jnp.int32, (192, 128), 0)
    lanes = lax.broadcasted_iota(jnp.int32, (192, 128), 1)
    depth = cell // 64 + position[0] - 1
    small = (depth >> 1) * 16 + ((cell % 64) >> 4) * 4 + ((cell % 8) >> 1)
    hit = (small == lanes) & (depth >= 0) & (depth < 16)
    grow = jnp.where(hit, 1.0, 0.0).astype(jnp.bfloat16)
    cot = gathered[:, 128:144, :].reshape(256, 128)
    upstream = lax.dot_general(grow, cot, NT, preferred_element_type=jnp.float32)
    grad_six = (upstream * slant).astype(jnp.bfloat16).astype(jnp.float32)
    grad_pooled = jnp.zeros((64, 256), jnp.float32)
    blank = jnp.zeros((8, 256), jnp.float32)
    for depth_tap in range(3):
        values = grad_six[(2 - depth_tap) * 64 : (3 - depth_tap) * 64]
        for col_tap in range(3):
            moved = shifted_rows(values, 1 - col_tap, 8)
            for row_tap in range(3):
                if row_tap == 0:
                    cells = jnp.concatenate([moved[8:], blank], axis=0)
                elif row_tap == 1:
                    cells = moved
                else:
                    cells = jnp.concatenate([blank, moved[:56]], axis=0)
                grad_pooled += lax.dot_general(
                    cells.astype(jnp.bfloat16),
                    kernel[depth_tap * 9 + row_tap * 3 + col_tap],
                    NT,
                    preferred_element_type=jnp.float32,
                )
    for side in range(2):
        tall[side, pl.ds(0, 64, stride=2), :] = grad_pooled[:, side * 128 : (side + 1) * 128]
        tall[side, pl.ds(1, 64, stride=2), :] = grad_pooled[:, side * 128 : (side + 1) * 128]
    both = jnp.concatenate([tall[0], tall[1]], axis=1)
    wide = jnp.broadcast_to(both.reshape(8, 1, 16, 256), (8, 2, 16, 256)).reshape(256, 256)
    for plane in range(2):
        grad = wide * slope[plane * 256 : (plane + 1) * 256, :]
        rows_out[:, plane * 256 : (plane + 1) * 256] = grad.T.astype(jnp.bfloat16)


def half_of_five(first, rows, padded, out):
    for step in range(HALF_TAPS):
        tap = jnp.minimum(first + step, 26)
        depth_tap, row_tap, col_tap = tap // 9, (tap // 3) % 3, tap % 3
        total = jnp.zeros((256, 128), jnp.float32)
        for plane in range(2):
            cells = padded[
                plane + depth_tap,
                pl.ds(pl.multiple_of(row_tap * 16, 16), 256),
                pl.ds(pl.multiple_of(col_tap * 128, 128), 128),
            ]
            total += jnp.dot(
                rows[:, plane * 256 : (plane + 1) * 256],
                cells,
                preferred_element_type=jnp.float32,
            )
        out[:, step] = total.astype(jnp.bfloat16).reshape(16, 16, 128)


def back_kernel(position, half, gathered, kernel, slope, padded, rows, theirs, near, tall):
    six_to_five(position, gathered, kernel, slope, rows, near, tall)
    half_of_five((1 - half[0]) * HALF_TAPS, rows, padded, theirs)


def back_five(gathered, kernel, slope, padded, position, half):
    return call(
        back_kernel,
        (shape((256, 512), jnp.bfloat16), shape((16, HALF_TAPS, 16, 128), jnp.bfloat16)),
        [VMEM((5, 64, 2304), jnp.bfloat16), VMEM((2, 128, 128), jnp.float32)],
        (gathered, kernel.reshape(27, 256, 256), slope, padded),
        (position, half),
        flops=3_000_000_000,
    )


def mine_kernel(half, rows, padded, mine):
    half_of_five(half[0] * HALF_TAPS, rows, padded, mine)


def mine_of_five(rows, padded, half):
    return call(
        mine_kernel,
        shape((16, HALF_TAPS, 16, 128), jnp.bfloat16),
        [],
        (rows, padded),
        (half,),
        flops=900_000_000,
    )


def shifted_lanes(values, step, period, inner):
    if step == 0:
        return values
    count = values.shape[1]
    place = (lax.broadcasted_iota(jnp.int32, values.shape, 1) // inner) % period
    rolled = pltpu.roll(values, (-step * inner) % count, 1)
    inside = (place + step >= 0) & (place + step < period)
    return jnp.where(inside, rolled, 0.0)


def six_kernel(half, gathered, own, cot, next_rows, mine, theirs, cells, grads, whole):
    blank = jnp.zeros((64, 256), jnp.bfloat16)
    cells[0:64, :] = blank
    cells[1088:1152, :] = blank
    cells[64:1088, 0:128] = gathered[:, 0:64, :].reshape(1024, 128)
    cells[64:1088, 128:256] = gathered[:, 64:128, :].reshape(1024, 128)
    taps = jnp.zeros((144, 1024), jnp.float32)
    for depth_tap in range(3):
        taps += lax.dot_general(
            own[depth_tap * 9 : depth_tap * 9 + 9].reshape(144, 256),
            cells[depth_tap * 64 : depth_tap * 64 + 1024, :],
            NT,
            preferred_element_type=jnp.float32,
        )
    pre = jnp.zeros((16, 1024), jnp.float32)
    for row_tap in range(3):
        line = jnp.zeros((16, 1024), jnp.float32)
        for col_tap in range(3):
            start = (row_tap * 3 + col_tap) * 16
            line += shifted_lanes(taps[start : start + 16], col_tap - 1, 8, 1)
        pre += shifted_lanes(line, row_tap - 1, 8, 8)
    act, slant = both_of(pre)
    small = lax.broadcasted_iota(jnp.int32, (128, 1024), 0)
    cell = lax.broadcasted_iota(jnp.int32, (128, 1024), 1)
    target = (cell >> 7) * 16 + ((cell % 64) >> 4) * 4 + ((cell % 8) >> 1)
    grow = jnp.where(small == target, 1.0, 0.0).astype(jnp.bfloat16)
    upstream = jnp.dot(cot[...], grow, preferred_element_type=jnp.float32)
    high = act.astype(jnp.bfloat16)
    rest = act - high.astype(jnp.float32)
    middle = rest.astype(jnp.bfloat16)
    low = (rest - middle.astype(jnp.float32)).astype(jnp.bfloat16)
    sums = lax.dot_general(
        jnp.concatenate([high, middle, low], axis=0), grow, NT, preferred_element_type=jnp.float32
    )
    next_rows[...] = ((sums[0:16] + sums[16:32] + sums[32:48]) * 0.125).astype(jnp.bfloat16)
    grad = (upstream * slant).astype(jnp.bfloat16).astype(jnp.float32)
    for row_tap in range(3):
        line = shifted_lanes(grad, 1 - row_tap, 8, 8)
        for col_tap in range(3):
            start = (row_tap * 3 + col_tap) * 16
            moved = shifted_lanes(line, 1 - col_tap, 8, 1)
            grads[start : start + 16, :] = moved.astype(jnp.bfloat16)
    for depth_tap in range(3):
        part = jnp.dot(
            grads[...],
            cells[depth_tap * 64 : depth_tap * 64 + 1024, :],
            preferred_element_type=jnp.float32,
        )
        whole[depth_tap * 9 : depth_tap * 9 + 9] = part.astype(jnp.bfloat16).reshape(9, 16, 256)
    whole[27] = jnp.zeros((16, 256), jnp.bfloat16)
    mine[...] = whole[pl.ds(half[0] * HALF_TAPS, HALF_TAPS)]
    theirs[...] = whole[pl.ds((1 - half[0]) * HALF_TAPS, HALF_TAPS)]


def six_own(gathered, own, cot_rows, half):
    part = shape((HALF_TAPS, 16, 256), jnp.bfloat16)
    return call(
        six_kernel,
        (shape((16, 128), jnp.bfloat16), part, part),
        [
            VMEM((1152, 256), jnp.bfloat16),
            VMEM((144, 1024), jnp.bfloat16),
            VMEM((28, 16, 256), jnp.bfloat16),
        ],
        (gathered, own, cot_rows),
        (half,),
        flops=2_000_000_000,
    )


def shift_perm(axis, step):
    count = lax.axis_size(axis)
    return [(i, i + step) for i in range(count) if 0 <= i + step < count]


def core_swap(values):
    count = lax.axis_size("dp")
    return lax.ppermute(values, "dp", [(i, i ^ 1) for i in range(count)])


def sum_over_chips(values):
    count = lax.axis_size("dp")
    total = values.astype(jnp.float32)
    for step in range(1, count // 2):
        pairs = [(i, (i + 2 * step) % count) for i in range(count)]
        total = total + lax.ppermute(values, "dp", pairs).astype(jnp.float32)
    return total


def shards(volume, kernel_five, kernel_six, cotangent):
    position = lax.axis_index("wide").astype(jnp.int32).reshape(1)
    half = (lax.axis_index("dp") % 2).astype(jnp.int32).reshape(1)
    slab = volume[0]
    low = lax.ppermute(slab[-1:], "wide", shift_perm("wide", 1))
    high = lax.ppermute(slab[:1], "wide", shift_perm("wide", -1))
    cot_rows = cotangent[0].reshape(128, 16).T
    own = own_taps(kernel_six, position)
    message, slope, padded = forward_five(slab, low, high, kernel_five, cot_rows)
    gathered = lax.all_to_all(message, "wide", split_axis=0, concat_axis=0, tiled=True)
    rows, theirs_five = back_five(gathered, kernel_six, slope, padded, position, half)
    got_five = core_swap(theirs_five)
    mine_five = mine_of_five(rows, padded, half)
    pair_five = mine_five + got_five
    spread = lax.all_to_all(pair_five, "wide", split_axis=0, concat_axis=0, tiled=True)
    next_rows, mine_six, theirs_six = six_own(gathered, own, cot_rows, half)
    pair_six = mine_six + core_swap(theirs_six)
    depth_five = spread.astype(jnp.float32).sum(0).astype(jnp.bfloat16)
    both = jnp.concatenate([depth_five, pair_six], axis=-1)
    total = sum_over_chips(both).astype(jnp.bfloat16)
    other = core_swap(total)
    first = jnp.where(half == 0, total, other)
    second = jnp.where(half == 0, other, total)
    whole = jnp.concatenate([first, second], axis=0)[:27].astype(jnp.float32)
    out_five = whole[:, :, :128].transpose(0, 2, 1).reshape(3, 3, 3, 128, 16)
    out_six = whole[:, :, 128:].transpose(0, 2, 1).reshape(3, 3, 3, 256, 16)
    return (next_rows.T.reshape(1, 8, 4, 4, 16), out_five, out_six)


def solution(mesh):
    in_specs = (P("dp", "wide", None, None, None), P(), P(), P("dp", None, None, None, "wide"))
    out_specs = (
        P("dp", None, None, None, "wide"),
        P(None, None, None, None, "wide"),
        P(None, None, None, None, "wide"),
    )
    return jax.shard_map(shards, mesh=mesh, in_specs=in_specs, out_specs=out_specs, check_vma=False)
```

time: 167 us -> 92.3 us (0.55)
  local copies, waits for them, and re-layouts: 70.1 us -> 10.4 us
  matrix products: 32.9 us -> 0 us
  waiting for transfers between devices: 18.2 us -> 35.3 us
  Pallas kernels: 0 us -> 13.4 us
  other arithmetic: 10.2 us -> 4.19 us
  starting transfers between devices: 32.1 us -> 27.6 us
    unnamed x218 -> x18, local copies, waits for them, and re-layouts: 49 us -> 7.16 us
    dot_general x58 -> x0, matrix products: 32.9 us -> none  [the longest x4 14.7 us: convolve(): jnp.dot(wide, kernel.reshape(-1, kernel.shape[-1]), preferred_element_typ...]
    pallas_call x0 -> x5, Pallas kernels: none -> 13.4 us  [call(): pl.pallas_call(body, out_shape=out_shape, in_specs=specs, out_specs=outs,...]
    all_to_all x1, waiting for transfers between devices: 0.01 us -> 10.2 us  [shards(): lax.all_to_all(message, 'wide', split_axis=0, concat_axis=0, tiled=True)]
    ppermute x3, waiting for transfers between devices: 3.75 us -> 9.53 us  [sum_over_chips(): total = total + lax.ppermute(values, 'dp', pairs).astype(jnp.float32)]
    dynamic_slice x4 -> x0, local copies, waits for them, and re-layouts: 4.41 us -> none  [the longest x1 3.28 us: six_own(): own = lax.dynamic_slice_in_dim(kernel, position * share, share, 4)]
    rev x1 -> x0, local copies, waits for them, and re-layouts: 4.16 us -> none  [back_five(): flipped = jnp.flip(kernel, (0, 1, 2)).transpose(0, 1, 2, 4, 3)]
    all_to_all x1, starting transfers between devices: 6.9 us -> 4.32 us  [shards(): lax.all_to_all(pair_five, 'wide', split_axis=0, concat_axis=0, tiled=True)]
  transfers between devices with their start and end apart: 10 -> 10, of which waited for: 5 -> 9; matrix products, arithmetic and copies ran while one was open for 36% -> 2% of each run, Pallas kernels for 0% -> 5%
where the time goes in v2:
time: 92.3 us; the launch traced here: 91.6 us
  waiting for transfers between devices  35.3 us (38%)
  starting transfers between devices  27.6 us (30%)
  Pallas kernels  13.4 us (15%)
  local copies, waits for them, and re-layouts  10.4 us (11%)
  other arithmetic  4.19 us (5%)
    pallas_call x5, Pallas kernels, call(): pl.pallas_call(body, out_shape=out_shape, in_specs=specs, out_specs=outs,...  13.4 us
    all_to_all x1, waiting for transfers between devices, shards(): lax.all_to_all(message, 'wide', split_axis=0, concat_axis=0, tiled=True)  10.2 us
    all_to_all x1, waiting for transfers between devices, shards(): lax.all_to_all(pair_five, 'wide', split_axis=0, concat_axis=0, tiled=True)  10.1 us
    ppermute x3, waiting for transfers between devices, sum_over_chips(): total = total + lax.ppermute(values, 'dp', pairs).astype(jnp.float32)  9.53 us
    all_to_all x1, starting transfers between devices, shards(): lax.all_to_all(message, 'wide', split_axis=0, concat_axis=0, tiled=True)  8.69 us
    unnamed x18, local copies, waits for them, and re-layouts  7.16 us
    ppermute x3, starting transfers between devices, core_swap(): return lax.ppermute(values, 'dp', [(i, i ^ 1) for i in range(count)])  5.04 us
    ppermute x1, starting transfers between devices, shards(): low = lax.ppermute(slab[-1:], 'wide', shift_perm('wide', 1))  4.64 us
  transfers between devices with their start and end apart: 10, of which 9 were waited for; matrix products, arithmetic and copies ran while one was open for 2% of the time, Pallas kernels for 5%

profile of v2, /device:TPU:1, one launch (start us, length us, event | category | flops | bytes accessed | tf_op | source)
XLA Modules:
  0.0 91.6 jit_solution(8067469021855792402)
XLA Ops:
  0.6 1.7 %slice_bitcast_fusion = (bf16[1,16,16,128]{3,2,1,0:T(8,128)(2,1)}, bf16[1,16,16,128]{3,2,1,0:T(8,128)(2,1)}) fusion(bf16[1,2,16,16,128]{4,3,2,1,0:T(8,128)(2,1)} %param.4), kind=kLoop, calls=%fused_computation.7 | loop fusion | bytes 262144 | tf_op jit(solution)/shard_map/slice | solution.py:352
  2.3 4.6 %collective-permute-start = (bf16[1,16,16,128]{3,2,1,0:T(8,128)(2,1)}, bf16[1,16,16,128]{3,2,1,0:T(8,128)(2,1)}, u32[]{:S(2)}, u32[]{:S(2)}) collective-permute-start(bf16[1,16,16,128]{3,2,1,0:T(8,128)(2,1)} %get-tuple-element.25), channel_id=1, source_target_pairs={{0,1},{1,2},{2,3},{3,4},{4,5},{5,6},{6,7},{7,8},{8,9},{9,10},{10,1... | collective-permute-start | bytes 196616 | tf_op jit(solution)/shard_map/ppermute | solution.py:351
  7.0 1.3 %collective-permute-start.1 = (bf16[1,16,16,128]{3,2,1,0:T(8,128)(2,1)}, bf16[1,16,16,128]{3,2,1,0:T(8,128)(2,1)}, u32[]{:S(2)}, u32[]{:S(2)}) collective-permute-start(bf16[1,16,16,128]{3,2,1,0:T(8,128)(2,1)} %get-tuple-element.24), channel_id=1, source_target_pairs={{1,0},{2,1},{3,2},{4,3},{5,4},{6,5},{7,6},{8,7},{9,8},{10,9},{11,1... | collective-permute-start | bytes 196616 | tf_op jit(solution)/shard_map/ppermute | solution.py:352
  9.1 3.2 %collective-permute-done.1 = bf16[1,16,16,128]{3,2,1,0:T(8,128)(2,1)} collective-permute-done((bf16[1,16,16,128]{3,2,1,0:T(8,128)(2,1)}, bf16[1,16,16,128]{3,2,1,0:T(8,128)(2,1)}, u32[]{:S(2)}, u32[]{:S(2)}) %collective-permute-start.1) | collective-permute-done | bytes 65568 | tf_op jit(solution)/shard_map/ppermute | solution.py:352
  13.2 1.5 %copy-done.3 = bf16[3,3,3,128,256]{4,3,2,1,0:T(8,128)(2,1)S(1)} copy-done((bf16[3,3,3,128,256]{4,3,2,1,0:T(8,128)(2,1)S(1)}, bf16[3,3,3,128,256]{4,3,2,1,0:T(8,128)(2,1)}, u32[]{:S(2)}) %copy-start.3) | copy-done | bytes 1769496
  14.7 2.5 %shard_map.67 = (bf16[16,144,128]{2,1,0:T(8,128)(2,1)S(1)}, f32[512,256]{1,0:T(8,128)S(1)}, bf16[4,288,384]{2,1,0:T(8,128)(2,1)S(1)}) custom-call(bf16[2,256,128]{2,1,0:T(8,128)(2,1)S(1)} %bitcast.24, bf16[256,128]{1,0:T(8,128)(2,1)} %bitcast.3.low, bf16[256,128]{1,0:T(8,128)(2,1)} %bitcast.5.high, bf16[3456,256]{1,0:T(8,128)(2,1)S(1)} %bitcast.28, ...), custom_call_target="tpu_custom_call" | custom-call | flops 900000000 | bytes 4000000 | tf_op jit(solution)/shard_map/pallas_call | solution.py:25
  19.8 8.7 %all-to-all-start = ((bf16[16,144,128]{2,1,0:T(8,128)(2,1)}), bf16[16,144,128]{2,1,0:T(8,128)(2,1)}, u32[]{:S(2)}, u32[]{:S(2)}) async-start(bf16[16,144,128]{2,1,0:T(8,128)(2,1)} %copy-done.1), calls=%async_computation | async-start | bytes 1179648 | tf_op jit(solution)/shard_map/all_to_all | solution.py:356
  28.5 10.2 %all-to-all-done.gathered = bf16[16,144,128]{2,1,0:T(8,128)(2,1)} async-done(((bf16[16,144,128]{2,1,0:T(8,128)(2,1)}), bf16[16,144,128]{2,1,0:T(8,128)(2,1)}, u32[]{:S(2)}, u32[]{:S(2)}) %all-to-all-start) | async-done | bytes 589856 | tf_op jit(solution)/shard_map/all_to_all | solution.py:356
  38.7 1.2 %copy-done.5 = bf16[4,288,384]{2,1,0:T(8,128)(2,1)S(1)} copy-done((bf16[4,288,384]{2,1,0:T(8,128)(2,1)S(1)}, bf16[4,288,384]{2,1,0:T(8,128)(2,1)}, u32[]{:S(2)}) %copy-start.5) | copy-done | bytes 884760
  39.8 1.0 %copy-done.8 = f32[512,256]{1,0:T(8,128)S(1)} copy-done((f32[512,256]{1,0:T(8,128)S(1)}, f32[512,256]{1,0:T(8,128)}, u32[]{:S(2)}) %copy-start.8) | copy-done | bytes 524312
  40.9 6.1 %shard_map.70 = (bf16[256,512]{1,0:T(8,128)(2,1)S(1)}, bf16[16,14,16,128]{3,2,1,0:T(8,128)(2,1)S(1)}) custom-call(s32[1]{0:T(128)} %bitcast.9.position, s32[1]{0:T(128)} %bitcast.half, bf16[16,144,128]{2,1,0:T(8,128)(2,1)} %all-to-all-done.gathered, bf16[27,256,256]{2,1,0:T(8,128)(2,1)S(1)} %bitcast.22, f32[512,256]{1,0:T(8,128)S(1)} %copy-done.8, ...), custom_call_target="tpu_custom_call" | custom-call | flops 3000000000 | bytes 4000000 | tf_op jit(solution)/shard_map/pallas_call | solution.py:25
  46.9 3.2 %collective-permute-start.2 = (bf16[16,14,16,128]{3,2,1,0:T(8,128)(2,1)S(1)}, bf16[16,14,16,128]{3,2,1,0:T(8,128)(2,1)S(1)}, u32[]{:S(2)}, u32[]{:S(2)}) collective-permute-start(bf16[16,14,16,128]{3,2,1,0:T(8,128)(2,1)S(1)} %get-tuple-element.16), channel_id=1, source_target_pairs={{0,16},{16,0},{32,48},{48,32},{64,80},{80,64},{96,112},{112,96},{1... | collective-permute-start | bytes 2752520 | tf_op jit(solution)/shard_map/ppermute | solution.py:335
  50.1 1.1 %shard_map.71 = bf16[16,14,16,128]{3,2,1,0:T(8,128)(2,1)S(1)} custom-call(s32[1]{0:T(128)} %bitcast.half, bf16[256,512]{1,0:T(8,128)(2,1)S(1)} %get-tuple-element.15.rows, bf16[4,288,384]{2,1,0:T(8,128)(2,1)S(1)} %copy-done.6), custom_call_target="tpu_custom_call" | custom-call | flops 900000000 | bytes 4000000 | tf_op jit(solution)/shard_map/pallas_call | solution.py:25
  52.2 1.2 %add.20 = bf16[16,14,16,128]{3,2,1,0:T(8,128)(2,1)} add(bf16[16,14,16,128]{3,2,1,0:T(8,128)(2,1)S(1)} %shard_map.71, bf16[16,14,16,128]{3,2,1,0:T(8,128)(2,1)S(1)} %collective-permute-done.2) | non-fusion elementwise | flops 458752 | bytes 2752512 | tf_op jit(solution)/shard_map/add | solution.py:360
  53.4 4.3 %all-to-all-start.1 = ((bf16[16,14,16,128]{3,2,1,0:T(8,128)(2,1)}), bf16[16,14,16,128]{3,2,1,0:T(8,128)(2,1)}, u32[]{:S(2)}, u32[]{:S(2)}) async-start(bf16[16,14,16,128]{3,2,1,0:T(8,128)(2,1)} %add.20), calls=%async_computation.1 | async-start | bytes 1835008 | tf_op jit(solution)/shard_map/all_to_all | solution.py:361
  57.7 1.1 %shard_map.68.own = bf16[27,16,256]{2,1,0:T(8,128)(2,1)S(1)} custom-call(s32[1]{0:T(128)} %bitcast.9.position, bf16[27,256,256]{2,1,0:T(8,128)(2,1)S(1)} %bitcast.23), custom_call_target="tpu_custom_call" | custom-call | flops 900000000 | bytes 4000000 | tf_op jit(solution)/shard_map/pallas_call | solution.py:25
  58.8 2.6 %shard_map.69 = (bf16[16,128]{1,0:T(8,128)(2,1)S(1)}, bf16[14,16,256]{2,1,0:T(8,128)(2,1)S(1)}, bf16[14,16,256]{2,1,0:T(8,128)(2,1)S(1)}) custom-call(s32[1]{0:T(128)} %bitcast.half, bf16[16,144,128]{2,1,0:T(8,128)(2,1)} %all-to-all-done.gathered, bf16[27,16,256]{2,1,0:T(8,128)(2,1)S(1)} %shard_map.68.own, bf16[16,128]{1,0:T(8,128)(2,1)S(1)} %bitcast.26), custom_call_target="tpu_custom_call" | custom-call | flops 2000000000 | bytes 4000000 | tf_op jit(solution)/shard_map/pallas_call | solution.py:25
  62.9 10.1 %all-to-all-done.1 = bf16[16,14,16,128]{3,2,1,0:T(8,128)(2,1)} async-done(((bf16[16,14,16,128]{3,2,1,0:T(8,128)(2,1)}), bf16[16,14,16,128]{3,2,1,0:T(8,128)(2,1)}, u32[]{:S(2)}, u32[]{:S(2)}) %all-to-all-start.1) | async-done | bytes 917536 | tf_op jit(solution)/shard_map/all_to_all | solution.py:361
  73.0 1.3 %reduce_sum.12 = bf16[14,16,128]{2,1,0:T(8,128)(2,1)S(1)} reduce(bf16[16,14,16,128]{3,2,1,0:T(8,128)(2,1)} %all-to-all-done.1, bf16[]{:T(256)} %constant.26.clone.1), dimensions={0}, to_apply=%region_0.1 | reduce | flops 430080 | bytes 974850 | tf_op jit(solution)/shard_map/reduce_sum | solution.py:364
  74.3 2.6 %collective-permute-start.6 = (bf16[14,16,384]{2,1,0:T(8,128)(2,1)S(1)}, bf16[14,16,384]{2,1,0:T(8,128)(2,1)S(1)}, u32[]{:S(2)}, u32[]{:S(2)}) collective-permute-start(bf16[14,16,384]{2,1,0:T(8,128)(2,1)S(1)} %pad_maximum_fusion.1), channel_id=1, source_target_pairs={{0,96},{16,112},{32,0},{48,16},{64,32},{80,48},{96,64},{112,80},{1... | collective-permute-start | bytes 516104 | tf_op jit(solution)/shard_map/ppermute | solution.py:343
  78.0 2.3 %collective-permute-done.6 = bf16[14,16,384]{2,1,0:T(8,128)(2,1)S(1)} collective-permute-done((bf16[14,16,384]{2,1,0:T(8,128)(2,1)S(1)}, bf16[14,16,384]{2,1,0:T(8,128)(2,1)S(1)}, u32[]{:S(2)}, u32[]{:S(2)}) %collective-permute-start.6) | collective-permute-done | bytes 172064 | tf_op jit(solution)/shard_map/ppermute | solution.py:343
  80.3 2.4 %collective-permute-done.5 = bf16[14,16,384]{2,1,0:T(8,128)(2,1)S(1)} collective-permute-done((bf16[14,16,384]{2,1,0:T(8,128)(2,1)S(1)}, bf16[14,16,384]{2,1,0:T(8,128)(2,1)S(1)}, u32[]{:S(2)}, u32[]{:S(2)}) %collective-permute-start.5) | collective-permute-done | bytes 172064 | tf_op jit(solution)/shard_map/ppermute | solution.py:343
  82.7 4.8 %collective-permute-done.4 = bf16[14,16,384]{2,1,0:T(8,128)(2,1)S(1)} collective-permute-done((bf16[14,16,384]{2,1,0:T(8,128)(2,1)S(1)}, bf16[14,16,384]{2,1,0:T(8,128)(2,1)S(1)}, u32[]{:S(2)}, u32[]{:S(2)}) %collective-permute-start.4) | collective-permute-done | bytes 172064 | tf_op jit(solution)/shard_map/ppermute | solution.py:343
  87.6 1.4 %collective-permute-start.7 = (bf16[14,16,384]{2,1,0:T(8,128)(2,1)S(1)}, bf16[14,16,384]{2,1,0:T(8,128)(2,1)S(1)}, u32[]{:S(2)}, u32[]{:S(2)}) collective-permute-start(bf16[14,16,384]{2,1,0:T(8,128)(2,1)S(1)} %add_convert_fusion), channel_id=1, source_target_pairs={{0,16},{16,0},{32,48},{48,32},{64,80},{80,64},{96,112},{112,96},{1... | collective-permute-start | bytes 516104 | tf_op jit(solution)/shard_map/ppermute | solution.py:335
  (30 shorter events, 10.5 us)
Async XLA Ops:
  0.6 38.0 %copy-start = (bf16[3,3,3,256,256]{4,3,2,1,0:T(8,128)(2,1)S(1)}, bf16[3,3,3,256,256]{4,3,2,1,0:T(8,128)(2,1)}, u32[]{:S(2)}) copy-start(bf16[3,3,3,256,256]{4,3,2,1,0:T(8,128)(2,1)} %param.6) | copy-start | bytes 10616836
  2.3 6.7 %collective-permute-start = (bf16[1,16,16,128]{3,2,1,0:T(8,128)(2,1)}, bf16[1,16,16,128]{3,2,1,0:T(8,128)(2,1)}, u32[]{:S(2)}, u32[]{:S(2)}) collective-permute-start(bf16[1,16,16,128]{3,2,1,0:T(8,128)(2,1)} %get-tuple-element.25), channel_id=1, source_target_pairs={{0,1},{1,2},{2,3},{3,4},{4,5},{5,6},{6,7},{7,8},{8,9},{9,10},{10,1... | collective-permute-start | bytes 196616 | tf_op jit(solution)/shard_map/ppermute | solution.py:351
  7.0 5.3 %collective-permute-start.1 = (bf16[1,16,16,128]{3,2,1,0:T(8,128)(2,1)}, bf16[1,16,16,128]{3,2,1,0:T(8,128)(2,1)}, u32[]{:S(2)}, u32[]{:S(2)}) collective-permute-start(bf16[1,16,16,128]{3,2,1,0:T(8,128)(2,1)} %get-tuple-element.24), channel_id=1, source_target_pairs={{1,0},{2,1},{3,2},{4,3},{5,4},{6,5},{7,6},{8,7},{9,8},{10,9},{11,1... | collective-permute-start | bytes 196616 | tf_op jit(solution)/shard_map/ppermute | solution.py:352
  12.3 0.9 copy-start.2
  13.2 1.5 %copy-start.3 = (bf16[3,3,3,128,256]{4,3,2,1,0:T(8,128)(2,1)S(1)}, bf16[3,3,3,128,256]{4,3,2,1,0:T(8,128)(2,1)}, u32[]{:S(2)}) copy-start(bf16[3,3,3,128,256]{4,3,2,1,0:T(8,128)(2,1)} %param.5) | copy-start | bytes 5308420
  17.2 0.8 copy-start.1
  18.0 0.9 %copy-start.4 = (bf16[4,288,384]{2,1,0:T(8,128)(2,1)}, bf16[4,288,384]{2,1,0:T(8,128)(2,1)S(1)}, u32[]{:S(2)}) copy-start(bf16[4,288,384]{2,1,0:T(8,128)(2,1)S(1)} %get-tuple-element.14.padded) | copy-start | bytes 2654212
  19.0 0.8 copy-start.7
  19.8 18.9 %all-to-all-start = ((bf16[16,144,128]{2,1,0:T(8,128)(2,1)}), bf16[16,144,128]{2,1,0:T(8,128)(2,1)}, u32[]{:S(2)}, u32[]{:S(2)}) async-start(bf16[16,144,128]{2,1,0:T(8,128)(2,1)} %copy-done.1), calls=%async_computation | async-start | bytes 1179648 | tf_op jit(solution)/shard_map/all_to_all | solution.py:356
  38.7 1.2 %copy-start.5 = (bf16[4,288,384]{2,1,0:T(8,128)(2,1)S(1)}, bf16[4,288,384]{2,1,0:T(8,128)(2,1)}, u32[]{:S(2)}) copy-start(bf16[4,288,384]{2,1,0:T(8,128)(2,1)} %copy-done.4) | copy-start | bytes 2654212
  39.8 1.0 %copy-start.8 = (f32[512,256]{1,0:T(8,128)S(1)}, f32[512,256]{1,0:T(8,128)}, u32[]{:S(2)}) copy-start(f32[512,256]{1,0:T(8,128)} %copy-done.7) | copy-start | bytes 1572868
  40.9 9.2 %copy-start.6 = (bf16[4,288,384]{2,1,0:T(8,128)(2,1)S(1)}, bf16[4,288,384]{2,1,0:T(8,128)(2,1)}, u32[]{:S(2)}) copy-start(bf16[4,288,384]{2,1,0:T(8,128)(2,1)} %copy-done.4) | copy-start | bytes 2654212
  46.9 5.3 %collective-permute-start.2 = (bf16[16,14,16,128]{3,2,1,0:T(8,128)(2,1)S(1)}, bf16[16,14,16,128]{3,2,1,0:T(8,128)(2,1)S(1)}, u32[]{:S(2)}, u32[]{:S(2)}) collective-permute-start(bf16[16,14,16,128]{3,2,1,0:T(8,128)(2,1)S(1)} %get-tuple-element.16), channel_id=1, source_target_pairs={{0,16},{16,0},{32,48},{48,32},{64,80},{80,64},{96,112},{112,96},{1... | collective-permute-start | bytes 2752520 | tf_op jit(solution)/shard_map/ppermute | solution.py:335
  53.4 19.6 %all-to-all-start.1 = ((bf16[16,14,16,128]{3,2,1,0:T(8,128)(2,1)}), bf16[16,14,16,128]{3,2,1,0:T(8,128)(2,1)}, u32[]{:S(2)}, u32[]{:S(2)}) async-start(bf16[16,14,16,128]{3,2,1,0:T(8,128)(2,1)} %add.20), calls=%async_computation.1 | async-start | bytes 1835008 | tf_op jit(solution)/shard_map/all_to_all | solution.py:361
  61.4 1.4 %collective-permute-start.3 = (bf16[14,16,256]{2,1,0:T(8,128)(2,1)S(1)}, bf16[14,16,256]{2,1,0:T(8,128)(2,1)S(1)}, u32[]{:S(2)}, u32[]{:S(2)}) collective-permute-start(bf16[14,16,256]{2,1,0:T(8,128)(2,1)S(1)} %get-tuple-element.18), channel_id=1, source_target_pairs={{0,16},{16,0},{32,48},{48,32},{64,80},{80,64},{96,112},{112,96},{1... | collective-permute-start | bytes 344072 | tf_op jit(solution)/shard_map/ppermute | solution.py:335
  74.3 6.0 %collective-permute-start.6 = (bf16[14,16,384]{2,1,0:T(8,128)(2,1)S(1)}, bf16[14,16,384]{2,1,0:T(8,128)(2,1)S(1)}, u32[]{:S(2)}, u32[]{:S(2)}) collective-permute-start(bf16[14,16,384]{2,1,0:T(8,128)(2,1)S(1)} %pad_maximum_fusion.1), channel_id=1, source_target_pairs={{0,96},{16,112},{32,0},{48,16},{64,32},{80,48},{96,64},{112,80},{1... | collective-permute-start | bytes 516104 | tf_op jit(solution)/shard_map/ppermute | solution.py:343
  76.9 5.9 %collective-permute-start.5 = (bf16[14,16,384]{2,1,0:T(8,128)(2,1)S(1)}, bf16[14,16,384]{2,1,0:T(8,128)(2,1)S(1)}, u32[]{:S(2)}, u32[]{:S(2)}) collective-permute-start(bf16[14,16,384]{2,1,0:T(8,128)(2,1)S(1)} %pad_maximum_fusion.1), channel_id=1, source_target_pairs={{0,64},{16,80},{32,96},{48,112},{64,0},{80,16},{96,32},{112,48},{1... | collective-permute-start | bytes 516104 | tf_op jit(solution)/shard_map/ppermute | solution.py:343
  77.4 10.1 %collective-permute-start.4 = (bf16[14,16,384]{2,1,0:T(8,128)(2,1)S(1)}, bf16[14,16,384]{2,1,0:T(8,128)(2,1)S(1)}, u32[]{:S(2)}, u32[]{:S(2)}) collective-permute-start(bf16[14,16,384]{2,1,0:T(8,128)(2,1)S(1)} %pad_maximum_fusion.1), channel_id=1, source_target_pairs={{0,32},{16,48},{32,64},{48,80},{64,96},{80,112},{96,0},{112,16},{1... | collective-permute-start | bytes 516104 | tf_op jit(solution)/shard_map/ppermute | solution.py:343
  87.6 2.4 %collective-permute-start.7 = (bf16[14,16,384]{2,1,0:T(8,128)(2,1)S(1)}, bf16[14,16,384]{2,1,0:T(8,128)(2,1)S(1)}, u32[]{:S(2)}, u32[]{:S(2)}) collective-permute-start(bf16[14,16,384]{2,1,0:T(8,128)(2,1)S(1)} %add_convert_fusion), channel_id=1, source_target_pairs={{0,16},{16,0},{32,48},{48,32},{64,80},{80,64},{96,112},{112,96},{1... | collective-permute-start | bytes 516104 | tf_op jit(solution)/shard_map/ppermute | solution.py:335

commit v3 on v2

--- a/solution.py
+++ b/solution.py
@@ -18,9 +18,9 @@
     return act, slope
 
 
-def call(body, out_shape, scratch, operands, scalars=(), flops=0, limit=32):
+def call(body, out_shape, scratch, operands, scalars=(), flops=0, limit=16, space=VMEM):
     specs = [pl.BlockSpec(memory_space=pltpu.SMEM)] * len(scalars)
-    specs += [pl.BlockSpec(memory_space=VMEM)] * len(operands)
+    specs += [pl.BlockSpec(memory_space=space)] * len(operands)
     outs = jax.tree.map(lambda _: pl.BlockSpec(memory_space=VMEM), out_shape)
     return pl.pallas_call(
         body,
@@ -47,31 +47,72 @@
     return jnp.where(inside, rolled, 0.0)
 
 
-def forward_five_kernel(slab, low, high, kernel, cot, message, slope, padded, tall):
-    for plane in range(4):
-        if plane == 0:
-            source = low[...]
-        elif plane == 3:
-            source = high[...]
-        else:
-            source = slab[plane - 1]
-        values = source.astype(jnp.float32)
-        padded[plane, 0:16, :] = jnp.zeros((16, 384), jnp.bfloat16)
-        padded[plane, 272:288, :] = jnp.zeros((16, 384), jnp.bfloat16)
-        padded[plane, 16:272, 0:128] = shifted_rows(values, -1, 16).astype(jnp.bfloat16)
-        padded[plane, 16:272, 128:256] = source
-        padded[plane, 16:272, 256:384] = shifted_rows(values, 1, 16).astype(jnp.bfloat16)
+def columns_of(padded, index, source):
+    values = source.astype(jnp.float32)
+    padded[index, 0:16, :] = jnp.zeros((16, 384), jnp.bfloat16)
+    padded[index, 272:288, :] = jnp.zeros((16, 384), jnp.bfloat16)
+    padded[index, 16:272, 0:128] = shifted_rows(values, -1, 16).astype(jnp.bfloat16)
+    padded[index, 16:272, 128:256] = source
+    padded[index, 16:272, 256:384] = shifted_rows(values, 1, 16).astype(jnp.bfloat16)
+
+
+def depth_term(padded, index, kernel, depth_tap):
+    total = jnp.zeros((256, 256), jnp.float32)
+    for row_tap in range(3):
+        start = (depth_tap * 3 + row_tap) * 384
+        total += jnp.dot(
+            padded[index, 16 * row_tap : 16 * row_tap + 256, :],
+            kernel[start : start + 384, :],
+            preferred_element_type=jnp.float32,
+        )
+    return total
+
+
+def inner_kernel(slab_far, kernel_far, part, padded, kernel, slab, marks):
+    loads = [pltpu.make_async_copy(slab_far, slab, marks.at[3])]
+    loads[0].start()
+    takes = {}
+    for depth_tap in (1, 2, 0):
+        rows = pl.ds(depth_tap * 1152, 1152)
+        takes[depth_tap] = pltpu.make_async_copy(
+            kernel_far.at[rows], kernel.at[rows], marks.at[depth_tap]
+        )
+        takes[depth_tap].start()
+    loads[0].wait()
+    for plane in range(2):
+        columns_of(padded, plane, slab[plane])
+    takes[1].wait()
+    for plane in range(2):
+        part[plane * 256 : (plane + 1) * 256, :] = depth_term(padded, plane, kernel, 1)
+    takes[2].wait()
+    part[0:256, :] += depth_term(padded, 1, kernel, 2)
+    takes[0].wait()
+    part[256:512, :] += depth_term(padded, 0, kernel, 0)
+
+
+def inner_five(slab, kernel):
+    return call(
+        inner_kernel,
+        (
+            shape((512, 256), jnp.float32),
+            shape((2, 288, 384), jnp.bfloat16),
+            shape((3456, 256), jnp.bfloat16),
+        ),
+        [VMEM((2, 256, 128), jnp.bfloat16), pltpu.SemaphoreType.DMA((4,))],
+        (slab.reshape(2, 256, 128), kernel.reshape(3456, 256)),
+        flops=600_000_000,
+        space=pltpu.HBM,
+    )
+
+
+def outer_kernel(low, high, kernel, part, inner, cot, message, slope, padded, tall):
+    columns_of(padded, 0, low[1])
+    columns_of(padded, 3, high[0])
+    padded[1:3] = inner[...]
     acts = []
     for plane in range(2):
-        total = jnp.zeros((256, 256), jnp.float32)
-        for depth_tap in range(3):
-            for row_tap in range(3):
-                start = (depth_tap * 3 + row_tap) * 384
-                total += jnp.dot(
-                    padded[plane + depth_tap, 16 * row_tap : 16 * row_tap + 256, :],
-                    kernel[start : start + 384, :],
-                    preferred_element_type=jnp.float32,
-                )
+        total = part[plane * 256 : (plane + 1) * 256, :]
+        total += depth_term(padded, 3 * plane, kernel, 2 * plane)
         act, slant = both_of(total)
         slope[plane * 256 : (plane + 1) * 256, :] = slant
         acts.append(act)
@@ -90,9 +131,9 @@
         message[target, 128:144, :] = marks
 
 
-def forward_five(slab, low, high, kernel, cot_rows):
-    return call(
-        forward_five_kernel,
+def outer_five(low, high, kernel, part, inner, cot_rows):
+    return call(
+        outer_kernel,
         (
             shape((16, 144, 128), jnp.bfloat16),
             shape((512, 256), jnp.float32),
@@ -100,13 +141,14 @@
         ),
         [VMEM((2, 128, 128), jnp.float32)],
         (
-            slab.reshape(2, 256, 128),
-            low.reshape(256, 128),
-            high.reshape(256, 128),
-            kernel.reshape(3456, 256),
+            low.reshape(2, 256, 128),
+            high.reshape(2, 256, 128),
+            kernel,
+            part,
+            inner,
             cot_rows,
         ),
-        flops=900_000_000,
+        flops=300_000_000,
     )
 
 
@@ -195,7 +237,7 @@
         rows_out[:, plane * 256 : (plane + 1) * 256] = grad.T.astype(jnp.bfloat16)
 
 
-def half_of_five(first, rows, padded, out):
+def half_of_five(first, rows, padded, out, got=None):
     for step in range(HALF_TAPS):
         tap = jnp.minimum(first + step, 26)
         depth_tap, row_tap, col_tap = tap // 9, (tap // 3) % 3, tap % 3
@@ -211,6 +253,8 @@
                 cells,
                 preferred_element_type=jnp.float32,
             )
+        if got is not None:
+            total += got[:, step].reshape(256, 128).astype(jnp.float32)
         out[:, step] = total.astype(jnp.bfloat16).reshape(16, 16, 128)
 
 
@@ -230,16 +274,16 @@
     )
 
 
-def mine_kernel(half, rows, padded, mine):
-    half_of_five(half[0] * HALF_TAPS, rows, padded, mine)
-
-
-def mine_of_five(rows, padded, half):
+def mine_kernel(half, rows, padded, got, mine):
+    half_of_five(half[0] * HALF_TAPS, rows, padded, mine, got)
+
+
+def mine_of_five(rows, padded, got, half):
     return call(
         mine_kernel,
         shape((16, HALF_TAPS, 16, 128), jnp.bfloat16),
         [],
-        (rows, padded),
+        (rows, padded, got),
         (half,),
         flops=900_000_000,
     )
@@ -304,7 +348,7 @@
             preferred_element_type=jnp.float32,
         )
         whole[depth_tap * 9 : depth_tap * 9 + 9] = part.astype(jnp.bfloat16).reshape(9, 16, 256)
-    whole[27] = jnp.zeros((16, 256), jnp.bfloat16)
+    whole[27] = whole[26]
     mine[...] = whole[pl.ds(half[0] * HALF_TAPS, HALF_TAPS)]
     theirs[...] = whole[pl.ds((1 - half[0]) * HALF_TAPS, HALF_TAPS)]
 
@@ -325,6 +369,27 @@
     )
 
 
+def halves_kernel(half, mine_five, other_five, mine_six, other_six, five, six):
+    for step in range(HALF_TAPS):
+        for first, part_five, part_six in (
+            (half[0] * HALF_TAPS, mine_five, mine_six),
+            ((1 - half[0]) * HALF_TAPS, other_five, other_six),
+        ):
+            tap = jnp.minimum(first + step, 26)
+            five[tap] = part_five[step].astype(jnp.float32)
+            six[tap] = part_six[step].astype(jnp.float32)
+
+
+def both_halves(half, mine_five, other_five, mine_six, other_six):
+    return call(
+        halves_kernel,
+        (shape((27, 16, 128), jnp.float32), shape((27, 16, 256), jnp.float32)),
+        [],
+        (mine_five, other_five, mine_six, other_six),
+        (half,),
+    )
+
+
 def shift_perm(axis, step):
     count = lax.axis_size(axis)
     return [(i, i + step) for i in range(count) if 0 <= i + step < count]
@@ -335,41 +400,59 @@
     return lax.ppermute(values, "dp", [(i, i ^ 1) for i in range(count)])
 
 
-def sum_over_chips(values):
+def from_chips(values):
     count = lax.axis_size("dp")
-    total = values.astype(jnp.float32)
+    got = []
     for step in range(1, count // 2):
         pairs = [(i, (i + 2 * step) % count) for i in range(count)]
-        total = total + lax.ppermute(values, "dp", pairs).astype(jnp.float32)
+        got.append(lax.ppermute(values, "dp", pairs))
+    return got
+
+
+def total_of(values, others):
+    total = values.astype(jnp.float32)
+    for other in others:
+        total = total + other.astype(jnp.float32)
     return total
+
+
+def exchange(values):
+    return lax.all_to_all(values, "wide", split_axis=0, concat_axis=0, tiled=True)
 
 
 def shards(volume, kernel_five, kernel_six, cotangent):
     position = lax.axis_index("wide").astype(jnp.int32).reshape(1)
     half = (lax.axis_index("dp") % 2).astype(jnp.int32).reshape(1)
-    slab = volume[0]
-    low = lax.ppermute(slab[-1:], "wide", shift_perm("wide", 1))
-    high = lax.ppermute(slab[:1], "wide", shift_perm("wide", -1))
+    low = lax.ppermute(volume, "wide", shift_perm("wide", 1))
+    high = lax.ppermute(volume, "wide", shift_perm("wide", -1))
     cot_rows = cotangent[0].reshape(128, 16).T
-    own = own_taps(kernel_six, position)
-    message, slope, padded = forward_five(slab, low, high, kernel_five, cot_rows)
-    gathered = lax.all_to_all(message, "wide", split_axis=0, concat_axis=0, tiled=True)
+    part, inner, near_kernel = inner_five(volume, kernel_five)
+    message, slope, padded = outer_five(low, high, near_kernel, part, inner, cot_rows)
+    message, position, half, slope, padded = lax.optimization_barrier(
+        (message, position, half, slope, padded)
+    )
+    gathered = exchange(message)
+    gathered, position, half, slope, padded = lax.optimization_barrier(
+        (gathered, position, half, slope, padded)
+    )
     rows, theirs_five = back_five(gathered, kernel_six, slope, padded, position, half)
     got_five = core_swap(theirs_five)
-    mine_five = mine_of_five(rows, padded, half)
-    pair_five = mine_five + got_five
-    spread = lax.all_to_all(pair_five, "wide", split_axis=0, concat_axis=0, tiled=True)
+    own = own_taps(kernel_six, position)
     next_rows, mine_six, theirs_six = six_own(gathered, own, cot_rows, half)
-    pair_six = mine_six + core_swap(theirs_six)
+    got_six = core_swap(theirs_six)
+    pair_five = mine_of_five(rows, padded, got_five, half)
+    pair_six = total_of(mine_six, [got_six]).astype(jnp.bfloat16)
+    chips_six = from_chips(pair_six)
+    pair_five, pair_six, next_rows = lax.optimization_barrier((pair_five, pair_six, next_rows))
+    spread = exchange(pair_five)
+    spread, chips_six = lax.optimization_barrier((spread, chips_six))
     depth_five = spread.astype(jnp.float32).sum(0).astype(jnp.bfloat16)
-    both = jnp.concatenate([depth_five, pair_six], axis=-1)
-    total = sum_over_chips(both).astype(jnp.bfloat16)
-    other = core_swap(total)
-    first = jnp.where(half == 0, total, other)
-    second = jnp.where(half == 0, other, total)
-    whole = jnp.concatenate([first, second], axis=0)[:27].astype(jnp.float32)
-    out_five = whole[:, :, :128].transpose(0, 2, 1).reshape(3, 3, 3, 128, 16)
-    out_six = whole[:, :, 128:].transpose(0, 2, 1).reshape(3, 3, 3, 256, 16)
+    total_six = total_of(pair_six, chips_six).astype(jnp.bfloat16)
+    total_five = total_of(depth_five, from_chips(depth_five)).astype(jnp.bfloat16)
+    other_five, other_six = core_swap(total_five), core_swap(total_six)
+    out_five, out_six = both_halves(half, total_five, other_five, total_six, other_six)
+    out_five = out_five.transpose(0, 2, 1).reshape(3, 3, 3, 128, 16)
+    out_six = out_six.transpose(0, 2, 1).reshape(3, 3, 3, 256, 16)
     return (next_rows.T.reshape(1, 8, 4, 4, 16), out_five, out_six)
 
 

time: 92.3 us -> 77.6 us (0.84)
  waiting for transfers between devices: 35.3 us -> 14.9 us
  blocking collectives: 0 us -> 18.6 us
  local copies, waits for them, and re-layouts: 10.4 us -> 3.94 us
  other arithmetic: 4.19 us -> 0.27 us
  starting transfers between devices: 27.6 us -> 25.2 us
    all_to_all x0 -> x1, blocking collectives: none -> 18.6 us  [exchange(): lax.all_to_all(values, 'wide', split_axis=0, concat_axis=0, tiled=True)]
    all_to_all x2 -> x1, waiting for transfers between devices: 20.3 us -> 6.94 us  [exchange(): lax.all_to_all(values, 'wide', split_axis=0, concat_axis=0, tiled=True)]
    all_to_all x2 -> x1, starting transfers between devices: 13 us -> 3.63 us  [exchange(): lax.all_to_all(values, 'wide', split_axis=0, concat_axis=0, tiled=True)]
    ppermute x5 -> x8, waiting for transfers between devices: 12.7 us -> 6.5 us  [the longest x6 6.49 us: from_chips(): got.append(lax.ppermute(values, 'dp', pairs))]
    unnamed x18 -> x6, local copies, waits for them, and re-layouts: 7.16 us -> 2.41 us
    ppermute x5 -> x8, starting transfers between devices: 9.6 us -> 13.9 us  [the longest x6 8.57 us: from_chips(): got.append(lax.ppermute(values, 'dp', pairs))]
    ppermute x3 -> x4, starting transfers between devices: 5.04 us -> 7.65 us  [core_swap(): return lax.ppermute(values, 'dp', [(i, i ^ 1) for i in range(count)])]
    slice x1 -> x0, local copies, waits for them, and re-layouts: 1.68 us -> none  [shards(): high = lax.ppermute(slab[:1], 'wide', shift_perm('wide', -1))]
  transfers between devices with their start and end apart: 10 -> 13, of which waited for: 9 -> 7; matrix products, arithmetic and copies ran while one was open for 2% -> 2% of each run, Pallas kernels for 5% -> 6%
where the time goes in v3:
time: 77.6 us; the launch traced here: 77.2 us
  starting transfers between devices  25.2 us (32%)
  blocking collectives  18.6 us (24%)
  waiting for transfers between devices  14.9 us (19%)
  Pallas kernels  13.6 us (18%)
  local copies, waits for them, and re-layouts  3.94 us (5%)
    all_to_all x1, blocking collectives, exchange(): lax.all_to_all(values, 'wide', split_axis=0, concat_axis=0, tiled=True)  18.6 us
    pallas_call x7, Pallas kernels, call(): pl.pallas_call(body, out_shape=out_shape, in_specs=specs, out_specs=outs,...  13.6 us
    ppermute x6, starting transfers between devices, from_chips(): got.append(lax.ppermute(values, 'dp', pairs))  8.57 us
    ppermute x4, starting transfers between devices, core_swap(): return lax.ppermute(values, 'dp', [(i, i ^ 1) for i in range(count)])  7.65 us
    all_to_all x1, waiting for transfers between devices, exchange(): lax.all_to_all(values, 'wide', split_axis=0, concat_axis=0, tiled=True)  6.94 us
    ppermute x6, waiting for transfers between devices, from_chips(): got.append(lax.ppermute(values, 'dp', pairs))  6.49 us
    ppermute x1, starting transfers between devices, shards(): low = lax.ppermute(volume, 'wide', shift_perm('wide', 1))  4.04 us
    all_to_all x1, starting transfers between devices, exchange(): lax.all_to_all(values, 'wide', split_axis=0, concat_axis=0, tiled=True)  3.63 us
  transfers between devices with their start and end apart: 13, of which 7 were waited for; matrix products, arithmetic and copies ran while one was open for 2% of the time, Pallas kernels for 6%

profile of v3, /device:TPU:1, one launch (start us, length us, event | category | flops | bytes accessed | tf_op | source)
XLA Modules:
  0.0 77.2 jit_solution(3528678518104502024)
XLA Ops:
  0.6 4.0 %collective-permute-start = (bf16[1,2,16,16,128]{4,3,2,1,0:T(8,128)(2,1)}, bf16[1,2,16,16,128]{4,3,2,1,0:T(8,128)(2,1)S(1)}, u32[]{:S(2)}, u32[]{:S(2)}) collective-permute-start(bf16[1,2,16,16,128]{4,3,2,1,0:T(8,128)(2,1)} %param.4), channel_id=1, source_target_pairs={{0,1},{1,2},{2,3},{3,4},{4,5},{5,6},{6,7},{7,8},{8,9},{9,10},{10,1... | collective-permute-start | bytes 393224 | tf_op jit(solution)/shard_map/ppermute | solution.py:426
  4.7 1.3 %collective-permute-start.1 = (bf16[1,2,16,16,128]{4,3,2,1,0:T(8,128)(2,1)}, bf16[1,2,16,16,128]{4,3,2,1,0:T(8,128)(2,1)S(1)}, u32[]{:S(2)}, u32[]{:S(2)}) collective-permute-start(bf16[1,2,16,16,128]{4,3,2,1,0:T(8,128)(2,1)} %param.4), channel_id=1, source_target_pairs={{1,0},{2,1},{3,2},{4,3},{5,4},{6,5},{7,6},{8,7},{9,8},{10,9},{11,1... | collective-permute-start | bytes 393224 | tf_op jit(solution)/shard_map/ppermute | solution.py:427
  6.8 1.5 %copy-done.1 = bf16[3,3,3,128,256]{4,3,2,1,0:T(8,128)(2,1)S(1)} copy-done((bf16[3,3,3,128,256]{4,3,2,1,0:T(8,128)(2,1)S(1)}, bf16[3,3,3,128,256]{4,3,2,1,0:T(8,128)(2,1)}, u32[]{:S(2)}) %copy-start.1) | copy-done | bytes 1769496
  8.3 0.9 %copy-done.2 = bf16[1,2,16,16,128]{4,3,2,1,0:T(8,128)(2,1)S(1)} copy-done((bf16[1,2,16,16,128]{4,3,2,1,0:T(8,128)(2,1)S(1)}, bf16[1,2,16,16,128]{4,3,2,1,0:T(8,128)(2,1)}, u32[]{:S(2)}) %copy-start.2) | copy-done | bytes 131096
  9.2 2.2 %shard_map.67 = (f32[512,256]{1,0:T(8,128)S(1)}, bf16[2,288,384]{2,1,0:T(8,128)(2,1)S(1)}, bf16[3456,256]{1,0:T(8,128)(2,1)S(1)}) custom-call(bf16[2,256,128]{2,1,0:T(8,128)(2,1)S(1)} %bitcast.25, bf16[3456,256]{1,0:T(8,128)(2,1)S(1)} %bitcast.24), custom_call_target="tpu_custom_call" | custom-call | flops 600000000 | bytes 4000000 | tf_op jit(solution)/shard_map/pallas_call | solution.py:25
  11.5 0.9 %shard_map.68 = (bf16[16,144,128]{2,1,0:T(8,128)(2,1)S(1)}, f32[512,256]{1,0:T(8,128)S(1)}, bf16[4,288,384]{2,1,0:T(8,128)(2,1)S(1)}) custom-call(bf16[2,256,128]{2,1,0:T(8,128)(2,1)S(1)} %bitcast.19, bf16[2,256,128]{2,1,0:T(8,128)(2,1)S(1)} %bitcast.20, bf16[3456,256]{1,0:T(8,128)(2,1)S(1)} %get-tuple-element.33.kernel, ...), custom_call_target="tpu_custom_call" | custom-call | flops 300000000 | bytes 4000000 | tf_op jit(solution)/shard_map/pallas_call | solution.py:25
  12.4 18.6 %all_to_all.10.gathered = bf16[16,144,128]{2,1,0:T(8,128)(2,1)S(1)} all-to-all(bf16[16,144,128]{2,1,0:T(8,128)(2,1)S(1)} %get-tuple-element.39), channel_id=1, replica_groups=mesh['dp'=8,'wide'=16] {'wide'}, dimensions={0} | all-to-all | bytes 1179648 | tf_op jit(solution)/shard_map/all_to_all | solution.py:420
  30.9 4.9 %shard_map.69 = (bf16[256,512]{1,0:T(8,128)(2,1)S(1)}, bf16[16,14,16,128]{3,2,1,0:T(8,128)(2,1)S(1)}) custom-call(s32[1]{0:T(128)} %bitcast.6.position, s32[1]{0:T(128)} %bitcast.7.half, bf16[16,144,128]{2,1,0:T(8,128)(2,1)S(1)} %all_to_all.10.gathered, bf16[27,256,256]{2,1,0:T(8,128)(2,1)S(1)} %bitcast.17, f32[512,256]{1,0:T(8,128)S(1)} %get-tuple-element.47.slope, ...), custom_call_target="tpu_custom_call" | custom-call | flops 3000000000 | bytes 4000000 | tf_op jit(solution)/shard_map/pallas_call | solution.py:25
  35.9 3.2 %collective-permute-start.2 = (bf16[16,14,16,128]{3,2,1,0:T(8,128)(2,1)S(1)}, bf16[16,14,16,128]{3,2,1,0:T(8,128)(2,1)S(1)}, u32[]{:S(2)}, u32[]{:S(2)}) collective-permute-start(bf16[16,14,16,128]{3,2,1,0:T(8,128)(2,1)S(1)} %get-tuple-element.50), channel_id=1, source_target_pairs={{0,16},{16,0},{32,48},{48,32},{64,80},{80,64},{96,112},{112,96},{1... | collective-permute-start | bytes 2752520 | tf_op jit(solution)/shard_map/ppermute | solution.py:400
  39.1 1.0 %shard_map.71.own = bf16[27,16,256]{2,1,0:T(8,128)(2,1)S(1)} custom-call(s32[1]{0:T(128)} %bitcast.6.position, bf16[27,256,256]{2,1,0:T(8,128)(2,1)S(1)} %bitcast.18), custom_call_target="tpu_custom_call" | custom-call | flops 900000000 | bytes 4000000 | tf_op jit(solution)/shard_map/pallas_call | solution.py:25
  40.1 1.6 %shard_map.72 = (bf16[16,128]{1,0:T(8,128)(2,1)S(1)}, bf16[14,16,256]{2,1,0:T(8,128)(2,1)S(1)}, bf16[14,16,256]{2,1,0:T(8,128)(2,1)S(1)}) custom-call(s32[1]{0:T(128)} %bitcast.7.half, bf16[16,144,128]{2,1,0:T(8,128)(2,1)S(1)} %all_to_all.10.gathered, bf16[27,16,256]{2,1,0:T(8,128)(2,1)S(1)} %shard_map.71.own, bf16[16,128]{1,0:T(8,128)(2,1)S(1)} %bitcast.22), custom_call_target="tpu_custom_call" | custom-call | flops 2000000000 | bytes 4000000 | tf_op jit(solution)/shard_map/pallas_call | solution.py:25
  41.8 1.3 %collective-permute-done.3 = bf16[14,16,256]{2,1,0:T(8,128)(2,1)S(1)} collective-permute-done((bf16[14,16,256]{2,1,0:T(8,128)(2,1)S(1)}, bf16[14,16,256]{2,1,0:T(8,128)(2,1)S(1)}, u32[]{:S(2)}, u32[]{:S(2)}) %collective-permute-start.3) | collective-permute-done | bytes 114720 | tf_op jit(solution)/shard_map/ppermute | solution.py:400
  43.1 2.1 %shard_map.70 = bf16[16,14,16,128]{3,2,1,0:T(8,128)(2,1)} custom-call(s32[1]{0:T(128)} %bitcast.7.half, bf16[256,512]{1,0:T(8,128)(2,1)S(1)} %get-tuple-element.49.rows, bf16[4,288,384]{2,1,0:T(8,128)(2,1)S(1)} %get-tuple-element.48.padded, bf16[16,14,16,128]{3,2,1,0:T(8,128)(2,1)S(1)} %collective-permute-done.2.got), custom_call_target="tpu_custom_call" | custom-call | flops 900000000 | bytes 4000000 | tf_op jit(solution)/shard_map/pallas_call | solution.py:25
  45.2 3.6 %all-to-all-start.1 = ((bf16[16,14,16,128]{3,2,1,0:T(8,128)(2,1)}), bf16[16,14,16,128]{3,2,1,0:T(8,128)(2,1)S(1)}, u32[]{:S(2)}, u32[]{:S(2)}) async-start(bf16[16,14,16,128]{3,2,1,0:T(8,128)(2,1)} %shard_map.70), calls=%async_computation.1 | async-start | bytes 1835008 | tf_op jit(solution)/shard_map/all_to_all | solution.py:420
  48.8 1.3 %collective-permute-start.4 = (bf16[14,16,256]{2,1,0:T(8,128)(2,1)S(1)}, bf16[14,16,256]{2,1,0:T(8,128)(2,1)S(1)}, u32[]{:S(2)}, u32[]{:S(2)}) collective-permute-start(bf16[14,16,256]{2,1,0:T(8,128)(2,1)S(1)} %add_convert_fusion.1), channel_id=1, source_target_pairs={{0,32},{16,48},{32,64},{48,80},{64,96},{80,112},{96,0},{112,16},{1... | collective-permute-start | bytes 344072 | tf_op jit(solution)/shard_map/ppermute | solution.py:408
  50.1 2.4 %collective-permute-start.5 = (bf16[14,16,256]{2,1,0:T(8,128)(2,1)S(1)}, bf16[14,16,256]{2,1,0:T(8,128)(2,1)S(1)}, u32[]{:S(2)}, u32[]{:S(2)}) collective-permute-start(bf16[14,16,256]{2,1,0:T(8,128)(2,1)S(1)} %add_convert_fusion.1), channel_id=1, source_target_pairs={{0,64},{16,80},{32,96},{48,112},{64,0},{80,16},{96,32},{112,48},{1... | collective-permute-start | bytes 344072 | tf_op jit(solution)/shard_map/ppermute | solution.py:408
  52.6 1.2 %collective-permute-start.6 = (bf16[14,16,256]{2,1,0:T(8,128)(2,1)S(1)}, bf16[14,16,256]{2,1,0:T(8,128)(2,1)S(1)}, u32[]{:S(2)}, u32[]{:S(2)}) collective-permute-start(bf16[14,16,256]{2,1,0:T(8,128)(2,1)S(1)} %add_convert_fusion.1), channel_id=1, source_target_pairs={{0,96},{16,112},{32,0},{48,16},{64,32},{80,48},{96,64},{112,80},{1... | collective-permute-start | bytes 344072 | tf_op jit(solution)/shard_map/ppermute | solution.py:408
  53.7 1.0 %collective-permute-done.4 = bf16[14,16,256]{2,1,0:T(8,128)(2,1)S(1)} collective-permute-done((bf16[14,16,256]{2,1,0:T(8,128)(2,1)S(1)}, bf16[14,16,256]{2,1,0:T(8,128)(2,1)S(1)}, u32[]{:S(2)}, u32[]{:S(2)}) %collective-permute-start.4) | collective-permute-done | bytes 114720 | tf_op jit(solution)/shard_map/ppermute | solution.py:408
  54.7 3.4 %collective-permute-done.5 = bf16[14,16,256]{2,1,0:T(8,128)(2,1)S(1)} collective-permute-done((bf16[14,16,256]{2,1,0:T(8,128)(2,1)S(1)}, bf16[14,16,256]{2,1,0:T(8,128)(2,1)S(1)}, u32[]{:S(2)}, u32[]{:S(2)}) %collective-permute-start.5) | collective-permute-done | bytes 114720 | tf_op jit(solution)/shard_map/ppermute | solution.py:408
  58.2 6.9 %all-to-all-done.1 = bf16[16,14,16,128]{3,2,1,0:T(8,128)(2,1)S(1)} async-done(((bf16[16,14,16,128]{3,2,1,0:T(8,128)(2,1)}), bf16[16,14,16,128]{3,2,1,0:T(8,128)(2,1)S(1)}, u32[]{:S(2)}, u32[]{:S(2)}) %all-to-all-start.1) | async-done | bytes 917536 | tf_op jit(solution)/shard_map/all_to_all | solution.py:420
  65.2 2.5 %collective-permute-start.9 = (bf16[14,16,128]{2,1,0:T(8,128)(2,1)S(1)}, bf16[14,16,128]{2,1,0:T(8,128)(2,1)S(1)}, u32[]{:S(2)}, u32[]{:S(2)}) collective-permute-start(bf16[14,16,128]{2,1,0:T(8,128)(2,1)S(1)} %reduce_sum.12), channel_id=1, source_target_pairs={{0,96},{16,112},{32,0},{48,16},{64,32},{80,48},{96,64},{112,80},{1... | collective-permute-start | bytes 172040 | tf_op jit(solution)/shard_map/ppermute | solution.py:408
  69.0 1.9 %collective-permute-start.11 = (bf16[14,16,256]{2,1,0:T(8,128)(2,1)S(1)}, bf16[14,16,256]{2,1,0:T(8,128)(2,1)S(1)}, u32[]{:S(2)}, u32[]{:S(2)}) collective-permute-start(bf16[14,16,256]{2,1,0:T(8,128)(2,1)S(1)} %add_convert_fusion.mine_six), channel_id=1, source_target_pairs={{0,16},{16,0},{32,48},{48,32},{64,80},{80,64},{96,112},{112,96},{1... | collective-permute-start | bytes 344072 | tf_op jit(solution)/shard_map/ppermute | solution.py:400
  70.9 1.5 %collective-permute-done.8 = bf16[14,16,128]{2,1,0:T(8,128)(2,1)S(1)} collective-permute-done((bf16[14,16,128]{2,1,0:T(8,128)(2,1)S(1)}, bf16[14,16,128]{2,1,0:T(8,128)(2,1)S(1)}, u32[]{:S(2)}, u32[]{:S(2)}) %collective-permute-start.8) | collective-permute-done | bytes 57376 | tf_op jit(solution)/shard_map/ppermute | solution.py:408
  73.0 2.5 %collective-permute-start.10 = (bf16[14,16,128]{2,1,0:T(8,128)(2,1)S(1)}, bf16[14,16,128]{2,1,0:T(8,128)(2,1)S(1)}, u32[]{:S(2)}, u32[]{:S(2)}) collective-permute-start(bf16[14,16,128]{2,1,0:T(8,128)(2,1)S(1)} %add_convert_fusion.2.mine_five), channel_id=1, source_target_pairs={{0,16},{16,0},{32,48},{48,32},{64,80},{80,64},{96,112},{112,96},{1... | collective-permute-start | bytes 172040 | tf_op jit(solution)/shard_map/ppermute | solution.py:400
  (22 shorter events, 4.7 us)
Async XLA Ops:
  0.6 10.8 %collective-permute-start = (bf16[1,2,16,16,128]{4,3,2,1,0:T(8,128)(2,1)}, bf16[1,2,16,16,128]{4,3,2,1,0:T(8,128)(2,1)S(1)}, u32[]{:S(2)}, u32[]{:S(2)}) collective-permute-start(bf16[1,2,16,16,128]{4,3,2,1,0:T(8,128)(2,1)} %param.4), channel_id=1, source_target_pairs={{0,1},{1,2},{2,3},{3,4},{4,5},{5,6},{6,7},{7,8},{8,9},{9,10},{10,1... | collective-permute-start | bytes 393224 | tf_op jit(solution)/shard_map/ppermute | solution.py:426
  4.7 6.8 %collective-permute-start.1 = (bf16[1,2,16,16,128]{4,3,2,1,0:T(8,128)(2,1)}, bf16[1,2,16,16,128]{4,3,2,1,0:T(8,128)(2,1)S(1)}, u32[]{:S(2)}, u32[]{:S(2)}) collective-permute-start(bf16[1,2,16,16,128]{4,3,2,1,0:T(8,128)(2,1)} %param.4), channel_id=1, source_target_pairs={{1,0},{2,1},{3,2},{4,3},{5,4},{6,5},{7,6},{8,7},{9,8},{10,9},{11,1... | collective-permute-start | bytes 393224 | tf_op jit(solution)/shard_map/ppermute | solution.py:427
  6.8 1.5 %copy-start.1 = (bf16[3,3,3,128,256]{4,3,2,1,0:T(8,128)(2,1)S(1)}, bf16[3,3,3,128,256]{4,3,2,1,0:T(8,128)(2,1)}, u32[]{:S(2)}) copy-start(bf16[3,3,3,128,256]{4,3,2,1,0:T(8,128)(2,1)} %param.5) | copy-start | bytes 5308420
  8.3 0.9 %copy-start.2 = (bf16[1,2,16,16,128]{4,3,2,1,0:T(8,128)(2,1)S(1)}, bf16[1,2,16,16,128]{4,3,2,1,0:T(8,128)(2,1)}, u32[]{:S(2)}) copy-start(bf16[1,2,16,16,128]{4,3,2,1,0:T(8,128)(2,1)} %param.4) | copy-start | bytes 393220
  11.4 19.5 %copy-start = (bf16[3,3,3,256,256]{4,3,2,1,0:T(8,128)(2,1)S(1)}, bf16[3,3,3,256,256]{4,3,2,1,0:T(8,128)(2,1)}, u32[]{:S(2)}) copy-start(bf16[3,3,3,256,256]{4,3,2,1,0:T(8,128)(2,1)} %param.6) | copy-start | bytes 10616836
  35.9 7.3 %collective-permute-start.2 = (bf16[16,14,16,128]{3,2,1,0:T(8,128)(2,1)S(1)}, bf16[16,14,16,128]{3,2,1,0:T(8,128)(2,1)S(1)}, u32[]{:S(2)}, u32[]{:S(2)}) collective-permute-start(bf16[16,14,16,128]{3,2,1,0:T(8,128)(2,1)S(1)} %get-tuple-element.50), channel_id=1, source_target_pairs={{0,16},{16,0},{32,48},{48,32},{64,80},{80,64},{96,112},{112,96},{1... | collective-permute-start | bytes 2752520 | tf_op jit(solution)/shard_map/ppermute | solution.py:400
  41.7 1.4 %collective-permute-start.3 = (bf16[14,16,256]{2,1,0:T(8,128)(2,1)S(1)}, bf16[14,16,256]{2,1,0:T(8,128)(2,1)S(1)}, u32[]{:S(2)}, u32[]{:S(2)}) collective-permute-start(bf16[14,16,256]{2,1,0:T(8,128)(2,1)S(1)} %get-tuple-element.52), channel_id=1, source_target_pairs={{0,16},{16,0},{32,48},{48,32},{64,80},{80,64},{96,112},{112,96},{1... | collective-permute-start | bytes 344072 | tf_op jit(solution)/shard_map/ppermute | solution.py:400
  45.2 19.9 %all-to-all-start.1 = ((bf16[16,14,16,128]{3,2,1,0:T(8,128)(2,1)}), bf16[16,14,16,128]{3,2,1,0:T(8,128)(2,1)S(1)}, u32[]{:S(2)}, u32[]{:S(2)}) async-start(bf16[16,14,16,128]{3,2,1,0:T(8,128)(2,1)} %shard_map.70), calls=%async_computation.1 | async-start | bytes 1835008 | tf_op jit(solution)/shard_map/all_to_all | solution.py:420
  48.8 5.9 %collective-permute-start.4 = (bf16[14,16,256]{2,1,0:T(8,128)(2,1)S(1)}, bf16[14,16,256]{2,1,0:T(8,128)(2,1)S(1)}, u32[]{:S(2)}, u32[]{:S(2)}) collective-permute-start(bf16[14,16,256]{2,1,0:T(8,128)(2,1)S(1)} %add_convert_fusion.1), channel_id=1, source_target_pairs={{0,32},{16,48},{32,64},{48,80},{64,96},{80,112},{96,0},{112,16},{1... | collective-permute-start | bytes 344072 | tf_op jit(solution)/shard_map/ppermute | solution.py:408
  50.1 8.0 %collective-permute-start.5 = (bf16[14,16,256]{2,1,0:T(8,128)(2,1)S(1)}, bf16[14,16,256]{2,1,0:T(8,128)(2,1)S(1)}, u32[]{:S(2)}, u32[]{:S(2)}) collective-permute-start(bf16[14,16,256]{2,1,0:T(8,128)(2,1)S(1)} %add_convert_fusion.1), channel_id=1, source_target_pairs={{0,64},{16,80},{32,96},{48,112},{64,0},{80,16},{96,32},{112,48},{1... | collective-permute-start | bytes 344072 | tf_op jit(solution)/shard_map/ppermute | solution.py:408
  52.6 5.6 %collective-permute-start.6 = (bf16[14,16,256]{2,1,0:T(8,128)(2,1)S(1)}, bf16[14,16,256]{2,1,0:T(8,128)(2,1)S(1)}, u32[]{:S(2)}, u32[]{:S(2)}) collective-permute-start(bf16[14,16,256]{2,1,0:T(8,128)(2,1)S(1)} %add_convert_fusion.1), channel_id=1, source_target_pairs={{0,96},{16,112},{32,0},{48,16},{64,32},{80,48},{96,64},{112,80},{1... | collective-permute-start | bytes 344072 | tf_op jit(solution)/shard_map/ppermute | solution.py:408
  65.2 5.6 %collective-permute-start.9 = (bf16[14,16,128]{2,1,0:T(8,128)(2,1)S(1)}, bf16[14,16,128]{2,1,0:T(8,128)(2,1)S(1)}, u32[]{:S(2)}, u32[]{:S(2)}) collective-permute-start(bf16[14,16,128]{2,1,0:T(8,128)(2,1)S(1)} %reduce_sum.12), channel_id=1, source_target_pairs={{0,96},{16,112},{32,0},{48,16},{64,32},{80,48},{96,64},{112,80},{1... | collective-permute-start | bytes 172040 | tf_op jit(solution)/shard_map/ppermute | solution.py:408
  67.8 4.6 %collective-permute-start.8 = (bf16[14,16,128]{2,1,0:T(8,128)(2,1)S(1)}, bf16[14,16,128]{2,1,0:T(8,128)(2,1)S(1)}, u32[]{:S(2)}, u32[]{:S(2)}) collective-permute-start(bf16[14,16,128]{2,1,0:T(8,128)(2,1)S(1)} %reduce_sum.12), channel_id=1, source_target_pairs={{0,64},{16,80},{32,96},{48,112},{64,0},{80,16},{96,32},{112,48},{1... | collective-permute-start | bytes 172040 | tf_op jit(solution)/shard_map/ppermute | solution.py:408
  68.3 4.6 %collective-permute-start.7 = (bf16[14,16,128]{2,1,0:T(8,128)(2,1)S(1)}, bf16[14,16,128]{2,1,0:T(8,128)(2,1)S(1)}, u32[]{:S(2)}, u32[]{:S(2)}) collective-permute-start(bf16[14,16,128]{2,1,0:T(8,128)(2,1)S(1)} %reduce_sum.12), channel_id=1, source_target_pairs={{0,32},{16,48},{32,64},{48,80},{64,96},{80,112},{96,0},{112,16},{1... | collective-permute-start | bytes 172040 | tf_op jit(solution)/shard_map/ppermute | solution.py:408
  69.0 7.4 %collective-permute-start.11 = (bf16[14,16,256]{2,1,0:T(8,128)(2,1)S(1)}, bf16[14,16,256]{2,1,0:T(8,128)(2,1)S(1)}, u32[]{:S(2)}, u32[]{:S(2)}) collective-permute-start(bf16[14,16,256]{2,1,0:T(8,128)(2,1)S(1)} %add_convert_fusion.mine_six), channel_id=1, source_target_pairs={{0,16},{16,0},{32,48},{48,32},{64,80},{80,64},{96,112},{112,96},{1... | collective-permute-start | bytes 344072 | tf_op jit(solution)/shard_map/ppermute | solution.py:400
  73.0 3.4 %collective-permute-start.10 = (bf16[14,16,128]{2,1,0:T(8,128)(2,1)S(1)}, bf16[14,16,128]{2,1,0:T(8,128)(2,1)S(1)}, u32[]{:S(2)}, u32[]{:S(2)}) collective-permute-start(bf16[14,16,128]{2,1,0:T(8,128)(2,1)S(1)} %add_convert_fusion.2.mine_five), channel_id=1, source_target_pairs={{0,16},{16,0},{32,48},{48,32},{64,80},{80,64},{96,112},{112,96},{1... | collective-permute-start | bytes 172040 | tf_op jit(solution)/shard_map/ppermute | solution.py:400

commit v4 on v3

--- a/solution.py
+++ b/solution.py
@@ -18,9 +18,12 @@
     return act, slope
 
 
-def call(body, out_shape, scratch, operands, scalars=(), flops=0, limit=16, space=VMEM):
+def call(body, out_shape, scratch, operands, scalars=(), flops=0, limit=16, far=()):
     specs = [pl.BlockSpec(memory_space=pltpu.SMEM)] * len(scalars)
-    specs += [pl.BlockSpec(memory_space=space)] * len(operands)
+    specs += [
+        pl.BlockSpec(memory_space=pltpu.HBM if index in far else VMEM)
+        for index in range(len(operands))
+    ]
     outs = jax.tree.map(lambda _: pl.BlockSpec(memory_space=VMEM), out_shape)
     return pl.pallas_call(
         body,
@@ -28,7 +31,7 @@
         in_specs=specs,
         out_specs=outs,
         scratch_shapes=scratch,
-        compiler_params=pltpu.CompilerParams(vmem_limit_bytes=limit * 1024 * 1024),
+        compiler_params=pltpu.CompilerParams(vmem_limit_bytes=int(limit * 1024 * 1024)),
         cost_estimate=pl.CostEstimate(flops=flops, bytes_accessed=4_000_000, transcendentals=0),
     )(*scalars, *operands)
 
@@ -68,25 +71,22 @@
     return total
 
 
-def inner_kernel(slab_far, kernel_far, part, padded, kernel, slab, marks):
-    loads = [pltpu.make_async_copy(slab_far, slab, marks.at[3])]
-    loads[0].start()
-    takes = {}
+def inner_kernel(slab, kernel_far, part, padded, kernel, marks):
+    loads = {}
     for depth_tap in (1, 2, 0):
         rows = pl.ds(depth_tap * 1152, 1152)
-        takes[depth_tap] = pltpu.make_async_copy(
+        loads[depth_tap] = pltpu.make_async_copy(
             kernel_far.at[rows], kernel.at[rows], marks.at[depth_tap]
         )
-        takes[depth_tap].start()
-    loads[0].wait()
+        loads[depth_tap].start()
     for plane in range(2):
         columns_of(padded, plane, slab[plane])
-    takes[1].wait()
+    loads[1].wait()
     for plane in range(2):
         part[plane * 256 : (plane + 1) * 256, :] = depth_term(padded, plane, kernel, 1)
-    takes[2].wait()
+    loads[2].wait()
     part[0:256, :] += depth_term(padded, 1, kernel, 2)
-    takes[0].wait()
+    loads[0].wait()
     part[256:512, :] += depth_term(padded, 0, kernel, 0)
 
 
@@ -98,16 +98,17 @@
             shape((2, 288, 384), jnp.bfloat16),
             shape((3456, 256), jnp.bfloat16),
         ),
-        [VMEM((2, 256, 128), jnp.bfloat16), pltpu.SemaphoreType.DMA((4,))],
+        [pltpu.SemaphoreType.DMA((3,))],
         (slab.reshape(2, 256, 128), kernel.reshape(3456, 256)),
         flops=600_000_000,
-        space=pltpu.HBM,
-    )
-
-
-def outer_kernel(low, high, kernel, part, inner, cot, message, slope, padded, tall):
-    columns_of(padded, 0, low[1])
-    columns_of(padded, 3, high[0])
+        limit=51,
+        far=(1,),
+    )
+
+
+def outer_kernel(position, low, high, kernel, part, inner, cot, message, slope, padded, tall):
+    columns_of(padded, 0, jnp.where(position[0] == 0, jnp.zeros((256, 128), jnp.bfloat16), low[1]))
+    columns_of(padded, 3, jnp.where(position[0] == 15, jnp.zeros((256, 128), jnp.bfloat16), high[0]))
     padded[1:3] = inner[...]
     acts = []
     for plane in range(2):
@@ -131,7 +132,7 @@
         message[target, 128:144, :] = marks
 
 
-def outer_five(low, high, kernel, part, inner, cot_rows):
+def outer_five(low, high, kernel, part, inner, cot_rows, position):
     return call(
         outer_kernel,
         (
@@ -148,27 +149,8 @@
             inner,
             cot_rows,
         ),
+        (position,),
         flops=300_000_000,
-    )
-
-
-def own_taps_kernel(position, kernel, own):
-    rows = lax.broadcasted_iota(jnp.int32, (16, 256), 0) + position[0] * 16
-    lanes = lax.broadcasted_iota(jnp.int32, (16, 256), 1)
-    pick = jnp.where(rows == lanes, 1.0, 0.0).astype(jnp.bfloat16)
-    for tap in range(27):
-        chosen = lax.dot_general(pick, kernel[tap], NT, preferred_element_type=jnp.float32)
-        own[tap] = chosen.astype(jnp.bfloat16)
-
-
-def own_taps(kernel, position):
-    return call(
-        own_taps_kernel,
-        shape((27, 16, 256), jnp.bfloat16),
-        [],
-        (kernel.reshape(27, 256, 256),),
-        (position,),
-        flops=900_000_000,
     )
 
 
@@ -299,7 +281,15 @@
     return jnp.where(inside, rolled, 0.0)
 
 
-def six_kernel(half, gathered, own, cot, next_rows, mine, theirs, cells, grads, whole):
+def six_kernel(
+    position, half, gathered, kernel, cot, next_rows, mine, theirs, own, cells, grads, whole
+):
+    rows = lax.broadcasted_iota(jnp.int32, (16, 256), 0) + position[0] * 16
+    lanes = lax.broadcasted_iota(jnp.int32, (16, 256), 1)
+    pick = jnp.where(rows == lanes, 1.0, 0.0).astype(jnp.bfloat16)
+    for tap in range(27):
+        chosen = lax.dot_general(pick, kernel[tap], NT, preferred_element_type=jnp.float32)
+        own[tap] = chosen.astype(jnp.bfloat16)
     blank = jnp.zeros((64, 256), jnp.bfloat16)
     cells[0:64, :] = blank
     cells[1088:1152, :] = blank
@@ -353,18 +343,19 @@
     theirs[...] = whole[pl.ds((1 - half[0]) * HALF_TAPS, HALF_TAPS)]
 
 
-def six_own(gathered, own, cot_rows, half):
+def six_own(gathered, kernel, cot_rows, position, half):
     part = shape((HALF_TAPS, 16, 256), jnp.bfloat16)
     return call(
         six_kernel,
         (shape((16, 128), jnp.bfloat16), part, part),
         [
+            VMEM((27, 16, 256), jnp.bfloat16),
             VMEM((1152, 256), jnp.bfloat16),
             VMEM((144, 1024), jnp.bfloat16),
             VMEM((28, 16, 256), jnp.bfloat16),
         ],
-        (gathered, own, cot_rows),
-        (half,),
+        (gathered, kernel.reshape(27, 256, 256), cot_rows),
+        (position, half),
         flops=2_000_000_000,
     )
 
@@ -390,9 +381,9 @@
     )
 
 
-def shift_perm(axis, step):
+def ring_perm(axis, step):
     count = lax.axis_size(axis)
-    return [(i, i + step) for i in range(count) if 0 <= i + step < count]
+    return [(i, (i + step) % count) for i in range(count)]
 
 
 def core_swap(values):
@@ -417,17 +408,19 @@
 
 
 def exchange(values):
-    return lax.all_to_all(values, "wide", split_axis=0, concat_axis=0, tiled=True)
+    flat = values.reshape(values.shape[0], -1, values.shape[-1])
+    got = lax.all_to_all(flat, "wide", split_axis=0, concat_axis=0, tiled=True)
+    return got.reshape(values.shape)
 
 
 def shards(volume, kernel_five, kernel_six, cotangent):
     position = lax.axis_index("wide").astype(jnp.int32).reshape(1)
     half = (lax.axis_index("dp") % 2).astype(jnp.int32).reshape(1)
-    low = lax.ppermute(volume, "wide", shift_perm("wide", 1))
-    high = lax.ppermute(volume, "wide", shift_perm("wide", -1))
+    low = lax.ppermute(volume, "wide", ring_perm("wide", 1))
+    high = lax.ppermute(volume, "wide", ring_perm("wide", -1))
     cot_rows = cotangent[0].reshape(128, 16).T
     part, inner, near_kernel = inner_five(volume, kernel_five)
-    message, slope, padded = outer_five(low, high, near_kernel, part, inner, cot_rows)
+    message, slope, padded = outer_five(low, high, near_kernel, part, inner, cot_rows, position)
     message, position, half, slope, padded = lax.optimization_barrier(
         (message, position, half, slope, padded)
     )
@@ -437,13 +430,14 @@
     )
     rows, theirs_five = back_five(gathered, kernel_six, slope, padded, position, half)
     got_five = core_swap(theirs_five)
-    own = own_taps(kernel_six, position)
-    next_rows, mine_six, theirs_six = six_own(gathered, own, cot_rows, half)
+    next_rows, mine_six, theirs_six = six_own(gathered, kernel_six, cot_rows, position, half)
     got_six = core_swap(theirs_six)
     pair_five = mine_of_five(rows, padded, got_five, half)
+    pair_five, got_six, mine_six, next_rows = lax.optimization_barrier(
+        (pair_five, got_six, mine_six, next_rows)
+    )
     pair_six = total_of(mine_six, [got_six]).astype(jnp.bfloat16)
     chips_six = from_chips(pair_six)
-    pair_five, pair_six, next_rows = lax.optimization_barrier((pair_five, pair_six, next_rows))
     spread = exchange(pair_five)
     spread, chips_six = lax.optimization_barrier((spread, chips_six))
     depth_five = spread.astype(jnp.float32).sum(0).astype(jnp.bfloat16)

time: 77.6 us -> 72.7 us (0.937)
  blocking collectives: 18.6 us -> 15.3 us
  waiting for transfers between devices: 14.9 us -> 12.8 us
  starting transfers between devices: 25.2 us -> 26.9 us
  local copies, waits for them, and re-layouts: 3.94 us -> 2.47 us
    all_to_all x1, waiting for transfers between devices: 6.94 us -> 3.58 us  [exchange(): got = lax.all_to_all(flat, 'wide', split_axis=0, concat_axis=0, tiled=True)]
    all_to_all x1, blocking collectives: 18.6 us -> 15.3 us  [exchange(): got = lax.all_to_all(flat, 'wide', split_axis=0, concat_axis=0, tiled=True)]
    ppermute x6, waiting for transfers between devices: 6.49 us -> 9.08 us  [from_chips(): got.append(lax.ppermute(values, 'dp', pairs))]
    ppermute x2, starting transfers between devices: 5.33 us -> 7.19 us  [the longest x1 4.99 us: shards(): high = lax.ppermute(volume, 'wide', ring_perm('wide', -1))]
    unnamed x6 -> x4, local copies, waits for them, and re-layouts: 2.41 us -> 0.94 us
    ppermute x4, waiting for transfers between devices: 1.48 us -> 0.18 us  [core_swap(): return lax.ppermute(values, 'dp', [(i, i ^ 1) for i in range(count)])]
    ppermute x6, starting transfers between devices: 8.57 us -> 7.34 us  [from_chips(): got.append(lax.ppermute(values, 'dp', pairs))]
    ppermute x4, starting transfers between devices: 7.65 us -> 8.73 us  [core_swap(): return lax.ppermute(values, 'dp', [(i, i ^ 1) for i in range(count)])]
  transfers between devices with their start and end apart: 13 -> 13, of which waited for: 7 -> 7; matrix products, arithmetic and copies ran while one was open for 2% -> 2% of each run, Pallas kernels for 6% -> 10%
where the time goes in v4:
time: 72.7 us; the launch traced here: 72.4 us
  starting transfers between devices  26.9 us (37%)
  blocking collectives  15.3 us (21%)
  Pallas kernels  13.8 us (19%)
  waiting for transfers between devices  12.8 us (18%)
  local copies, waits for them, and re-layouts  2.47 us (3%)
    all_to_all x1, blocking collectives, exchange(): got = lax.all_to_all(flat, 'wide', split_axis=0, concat_axis=0, tiled=True)  15.3 us
    pallas_call x6, Pallas kernels, call(): pl.pallas_call(body, out_shape=out_shape, in_specs=specs, out_specs=outs,...  13.8 us
    ppermute x6, waiting for transfers between devices, from_chips(): got.append(lax.ppermute(values, 'dp', pairs))  9.08 us
    ppermute x4, starting transfers between devices, core_swap(): return lax.ppermute(values, 'dp', [(i, i ^ 1) for i in range(count)])  8.73 us
    ppermute x6, starting transfers between devices, from_chips(): got.append(lax.ppermute(values, 'dp', pairs))  7.34 us
    ppermute x1, starting transfers between devices, shards(): high = lax.ppermute(volume, 'wide', ring_perm('wide', -1))  4.99 us
    all_to_all x1, starting transfers between devices, exchange(): got = lax.all_to_all(flat, 'wide', split_axis=0, concat_axis=0, tiled=True)  3.63 us
    all_to_all x1, waiting for transfers between devices, exchange(): got = lax.all_to_all(flat, 'wide', split_axis=0, concat_axis=0, tiled=True)  3.58 us
  transfers between devices with their start and end apart: 13, of which 7 were waited for; matrix products, arithmetic and copies ran while one was open for 2% of the time, Pallas kernels for 10%

profile of v4, /device:TPU:1, one launch (start us, length us, event | category | flops | bytes accessed | tf_op | source)
XLA Modules:
  0.0 72.4 jit_solution(17387928106714662135)
XLA Ops:
  0.6 2.2 %collective-permute-start = (bf16[1,2,16,16,128]{4,3,2,1,0:T(8,128)(2,1)}, bf16[1,2,16,16,128]{4,3,2,1,0:T(8,128)(2,1)S(1)}, u32[]{:S(2)}, u32[]{:S(2)}) collective-permute-start(bf16[1,2,16,16,128]{4,3,2,1,0:T(8,128)(2,1)} %param.4), channel_id=1, source_target_pairs={{0,1},{1,2},{2,3},{3,4},{4,5},{5,6},{6,7},{7,8},{8,9},{9,10},{10,1... | collective-permute-start | bytes 393224 | tf_op jit(solution)/shard_map/ppermute | solution.py:419
  2.8 5.0 %collective-permute-start.1 = (bf16[1,2,16,16,128]{4,3,2,1,0:T(8,128)(2,1)}, bf16[1,2,16,16,128]{4,3,2,1,0:T(8,128)(2,1)S(1)}, u32[]{:S(2)}, u32[]{:S(2)}) collective-permute-start(bf16[1,2,16,16,128]{4,3,2,1,0:T(8,128)(2,1)} %param.4), channel_id=1, source_target_pairs={{0,15},{1,0},{2,1},{3,2},{4,3},{5,4},{6,5},{7,6},{8,7},{9,8},{10,9... | collective-permute-start | bytes 393224 | tf_op jit(solution)/shard_map/ppermute | solution.py:420
  7.8 0.8 %copy.9 = bf16[128,16]{0,1:T(8,128)(2,1)S(1)} copy(bf16[128,16]{1,0:T(8,128)(2,1)} %bitcast.28) | data formatting | bytes 8192 | tf_op jit(solution)/shard_map/reshape;squeeze | solution.py:421
  8.6 0.9 %copy-done.1 = bf16[1,2,16,16,128]{4,3,2,1,0:T(8,128)(2,1)S(1)} copy-done((bf16[1,2,16,16,128]{4,3,2,1,0:T(8,128)(2,1)S(1)}, bf16[1,2,16,16,128]{4,3,2,1,0:T(8,128)(2,1)}, u32[]{:S(2)}) %copy-start.1) | copy-done | bytes 131096
  9.6 2.7 %shard_map.67 = (f32[512,256]{1,0:T(8,128)S(1)}, bf16[2,288,384]{2,1,0:T(8,128)(2,1)S(1)}, bf16[3456,256]{1,0:T(8,128)(2,1)S(1)}) custom-call(bf16[2,256,128]{2,1,0:T(8,128)(2,1)S(1)} %bitcast.26, bf16[3456,256]{1,0:T(8,128)(2,1)} %bitcast.30), custom_call_target="tpu_custom_call" | custom-call | flops 600000000 | bytes 4000000 | tf_op jit(solution)/shard_map/pallas_call | solution.py:28
  12.3 0.9 %shard_map.68 = (bf16[16,144,128]{2,1,0:T(8,128)(2,1)S(1)}, f32[512,256]{1,0:T(8,128)S(1)}, bf16[4,288,384]{2,1,0:T(8,128)(2,1)S(1)}) custom-call(s32[1]{0:T(128)} %bitcast.position, bf16[2,256,128]{2,1,0:T(8,128)(2,1)S(1)} %bitcast.19, bf16[2,256,128]{2,1,0:T(8,128)(2,1)S(1)} %bitcast.20, bf16[3456,256]{1,0:T(8,128)(2,1)S(1)} %get-tuple-element.34.kernel, ...), custom_call_target="tpu_custom_call" | custom-call | flops 300000000 | bytes 4000000 | tf_op jit(solution)/shard_map/pallas_call | solution.py:28
  13.1 15.3 %all_to_all.10.gathered = bf16[16,144,128]{2,1,0:T(8,128)(2,1)S(1)} all-to-all(bf16[16,144,128]{2,1,0:T(8,128)(2,1)S(1)} %get-tuple-element.40), channel_id=1, replica_groups=mesh['dp'=8,'wide'=16] {'wide'}, dimensions={0} | all-to-all | bytes 1179648 | tf_op jit(solution)/shard_map/all_to_all | solution.py:412
  28.5 4.9 %shard_map.69 = (bf16[256,512]{1,0:T(8,128)(2,1)S(1)}, bf16[16,14,16,128]{3,2,1,0:T(8,128)(2,1)S(1)}) custom-call(s32[1]{0:T(128)} %bitcast.position, s32[1]{0:T(128)} %bitcast.7.half, bf16[16,144,128]{2,1,0:T(8,128)(2,1)S(1)} %all_to_all.10.gathered, bf16[27,256,256]{2,1,0:T(8,128)(2,1)S(1)} %bitcast.24, f32[512,256]{1,0:T(8,128)S(1)} %get-tuple-element.48.slope, ...), custom_call_target="tpu_custom_call" | custom-call | flops 3000000000 | bytes 4000000 | tf_op jit(solution)/shard_map/pallas_call | solution.py:28
  33.4 2.8 %collective-permute-start.2 = (bf16[16,14,16,128]{3,2,1,0:T(8,128)(2,1)S(1)}, bf16[16,14,16,128]{3,2,1,0:T(8,128)(2,1)S(1)}, u32[]{:S(2)}, u32[]{:S(2)}) collective-permute-start(bf16[16,14,16,128]{3,2,1,0:T(8,128)(2,1)S(1)} %get-tuple-element.51), channel_id=1, source_target_pairs={{0,16},{16,0},{32,48},{48,32},{64,80},{80,64},{96,112},{112,96},{1... | collective-permute-start | bytes 2752520 | tf_op jit(solution)/shard_map/ppermute | solution.py:391
  36.2 2.4 %shard_map.71 = (bf16[16,128]{1,0:T(8,128)(2,1)S(1)}, bf16[14,16,256]{2,1,0:T(8,128)(2,1)S(1)}, bf16[14,16,256]{2,1,0:T(8,128)(2,1)S(1)}) custom-call(s32[1]{0:T(128)} %bitcast.position, s32[1]{0:T(128)} %bitcast.7.half, bf16[16,144,128]{2,1,0:T(8,128)(2,1)S(1)} %all_to_all.10.gathered, bf16[27,256,256]{2,1,0:T(8,128)(2,1)S(1)} %bitcast.25, ...), custom_call_target="tpu_custom_call" | custom-call | flops 2000000000 | bytes 4000000 | tf_op jit(solution)/shard_map/pallas_call | solution.py:28
  38.7 2.1 %shard_map.70 = bf16[16,14,16,128]{3,2,1,0:T(8,128)(2,1)} custom-call(s32[1]{0:T(128)} %bitcast.7.half, bf16[256,512]{1,0:T(8,128)(2,1)S(1)} %get-tuple-element.50.rows, bf16[4,288,384]{2,1,0:T(8,128)(2,1)S(1)} %get-tuple-element.49.padded, bf16[16,14,16,128]{3,2,1,0:T(8,128)(2,1)S(1)} %collective-permute-done.2.got), custom_call_target="tpu_custom_call" | custom-call | flops 900000000 | bytes 4000000 | tf_op jit(solution)/shard_map/pallas_call | solution.py:28
  40.8 3.6 %all-to-all-start.1 = ((bf16[16,224,128]{2,1,0:T(8,128)(2,1)}), bf16[16,224,128]{2,1,0:T(8,128)(2,1)S(1)}, u32[]{:S(2)}, u32[]{:S(2)}) async-start(bf16[16,224,128]{2,1,0:T(8,128)(2,1)} %bitcast.11), calls=%async_computation.1 | async-start | bytes 1835008 | tf_op jit(solution)/shard_map/all_to_all | solution.py:412
  44.5 2.5 %collective-permute-start.6 = (bf16[14,16,256]{2,1,0:T(8,128)(2,1)S(1)}, bf16[14,16,256]{2,1,0:T(8,128)(2,1)S(1)}, u32[]{:S(2)}, u32[]{:S(2)}) collective-permute-start(bf16[14,16,256]{2,1,0:T(8,128)(2,1)S(1)} %add_convert_fusion.1), channel_id=1, source_target_pairs={{0,96},{16,112},{32,0},{48,16},{64,32},{80,48},{96,64},{112,80},{1... | collective-permute-start | bytes 344072 | tf_op jit(solution)/shard_map/ppermute | solution.py:399
  47.5 0.6 collective-permute-start.4
  48.1 1.1 %collective-permute-done.6 = bf16[14,16,256]{2,1,0:T(8,128)(2,1)S(1)} collective-permute-done((bf16[14,16,256]{2,1,0:T(8,128)(2,1)S(1)}, bf16[14,16,256]{2,1,0:T(8,128)(2,1)S(1)}, u32[]{:S(2)}, u32[]{:S(2)}) %collective-permute-start.6) | collective-permute-done | bytes 114720 | tf_op jit(solution)/shard_map/ppermute | solution.py:399
  49.3 3.2 %collective-permute-done.5 = bf16[14,16,256]{2,1,0:T(8,128)(2,1)S(1)} collective-permute-done((bf16[14,16,256]{2,1,0:T(8,128)(2,1)S(1)}, bf16[14,16,256]{2,1,0:T(8,128)(2,1)S(1)}, u32[]{:S(2)}, u32[]{:S(2)}) %collective-permute-start.5) | collective-permute-done | bytes 114720 | tf_op jit(solution)/shard_map/ppermute | solution.py:399
  52.5 3.4 %collective-permute-done.4 = bf16[14,16,256]{2,1,0:T(8,128)(2,1)S(1)} collective-permute-done((bf16[14,16,256]{2,1,0:T(8,128)(2,1)S(1)}, bf16[14,16,256]{2,1,0:T(8,128)(2,1)S(1)}, u32[]{:S(2)}, u32[]{:S(2)}) %collective-permute-start.4) | collective-permute-done | bytes 114720 | tf_op jit(solution)/shard_map/ppermute | solution.py:399
  55.9 3.6 %all-to-all-done.1 = bf16[16,224,128]{2,1,0:T(8,128)(2,1)S(1)} async-done(((bf16[16,224,128]{2,1,0:T(8,128)(2,1)}), bf16[16,224,128]{2,1,0:T(8,128)(2,1)S(1)}, u32[]{:S(2)}, u32[]{:S(2)}) %all-to-all-start.1) | async-done | bytes 917536 | tf_op jit(solution)/shard_map/all_to_all | solution.py:412
  59.6 2.5 %collective-permute-start.9 = (bf16[14,16,128]{2,1,0:T(8,128)(2,1)S(1)}, bf16[14,16,128]{2,1,0:T(8,128)(2,1)S(1)}, u32[]{:S(2)}, u32[]{:S(2)}) collective-permute-start(bf16[14,16,128]{2,1,0:T(8,128)(2,1)S(1)} %reduce_sum.12), channel_id=1, source_target_pairs={{0,96},{16,112},{32,0},{48,16},{64,32},{80,48},{96,64},{112,80},{1... | collective-permute-start | bytes 172040 | tf_op jit(solution)/shard_map/ppermute | solution.py:399
  63.4 2.6 %collective-permute-start.11 = (bf16[14,16,256]{2,1,0:T(8,128)(2,1)S(1)}, bf16[14,16,256]{2,1,0:T(8,128)(2,1)S(1)}, u32[]{:S(2)}, u32[]{:S(2)}) collective-permute-start(bf16[14,16,256]{2,1,0:T(8,128)(2,1)S(1)} %add_convert_fusion.mine_six), channel_id=1, source_target_pairs={{0,16},{16,0},{32,48},{48,32},{64,80},{80,64},{96,112},{112,96},{1... | collective-permute-start | bytes 344072 | tf_op jit(solution)/shard_map/ppermute | solution.py:391
  66.0 0.8 %collective-permute-done.8 = bf16[14,16,128]{2,1,0:T(8,128)(2,1)S(1)} collective-permute-done((bf16[14,16,128]{2,1,0:T(8,128)(2,1)S(1)}, bf16[14,16,128]{2,1,0:T(8,128)(2,1)S(1)}, u32[]{:S(2)}, u32[]{:S(2)}) %collective-permute-start.8) | collective-permute-done | bytes 57376 | tf_op jit(solution)/shard_map/ppermute | solution.py:399
  67.4 3.2 %collective-permute-start.10 = (bf16[14,16,128]{2,1,0:T(8,128)(2,1)S(1)}, bf16[14,16,128]{2,1,0:T(8,128)(2,1)S(1)}, u32[]{:S(2)}, u32[]{:S(2)}) collective-permute-start(bf16[14,16,128]{2,1,0:T(8,128)(2,1)S(1)} %add_convert_fusion.2.mine_five), channel_id=1, source_target_pairs={{0,16},{16,0},{32,48},{48,32},{64,80},{80,64},{96,112},{112,96},{1... | collective-permute-start | bytes 172040 | tf_op jit(solution)/shard_map/ppermute | solution.py:391
  70.6 0.7 copy.10
  71.5 0.9 %shard_map.72 = (f32[27,16,128]{2,1,0:T(8,128)}, f32[27,16,256]{2,1,0:T(8,128)}) custom-call(s32[1]{0:T(128)} %bitcast.7.half, bf16[14,16,128]{2,1,0:T(8,128)(2,1)S(1)} %add_convert_fusion.2.mine_five, bf16[14,16,128]{2,1,0:T(8,128)(2,1)S(1)} %collective-permute-done.10.other_five, bf16[14,16,256]{2,1,0:T(8,128)(2,1)S(1)} %add_convert_fusion.mine_six, ...), custom_call_target="tpu_custom_call" | custom-call | bytes 4000000 | tf_op jit(solution)/shard_map/pallas_call | solution.py:28
  (19 shorter events, 2.8 us)
Async XLA Ops:
  0.6 11.6 %collective-permute-start = (bf16[1,2,16,16,128]{4,3,2,1,0:T(8,128)(2,1)}, bf16[1,2,16,16,128]{4,3,2,1,0:T(8,128)(2,1)S(1)}, u32[]{:S(2)}, u32[]{:S(2)}) collective-permute-start(bf16[1,2,16,16,128]{4,3,2,1,0:T(8,128)(2,1)} %param.4), channel_id=1, source_target_pairs={{0,1},{1,2},{2,3},{3,4},{4,5},{5,6},{6,7},{7,8},{8,9},{9,10},{10,1... | collective-permute-start | bytes 393224 | tf_op jit(solution)/shard_map/ppermute | solution.py:419
  2.8 9.4 %collective-permute-start.1 = (bf16[1,2,16,16,128]{4,3,2,1,0:T(8,128)(2,1)}, bf16[1,2,16,16,128]{4,3,2,1,0:T(8,128)(2,1)S(1)}, u32[]{:S(2)}, u32[]{:S(2)}) collective-permute-start(bf16[1,2,16,16,128]{4,3,2,1,0:T(8,128)(2,1)} %param.4), channel_id=1, source_target_pairs={{0,15},{1,0},{2,1},{3,2},{4,3},{5,4},{6,5},{7,6},{8,7},{9,8},{10,9... | collective-permute-start | bytes 393224 | tf_op jit(solution)/shard_map/ppermute | solution.py:420
  8.6 0.9 %copy-start.1 = (bf16[1,2,16,16,128]{4,3,2,1,0:T(8,128)(2,1)S(1)}, bf16[1,2,16,16,128]{4,3,2,1,0:T(8,128)(2,1)}, u32[]{:S(2)}) copy-start(bf16[1,2,16,16,128]{4,3,2,1,0:T(8,128)(2,1)} %param.4) | copy-start | bytes 393220
  12.2 16.2 %copy-start = (bf16[3,3,3,256,256]{4,3,2,1,0:T(8,128)(2,1)S(1)}, bf16[3,3,3,256,256]{4,3,2,1,0:T(8,128)(2,1)}, u32[]{:S(2)}) copy-start(bf16[3,3,3,256,256]{4,3,2,1,0:T(8,128)(2,1)} %param.6) | copy-start | bytes 10616836
  33.4 5.3 %collective-permute-start.2 = (bf16[16,14,16,128]{3,2,1,0:T(8,128)(2,1)S(1)}, bf16[16,14,16,128]{3,2,1,0:T(8,128)(2,1)S(1)}, u32[]{:S(2)}, u32[]{:S(2)}) collective-permute-start(bf16[16,14,16,128]{3,2,1,0:T(8,128)(2,1)S(1)} %get-tuple-element.51), channel_id=1, source_target_pairs={{0,16},{16,0},{32,48},{48,32},{64,80},{80,64},{96,112},{112,96},{1... | collective-permute-start | bytes 2752520 | tf_op jit(solution)/shard_map/ppermute | solution.py:391
  38.6 2.2 %collective-permute-start.3 = (bf16[14,16,256]{2,1,0:T(8,128)(2,1)S(1)}, bf16[14,16,256]{2,1,0:T(8,128)(2,1)S(1)}, u32[]{:S(2)}, u32[]{:S(2)}) collective-permute-start(bf16[14,16,256]{2,1,0:T(8,128)(2,1)S(1)} %get-tuple-element.52), channel_id=1, source_target_pairs={{0,16},{16,0},{32,48},{48,32},{64,80},{80,64},{96,112},{112,96},{1... | collective-permute-start | bytes 344072 | tf_op jit(solution)/shard_map/ppermute | solution.py:391
  40.8 18.7 %all-to-all-start.1 = ((bf16[16,224,128]{2,1,0:T(8,128)(2,1)}), bf16[16,224,128]{2,1,0:T(8,128)(2,1)S(1)}, u32[]{:S(2)}, u32[]{:S(2)}) async-start(bf16[16,224,128]{2,1,0:T(8,128)(2,1)} %bitcast.11), calls=%async_computation.1 | async-start | bytes 1835008 | tf_op jit(solution)/shard_map/all_to_all | solution.py:412
  44.5 4.8 %collective-permute-start.6 = (bf16[14,16,256]{2,1,0:T(8,128)(2,1)S(1)}, bf16[14,16,256]{2,1,0:T(8,128)(2,1)S(1)}, u32[]{:S(2)}, u32[]{:S(2)}) collective-permute-start(bf16[14,16,256]{2,1,0:T(8,128)(2,1)S(1)} %add_convert_fusion.1), channel_id=1, source_target_pairs={{0,96},{16,112},{32,0},{48,16},{64,32},{80,48},{96,64},{112,80},{1... | collective-permute-start | bytes 344072 | tf_op jit(solution)/shard_map/ppermute | solution.py:399
  47.0 5.4 %collective-permute-start.5 = (bf16[14,16,256]{2,1,0:T(8,128)(2,1)S(1)}, bf16[14,16,256]{2,1,0:T(8,128)(2,1)S(1)}, u32[]{:S(2)}, u32[]{:S(2)}) collective-permute-start(bf16[14,16,256]{2,1,0:T(8,128)(2,1)S(1)} %add_convert_fusion.1), channel_id=1, source_target_pairs={{0,64},{16,80},{32,96},{48,112},{64,0},{80,16},{96,32},{112,48},{1... | collective-permute-start | bytes 344072 | tf_op jit(solution)/shard_map/ppermute | solution.py:399
  47.5 8.4 %collective-permute-start.4 = (bf16[14,16,256]{2,1,0:T(8,128)(2,1)S(1)}, bf16[14,16,256]{2,1,0:T(8,128)(2,1)S(1)}, u32[]{:S(2)}, u32[]{:S(2)}) collective-permute-start(bf16[14,16,256]{2,1,0:T(8,128)(2,1)S(1)} %add_convert_fusion.1), channel_id=1, source_target_pairs={{0,32},{16,48},{32,64},{48,80},{64,96},{80,112},{96,0},{112,16},{1... | collective-permute-start | bytes 344072 | tf_op jit(solution)/shard_map/ppermute | solution.py:399
  59.6 6.4 %collective-permute-start.9 = (bf16[14,16,128]{2,1,0:T(8,128)(2,1)S(1)}, bf16[14,16,128]{2,1,0:T(8,128)(2,1)S(1)}, u32[]{:S(2)}, u32[]{:S(2)}) collective-permute-start(bf16[14,16,128]{2,1,0:T(8,128)(2,1)S(1)} %reduce_sum.12), channel_id=1, source_target_pairs={{0,96},{16,112},{32,0},{48,16},{64,32},{80,48},{96,64},{112,80},{1... | collective-permute-start | bytes 172040 | tf_op jit(solution)/shard_map/ppermute | solution.py:399
  62.2 4.6 %collective-permute-start.8 = (bf16[14,16,128]{2,1,0:T(8,128)(2,1)S(1)}, bf16[14,16,128]{2,1,0:T(8,128)(2,1)S(1)}, u32[]{:S(2)}, u32[]{:S(2)}) collective-permute-start(bf16[14,16,128]{2,1,0:T(8,128)(2,1)S(1)} %reduce_sum.12), channel_id=1, source_target_pairs={{0,64},{16,80},{32,96},{48,112},{64,0},{80,16},{96,32},{112,48},{1... | collective-permute-start | bytes 172040 | tf_op jit(solution)/shard_map/ppermute | solution.py:399
  62.7 4.6 %collective-permute-start.7 = (bf16[14,16,128]{2,1,0:T(8,128)(2,1)S(1)}, bf16[14,16,128]{2,1,0:T(8,128)(2,1)S(1)}, u32[]{:S(2)}, u32[]{:S(2)}) collective-permute-start(bf16[14,16,128]{2,1,0:T(8,128)(2,1)S(1)} %reduce_sum.12), channel_id=1, source_target_pairs={{0,32},{16,48},{32,64},{48,80},{64,96},{80,112},{96,0},{112,16},{1... | collective-permute-start | bytes 172040 | tf_op jit(solution)/shard_map/ppermute | solution.py:399
  63.4 8.1 %collective-permute-start.11 = (bf16[14,16,256]{2,1,0:T(8,128)(2,1)S(1)}, bf16[14,16,256]{2,1,0:T(8,128)(2,1)S(1)}, u32[]{:S(2)}, u32[]{:S(2)}) collective-permute-start(bf16[14,16,256]{2,1,0:T(8,128)(2,1)S(1)} %add_convert_fusion.mine_six), channel_id=1, source_target_pairs={{0,16},{16,0},{32,48},{48,32},{64,80},{80,64},{96,112},{112,96},{1... | collective-permute-start | bytes 344072 | tf_op jit(solution)/shard_map/ppermute | solution.py:391
  67.4 4.1 %collective-permute-start.10 = (bf16[14,16,128]{2,1,0:T(8,128)(2,1)S(1)}, bf16[14,16,128]{2,1,0:T(8,128)(2,1)S(1)}, u32[]{:S(2)}, u32[]{:S(2)}) collective-permute-start(bf16[14,16,128]{2,1,0:T(8,128)(2,1)S(1)} %add_convert_fusion.2.mine_five), channel_id=1, source_target_pairs={{0,16},{16,0},{32,48},{48,32},{64,80},{80,64},{96,112},{112,96},{1... | collective-permute-start | bytes 172040 | tf_op jit(solution)/shard_map/ppermute | solution.py:391

commit v5 on v4

--- a/solution.py
+++ b/solution.py
@@ -190,7 +190,6 @@
     cot = gathered[:, 128:144, :].reshape(256, 128)
     upstream = lax.dot_general(grow, cot, NT, preferred_element_type=jnp.float32)
     grad_six = (upstream * slant).astype(jnp.bfloat16).astype(jnp.float32)
-    grad_pooled = jnp.zeros((64, 256), jnp.float32)
     blank = jnp.zeros((8, 256), jnp.float32)
     for depth_tap in range(3):
         values = grad_six[(2 - depth_tap) * 64 : (3 - depth_tap) * 64]
@@ -203,12 +202,20 @@
                     cells = moved
                 else:
                     cells = jnp.concatenate([blank, moved[:56]], axis=0)
-                grad_pooled += lax.dot_general(
-                    cells.astype(jnp.bfloat16),
-                    kernel[depth_tap * 9 + row_tap * 3 + col_tap],
-                    NT,
-                    preferred_element_type=jnp.float32,
-                )
+                lane = (row_tap * 3 + col_tap) * 256
+                near[depth_tap, :, lane : lane + 256] = cells.astype(jnp.bfloat16)
+
+    def depth_of(depth_tap, total):
+        for tap in range(9):
+            total += lax.dot_general(
+                near[depth_tap, :, tap * 256 : tap * 256 + 256],
+                kernel[depth_tap * 9 + tap],
+                NT,
+                preferred_element_type=jnp.float32,
+            )
+        return total
+
+    grad_pooled = lax.fori_loop(0, 3, depth_of, jnp.zeros((64, 256), jnp.float32))
     for side in range(2):
         tall[side, pl.ds(0, 64, stride=2), :] = grad_pooled[:, side * 128 : (side + 1) * 128]
         tall[side, pl.ds(1, 64, stride=2), :] = grad_pooled[:, side * 128 : (side + 1) * 128]
@@ -219,25 +226,31 @@
         rows_out[:, plane * 256 : (plane + 1) * 256] = grad.T.astype(jnp.bfloat16)
 
 
+def tap_cells(padded, plane, tap):
+    depth_tap, row_tap, col_tap = tap // 9, (tap // 3) % 3, tap % 3
+    return padded[
+        plane + depth_tap,
+        pl.ds(pl.multiple_of(row_tap * 16, 16), 256),
+        pl.ds(pl.multiple_of(col_tap * 128, 128), 128),
+    ]
+
+
 def half_of_five(first, rows, padded, out, got=None):
-    for step in range(HALF_TAPS):
-        tap = jnp.minimum(first + step, 26)
-        depth_tap, row_tap, col_tap = tap // 9, (tap // 3) % 3, tap % 3
-        total = jnp.zeros((256, 128), jnp.float32)
+    for step in range(0, HALF_TAPS, 2):
+        taps = [jnp.minimum(first + step + other, 26) for other in range(2)]
+        total = jnp.zeros((256, 256), jnp.float32)
         for plane in range(2):
-            cells = padded[
-                plane + depth_tap,
-                pl.ds(pl.multiple_of(row_tap * 16, 16), 256),
-                pl.ds(pl.multiple_of(col_tap * 128, 128), 128),
-            ]
+            cells = jnp.concatenate([tap_cells(padded, plane, tap) for tap in taps], axis=1)
             total += jnp.dot(
                 rows[:, plane * 256 : (plane + 1) * 256],
                 cells,
                 preferred_element_type=jnp.float32,
             )
-        if got is not None:
-            total += got[:, step].reshape(256, 128).astype(jnp.float32)
-        out[:, step] = total.astype(jnp.bfloat16).reshape(16, 16, 128)
+        for other in range(2):
+            part = total[:, other * 128 : (other + 1) * 128]
+            if got is not None:
+                part += got[:, step + other].reshape(256, 128).astype(jnp.float32)
+            out[:, step + other] = part.astype(jnp.bfloat16).reshape(16, 16, 128)
 
 
 def back_kernel(position, half, gathered, kernel, slope, padded, rows, theirs, near, tall):
@@ -295,14 +308,10 @@
     cells[1088:1152, :] = blank
     cells[64:1088, 0:128] = gathered[:, 0:64, :].reshape(1024, 128)
     cells[64:1088, 128:256] = gathered[:, 64:128, :].reshape(1024, 128)
-    taps = jnp.zeros((144, 1024), jnp.float32)
-    for depth_tap in range(3):
-        taps += lax.dot_general(
-            own[depth_tap * 9 : depth_tap * 9 + 9].reshape(144, 256),
-            cells[depth_tap * 64 : depth_tap * 64 + 1024, :],
-            NT,
-            preferred_element_type=jnp.float32,
-        )
+    products = lax.dot_general(
+        own[...].reshape(432, 256), cells[...], NT, preferred_element_type=jnp.float32
+    )
+    taps = products[0:144, 0:1024] + products[144:288, 64:1088] + products[288:432, 128:1152]
     pre = jnp.zeros((16, 1024), jnp.float32)
     for row_tap in range(3):
         line = jnp.zeros((16, 1024), jnp.float32)

time: 72.7 us -> 70.6 us (0.971)
  Pallas kernels: 13.8 us -> 11.7 us
    pallas_call x6, Pallas kernels: 13.8 us -> 11.7 us  [call(): pl.pallas_call(body, out_shape=out_shape, in_specs=specs, out_specs=outs,...]
  transfers between devices with their start and end apart: 13 -> 13, of which waited for: 7 -> 7; matrix products, arithmetic and copies ran while one was open for 2% -> 2% of each run, Pallas kernels for 10% -> 9%
where the time goes in v5:
time: 70.6 us; the launch traced here: 70.3 us
  starting transfers between devices  26.9 us (38%)
  blocking collectives  15.3 us (22%)
  waiting for transfers between devices  12.9 us (18%)
  Pallas kernels  11.7 us (17%)
  local copies, waits for them, and re-layouts  2.47 us (3%)
  between operations  0.72 us (1%)
    all_to_all x1, blocking collectives, exchange(): got = lax.all_to_all(flat, 'wide', split_axis=0, concat_axis=0, tiled=True)  15.3 us
    pallas_call x6, Pallas kernels, call(): pl.pallas_call(body, out_shape=out_shape, in_specs=specs, out_specs=outs,...  11.7 us
    ppermute x6, waiting for transfers between devices, from_chips(): got.append(lax.ppermute(values, 'dp', pairs))  9.11 us
    ppermute x4, starting transfers between devices, core_swap(): return lax.ppermute(values, 'dp', [(i, i ^ 1) for i in range(count)])  8.74 us
    ppermute x6, starting transfers between devices, from_chips(): got.append(lax.ppermute(values, 'dp', pairs))  7.34 us
    ppermute x1, starting transfers between devices, shards(): high = lax.ppermute(volume, 'wide', ring_perm('wide', -1))  4.99 us
    all_to_all x1, starting transfers between devices, exchange(): got = lax.all_to_all(flat, 'wide', split_axis=0, concat_axis=0, tiled=True)  3.63 us
    all_to_all x1, waiting for transfers between devices, exchange(): got = lax.all_to_all(flat, 'wide', split_axis=0, concat_axis=0, tiled=True)  3.59 us
  transfers between devices with their start and end apart: 13, of which 7 were waited for; matrix products, arithmetic and copies ran while one was open for 2% of the time, Pallas kernels for 9%

profile of v5, /device:TPU:1, one launch (start us, length us, event | category | flops | bytes accessed | tf_op | source)
XLA Modules:
  0.0 70.3 jit_solution(3206141622956327863)
XLA Ops:
  0.6 2.2 %collective-permute-start = (bf16[1,2,16,16,128]{4,3,2,1,0:T(8,128)(2,1)}, bf16[1,2,16,16,128]{4,3,2,1,0:T(8,128)(2,1)S(1)}, u32[]{:S(2)}, u32[]{:S(2)}) collective-permute-start(bf16[1,2,16,16,128]{4,3,2,1,0:T(8,128)(2,1)} %param.4), channel_id=1, source_target_pairs={{0,1},{1,2},{2,3},{3,4},{4,5},{5,6},{6,7},{7,8},{8,9},{9,10},{10,1... | collective-permute-start | bytes 393224 | tf_op jit(solution)/shard_map/ppermute | solution.py:428
  2.8 5.0 %collective-permute-start.1 = (bf16[1,2,16,16,128]{4,3,2,1,0:T(8,128)(2,1)}, bf16[1,2,16,16,128]{4,3,2,1,0:T(8,128)(2,1)S(1)}, u32[]{:S(2)}, u32[]{:S(2)}) collective-permute-start(bf16[1,2,16,16,128]{4,3,2,1,0:T(8,128)(2,1)} %param.4), channel_id=1, source_target_pairs={{0,15},{1,0},{2,1},{3,2},{4,3},{5,4},{6,5},{7,6},{8,7},{9,8},{10,9... | collective-permute-start | bytes 393224 | tf_op jit(solution)/shard_map/ppermute | solution.py:429
  7.8 0.8 %copy.9 = bf16[128,16]{0,1:T(8,128)(2,1)S(1)} copy(bf16[128,16]{1,0:T(8,128)(2,1)} %bitcast.28) | data formatting | bytes 8192 | tf_op jit(solution)/shard_map/reshape;squeeze | solution.py:430
  8.6 0.9 %copy-done.1 = bf16[1,2,16,16,128]{4,3,2,1,0:T(8,128)(2,1)S(1)} copy-done((bf16[1,2,16,16,128]{4,3,2,1,0:T(8,128)(2,1)S(1)}, bf16[1,2,16,16,128]{4,3,2,1,0:T(8,128)(2,1)}, u32[]{:S(2)}) %copy-start.1) | copy-done | bytes 131096
  9.6 2.7 %shard_map.67 = (f32[512,256]{1,0:T(8,128)S(1)}, bf16[2,288,384]{2,1,0:T(8,128)(2,1)S(1)}, bf16[3456,256]{1,0:T(8,128)(2,1)S(1)}) custom-call(bf16[2,256,128]{2,1,0:T(8,128)(2,1)S(1)} %bitcast.26, bf16[3456,256]{1,0:T(8,128)(2,1)} %bitcast.30), custom_call_target="tpu_custom_call" | custom-call | flops 600000000 | bytes 4000000 | tf_op jit(solution)/shard_map/pallas_call | solution.py:28
  12.3 0.9 %shard_map.68 = (bf16[16,144,128]{2,1,0:T(8,128)(2,1)S(1)}, f32[512,256]{1,0:T(8,128)S(1)}, bf16[4,288,384]{2,1,0:T(8,128)(2,1)S(1)}) custom-call(s32[1]{0:T(128)} %bitcast.position, bf16[2,256,128]{2,1,0:T(8,128)(2,1)S(1)} %bitcast.19, bf16[2,256,128]{2,1,0:T(8,128)(2,1)S(1)} %bitcast.20, bf16[3456,256]{1,0:T(8,128)(2,1)S(1)} %get-tuple-element.34.kernel, ...), custom_call_target="tpu_custom_call" | custom-call | flops 300000000 | bytes 4000000 | tf_op jit(solution)/shard_map/pallas_call | solution.py:28
  13.1 15.3 %all_to_all.10.gathered = bf16[16,144,128]{2,1,0:T(8,128)(2,1)S(1)} all-to-all(bf16[16,144,128]{2,1,0:T(8,128)(2,1)S(1)} %get-tuple-element.40), channel_id=1, replica_groups=mesh['dp'=8,'wide'=16] {'wide'}, dimensions={0} | all-to-all | bytes 1179648 | tf_op jit(solution)/shard_map/all_to_all | solution.py:421
  28.5 3.3 %shard_map.69 = (bf16[256,512]{1,0:T(8,128)(2,1)S(1)}, bf16[16,14,16,128]{3,2,1,0:T(8,128)(2,1)S(1)}) custom-call(s32[1]{0:T(128)} %bitcast.position, s32[1]{0:T(128)} %bitcast.7.half, bf16[16,144,128]{2,1,0:T(8,128)(2,1)S(1)} %all_to_all.10.gathered, bf16[27,256,256]{2,1,0:T(8,128)(2,1)S(1)} %bitcast.24, f32[512,256]{1,0:T(8,128)S(1)} %get-tuple-element.48.slope, ...), custom_call_target="tpu_custom_call" | custom-call | flops 3000000000 | bytes 4000000 | tf_op jit(solution)/shard_map/pallas_call | solution.py:28
  31.8 2.8 %collective-permute-start.2 = (bf16[16,14,16,128]{3,2,1,0:T(8,128)(2,1)S(1)}, bf16[16,14,16,128]{3,2,1,0:T(8,128)(2,1)S(1)}, u32[]{:S(2)}, u32[]{:S(2)}) collective-permute-start(bf16[16,14,16,128]{3,2,1,0:T(8,128)(2,1)S(1)} %get-tuple-element.51), channel_id=1, source_target_pairs={{0,16},{16,0},{32,48},{48,32},{64,80},{80,64},{96,112},{112,96},{1... | collective-permute-start | bytes 2752520 | tf_op jit(solution)/shard_map/ppermute | solution.py:400
  34.6 2.3 %shard_map.71 = (bf16[16,128]{1,0:T(8,128)(2,1)S(1)}, bf16[14,16,256]{2,1,0:T(8,128)(2,1)S(1)}, bf16[14,16,256]{2,1,0:T(8,128)(2,1)S(1)}) custom-call(s32[1]{0:T(128)} %bitcast.position, s32[1]{0:T(128)} %bitcast.7.half, bf16[16,144,128]{2,1,0:T(8,128)(2,1)S(1)} %all_to_all.10.gathered, bf16[27,256,256]{2,1,0:T(8,128)(2,1)S(1)} %bitcast.25, ...), custom_call_target="tpu_custom_call" | custom-call | flops 2000000000 | bytes 4000000 | tf_op jit(solution)/shard_map/pallas_call | solution.py:28
  37.0 1.7 %shard_map.70 = bf16[16,14,16,128]{3,2,1,0:T(8,128)(2,1)} custom-call(s32[1]{0:T(128)} %bitcast.7.half, bf16[256,512]{1,0:T(8,128)(2,1)S(1)} %get-tuple-element.50.rows, bf16[4,288,384]{2,1,0:T(8,128)(2,1)S(1)} %get-tuple-element.49.padded, bf16[16,14,16,128]{3,2,1,0:T(8,128)(2,1)S(1)} %collective-permute-done.2.got), custom_call_target="tpu_custom_call" | custom-call | flops 900000000 | bytes 4000000 | tf_op jit(solution)/shard_map/pallas_call | solution.py:28
  38.7 3.6 %all-to-all-start.1 = ((bf16[16,224,128]{2,1,0:T(8,128)(2,1)}), bf16[16,224,128]{2,1,0:T(8,128)(2,1)S(1)}, u32[]{:S(2)}, u32[]{:S(2)}) async-start(bf16[16,224,128]{2,1,0:T(8,128)(2,1)} %bitcast.11), calls=%async_computation.1 | async-start | bytes 1835008 | tf_op jit(solution)/shard_map/all_to_all | solution.py:421
  42.4 2.5 %collective-permute-start.6 = (bf16[14,16,256]{2,1,0:T(8,128)(2,1)S(1)}, bf16[14,16,256]{2,1,0:T(8,128)(2,1)S(1)}, u32[]{:S(2)}, u32[]{:S(2)}) collective-permute-start(bf16[14,16,256]{2,1,0:T(8,128)(2,1)S(1)} %add_convert_fusion.1), channel_id=1, source_target_pairs={{0,96},{16,112},{32,0},{48,16},{64,32},{80,48},{96,64},{112,80},{1... | collective-permute-start | bytes 344072 | tf_op jit(solution)/shard_map/ppermute | solution.py:408
  46.0 1.1 %collective-permute-done.6 = bf16[14,16,256]{2,1,0:T(8,128)(2,1)S(1)} collective-permute-done((bf16[14,16,256]{2,1,0:T(8,128)(2,1)S(1)}, bf16[14,16,256]{2,1,0:T(8,128)(2,1)S(1)}, u32[]{:S(2)}, u32[]{:S(2)}) %collective-permute-start.6) | collective-permute-done | bytes 114720 | tf_op jit(solution)/shard_map/ppermute | solution.py:408
  47.2 3.2 %collective-permute-done.5 = bf16[14,16,256]{2,1,0:T(8,128)(2,1)S(1)} collective-permute-done((bf16[14,16,256]{2,1,0:T(8,128)(2,1)S(1)}, bf16[14,16,256]{2,1,0:T(8,128)(2,1)S(1)}, u32[]{:S(2)}, u32[]{:S(2)}) %collective-permute-start.5) | collective-permute-done | bytes 114720 | tf_op jit(solution)/shard_map/ppermute | solution.py:408
  50.4 3.5 %collective-permute-done.4 = bf16[14,16,256]{2,1,0:T(8,128)(2,1)S(1)} collective-permute-done((bf16[14,16,256]{2,1,0:T(8,128)(2,1)S(1)}, bf16[14,16,256]{2,1,0:T(8,128)(2,1)S(1)}, u32[]{:S(2)}, u32[]{:S(2)}) %collective-permute-start.4) | collective-permute-done | bytes 114720 | tf_op jit(solution)/shard_map/ppermute | solution.py:408
  53.8 3.6 %all-to-all-done.1 = bf16[16,224,128]{2,1,0:T(8,128)(2,1)S(1)} async-done(((bf16[16,224,128]{2,1,0:T(8,128)(2,1)}), bf16[16,224,128]{2,1,0:T(8,128)(2,1)S(1)}, u32[]{:S(2)}, u32[]{:S(2)}) %all-to-all-start.1) | async-done | bytes 917536 | tf_op jit(solution)/shard_map/all_to_all | solution.py:421
  57.5 2.5 %collective-permute-start.9 = (bf16[14,16,128]{2,1,0:T(8,128)(2,1)S(1)}, bf16[14,16,128]{2,1,0:T(8,128)(2,1)S(1)}, u32[]{:S(2)}, u32[]{:S(2)}) collective-permute-start(bf16[14,16,128]{2,1,0:T(8,128)(2,1)S(1)} %reduce_sum.12), channel_id=1, source_target_pairs={{0,96},{16,112},{32,0},{48,16},{64,32},{80,48},{96,64},{112,80},{1... | collective-permute-start | bytes 172040 | tf_op jit(solution)/shard_map/ppermute | solution.py:408
  60.6 0.6 collective-permute-start.7
  61.3 2.6 %collective-permute-start.11 = (bf16[14,16,256]{2,1,0:T(8,128)(2,1)S(1)}, bf16[14,16,256]{2,1,0:T(8,128)(2,1)S(1)}, u32[]{:S(2)}, u32[]{:S(2)}) collective-permute-start(bf16[14,16,256]{2,1,0:T(8,128)(2,1)S(1)} %add_convert_fusion.mine_six), channel_id=1, source_target_pairs={{0,16},{16,0},{32,48},{48,32},{64,80},{80,64},{96,112},{112,96},{1... | collective-permute-start | bytes 344072 | tf_op jit(solution)/shard_map/ppermute | solution.py:400
  63.9 0.8 %collective-permute-done.8 = bf16[14,16,128]{2,1,0:T(8,128)(2,1)S(1)} collective-permute-done((bf16[14,16,128]{2,1,0:T(8,128)(2,1)S(1)}, bf16[14,16,128]{2,1,0:T(8,128)(2,1)S(1)}, u32[]{:S(2)}, u32[]{:S(2)}) %collective-permute-start.8) | collective-permute-done | bytes 57376 | tf_op jit(solution)/shard_map/ppermute | solution.py:408
  65.3 3.2 %collective-permute-start.10 = (bf16[14,16,128]{2,1,0:T(8,128)(2,1)S(1)}, bf16[14,16,128]{2,1,0:T(8,128)(2,1)S(1)}, u32[]{:S(2)}, u32[]{:S(2)}) collective-permute-start(bf16[14,16,128]{2,1,0:T(8,128)(2,1)S(1)} %add_convert_fusion.2.mine_five), channel_id=1, source_target_pairs={{0,16},{16,0},{32,48},{48,32},{64,80},{80,64},{96,112},{112,96},{1... | collective-permute-start | bytes 172040 | tf_op jit(solution)/shard_map/ppermute | solution.py:400
  68.5 0.7 %copy.10 = bf16[128,16]{1,0:T(8,128)(2,1)} copy(bf16[128,16]{0,1:T(8,128)(2,1)S(1)} %bitcast.23) | data formatting | bytes 8192 | tf_op jit(solution)/shard_map/transpose | solution.py:459
  69.4 0.9 %shard_map.72 = (f32[27,16,128]{2,1,0:T(8,128)}, f32[27,16,256]{2,1,0:T(8,128)}) custom-call(s32[1]{0:T(128)} %bitcast.7.half, bf16[14,16,128]{2,1,0:T(8,128)(2,1)S(1)} %add_convert_fusion.2.mine_five, bf16[14,16,128]{2,1,0:T(8,128)(2,1)S(1)} %collective-permute-done.10.other_five, bf16[14,16,256]{2,1,0:T(8,128)(2,1)S(1)} %add_convert_fusion.mine_six, ...), custom_call_target="tpu_custom_call" | custom-call | bytes 4000000 | tf_op jit(solution)/shard_map/pallas_call | solution.py:28
  (19 shorter events, 2.8 us)
Async XLA Ops:
  0.6 11.6 %collective-permute-start = (bf16[1,2,16,16,128]{4,3,2,1,0:T(8,128)(2,1)}, bf16[1,2,16,16,128]{4,3,2,1,0:T(8,128)(2,1)S(1)}, u32[]{:S(2)}, u32[]{:S(2)}) collective-permute-start(bf16[1,2,16,16,128]{4,3,2,1,0:T(8,128)(2,1)} %param.4), channel_id=1, source_target_pairs={{0,1},{1,2},{2,3},{3,4},{4,5},{5,6},{6,7},{7,8},{8,9},{9,10},{10,1... | collective-permute-start | bytes 393224 | tf_op jit(solution)/shard_map/ppermute | solution.py:428
  2.8 9.4 %collective-permute-start.1 = (bf16[1,2,16,16,128]{4,3,2,1,0:T(8,128)(2,1)}, bf16[1,2,16,16,128]{4,3,2,1,0:T(8,128)(2,1)S(1)}, u32[]{:S(2)}, u32[]{:S(2)}) collective-permute-start(bf16[1,2,16,16,128]{4,3,2,1,0:T(8,128)(2,1)} %param.4), channel_id=1, source_target_pairs={{0,15},{1,0},{2,1},{3,2},{4,3},{5,4},{6,5},{7,6},{8,7},{9,8},{10,9... | collective-permute-start | bytes 393224 | tf_op jit(solution)/shard_map/ppermute | solution.py:429
  8.6 0.9 %copy-start.1 = (bf16[1,2,16,16,128]{4,3,2,1,0:T(8,128)(2,1)S(1)}, bf16[1,2,16,16,128]{4,3,2,1,0:T(8,128)(2,1)}, u32[]{:S(2)}) copy-start(bf16[1,2,16,16,128]{4,3,2,1,0:T(8,128)(2,1)} %param.4) | copy-start | bytes 393220
  12.2 16.2 %copy-start = (bf16[3,3,3,256,256]{4,3,2,1,0:T(8,128)(2,1)S(1)}, bf16[3,3,3,256,256]{4,3,2,1,0:T(8,128)(2,1)}, u32[]{:S(2)}) copy-start(bf16[3,3,3,256,256]{4,3,2,1,0:T(8,128)(2,1)} %param.6) | copy-start | bytes 10616836
  31.8 5.2 %collective-permute-start.2 = (bf16[16,14,16,128]{3,2,1,0:T(8,128)(2,1)S(1)}, bf16[16,14,16,128]{3,2,1,0:T(8,128)(2,1)S(1)}, u32[]{:S(2)}, u32[]{:S(2)}) collective-permute-start(bf16[16,14,16,128]{3,2,1,0:T(8,128)(2,1)S(1)} %get-tuple-element.51), channel_id=1, source_target_pairs={{0,16},{16,0},{32,48},{48,32},{64,80},{80,64},{96,112},{112,96},{1... | collective-permute-start | bytes 2752520 | tf_op jit(solution)/shard_map/ppermute | solution.py:400
  36.9 1.8 %collective-permute-start.3 = (bf16[14,16,256]{2,1,0:T(8,128)(2,1)S(1)}, bf16[14,16,256]{2,1,0:T(8,128)(2,1)S(1)}, u32[]{:S(2)}, u32[]{:S(2)}) collective-permute-start(bf16[14,16,256]{2,1,0:T(8,128)(2,1)S(1)} %get-tuple-element.52), channel_id=1, source_target_pairs={{0,16},{16,0},{32,48},{48,32},{64,80},{80,64},{96,112},{112,96},{1... | collective-permute-start | bytes 344072 | tf_op jit(solution)/shard_map/ppermute | solution.py:400
  38.7 18.7 %all-to-all-start.1 = ((bf16[16,224,128]{2,1,0:T(8,128)(2,1)}), bf16[16,224,128]{2,1,0:T(8,128)(2,1)S(1)}, u32[]{:S(2)}, u32[]{:S(2)}) async-start(bf16[16,224,128]{2,1,0:T(8,128)(2,1)} %bitcast.11), calls=%async_computation.1 | async-start | bytes 1835008 | tf_op jit(solution)/shard_map/all_to_all | solution.py:421
  42.4 4.8 %collective-permute-start.6 = (bf16[14,16,256]{2,1,0:T(8,128)(2,1)S(1)}, bf16[14,16,256]{2,1,0:T(8,128)(2,1)S(1)}, u32[]{:S(2)}, u32[]{:S(2)}) collective-permute-start(bf16[14,16,256]{2,1,0:T(8,128)(2,1)S(1)} %add_convert_fusion.1), channel_id=1, source_target_pairs={{0,96},{16,112},{32,0},{48,16},{64,32},{80,48},{96,64},{112,80},{1... | collective-permute-start | bytes 344072 | tf_op jit(solution)/shard_map/ppermute | solution.py:408
  44.9 5.4 %collective-permute-start.5 = (bf16[14,16,256]{2,1,0:T(8,128)(2,1)S(1)}, bf16[14,16,256]{2,1,0:T(8,128)(2,1)S(1)}, u32[]{:S(2)}, u32[]{:S(2)}) collective-permute-start(bf16[14,16,256]{2,1,0:T(8,128)(2,1)S(1)} %add_convert_fusion.1), channel_id=1, source_target_pairs={{0,64},{16,80},{32,96},{48,112},{64,0},{80,16},{96,32},{112,48},{1... | collective-permute-start | bytes 344072 | tf_op jit(solution)/shard_map/ppermute | solution.py:408
  45.4 8.4 %collective-permute-start.4 = (bf16[14,16,256]{2,1,0:T(8,128)(2,1)S(1)}, bf16[14,16,256]{2,1,0:T(8,128)(2,1)S(1)}, u32[]{:S(2)}, u32[]{:S(2)}) collective-permute-start(bf16[14,16,256]{2,1,0:T(8,128)(2,1)S(1)} %add_convert_fusion.1), channel_id=1, source_target_pairs={{0,32},{16,48},{32,64},{48,80},{64,96},{80,112},{96,0},{112,16},{1... | collective-permute-start | bytes 344072 | tf_op jit(solution)/shard_map/ppermute | solution.py:408
  57.5 6.4 %collective-permute-start.9 = (bf16[14,16,128]{2,1,0:T(8,128)(2,1)S(1)}, bf16[14,16,128]{2,1,0:T(8,128)(2,1)S(1)}, u32[]{:S(2)}, u32[]{:S(2)}) collective-permute-start(bf16[14,16,128]{2,1,0:T(8,128)(2,1)S(1)} %reduce_sum.12), channel_id=1, source_target_pairs={{0,96},{16,112},{32,0},{48,16},{64,32},{80,48},{96,64},{112,80},{1... | collective-permute-start | bytes 172040 | tf_op jit(solution)/shard_map/ppermute | solution.py:408
  60.1 4.6 %collective-permute-start.8 = (bf16[14,16,128]{2,1,0:T(8,128)(2,1)S(1)}, bf16[14,16,128]{2,1,0:T(8,128)(2,1)S(1)}, u32[]{:S(2)}, u32[]{:S(2)}) collective-permute-start(bf16[14,16,128]{2,1,0:T(8,128)(2,1)S(1)} %reduce_sum.12), channel_id=1, source_target_pairs={{0,64},{16,80},{32,96},{48,112},{64,0},{80,16},{96,32},{112,48},{1... | collective-permute-start | bytes 172040 | tf_op jit(solution)/shard_map/ppermute | solution.py:408
  60.6 4.6 %collective-permute-start.7 = (bf16[14,16,128]{2,1,0:T(8,128)(2,1)S(1)}, bf16[14,16,128]{2,1,0:T(8,128)(2,1)S(1)}, u32[]{:S(2)}, u32[]{:S(2)}) collective-permute-start(bf16[14,16,128]{2,1,0:T(8,128)(2,1)S(1)} %reduce_sum.12), channel_id=1, source_target_pairs={{0,32},{16,48},{32,64},{48,80},{64,96},{80,112},{96,0},{112,16},{1... | collective-permute-start | bytes 172040 | tf_op jit(solution)/shard_map/ppermute | solution.py:408
  61.3 8.1 %collective-permute-start.11 = (bf16[14,16,256]{2,1,0:T(8,128)(2,1)S(1)}, bf16[14,16,256]{2,1,0:T(8,128)(2,1)S(1)}, u32[]{:S(2)}, u32[]{:S(2)}) collective-permute-start(bf16[14,16,256]{2,1,0:T(8,128)(2,1)S(1)} %add_convert_fusion.mine_six), channel_id=1, source_target_pairs={{0,16},{16,0},{32,48},{48,32},{64,80},{80,64},{96,112},{112,96},{1... | collective-permute-start | bytes 344072 | tf_op jit(solution)/shard_map/ppermute | solution.py:400
  65.3 4.1 %collective-permute-start.10 = (bf16[14,16,128]{2,1,0:T(8,128)(2,1)S(1)}, bf16[14,16,128]{2,1,0:T(8,128)(2,1)S(1)}, u32[]{:S(2)}, u32[]{:S(2)}) collective-permute-start(bf16[14,16,128]{2,1,0:T(8,128)(2,1)S(1)} %add_convert_fusion.2.mine_five), channel_id=1, source_target_pairs={{0,16},{16,0},{32,48},{48,32},{64,80},{80,64},{96,112},{112,96},{1... | collective-permute-start | bytes 172040 | tf_op jit(solution)/shard_map/ppermute | solution.py:400

commit v6 on v5

--- a/solution.py
+++ b/solution.py
@@ -18,13 +18,14 @@
     return act, slope
 
 
-def call(body, out_shape, scratch, operands, scalars=(), flops=0, limit=16, far=()):
+def call(body, out_shape, scratch, operands, scalars=(), flops=0, limit=16, far=(), far_out=False):
     specs = [pl.BlockSpec(memory_space=pltpu.SMEM)] * len(scalars)
     specs += [
         pl.BlockSpec(memory_space=pltpu.HBM if index in far else VMEM)
         for index in range(len(operands))
     ]
-    outs = jax.tree.map(lambda _: pl.BlockSpec(memory_space=VMEM), out_shape)
+    place = pltpu.HBM if far_out else VMEM
+    outs = jax.tree.map(lambda _: pl.BlockSpec(memory_space=place), out_shape)
     return pl.pallas_call(
         body,
         out_shape=out_shape,
@@ -59,16 +60,18 @@
     padded[index, 16:272, 256:384] = shifted_rows(values, 1, 16).astype(jnp.bfloat16)
 
 
-def depth_term(padded, index, kernel, depth_tap):
-    total = jnp.zeros((256, 256), jnp.float32)
-    for row_tap in range(3):
-        start = (depth_tap * 3 + row_tap) * 384
-        total += jnp.dot(
-            padded[index, 16 * row_tap : 16 * row_tap + 256, :],
-            kernel[start : start + 384, :],
-            preferred_element_type=jnp.float32,
-        )
-    return total
+def depth_term(padded, first, planes, kernel, depth_tap):
+    cells = jnp.concatenate(
+        [
+            padded[first : first + planes, 16 * row_tap : 16 * row_tap + 256, :].reshape(
+                256 * planes, 384
+            )
+            for row_tap in range(3)
+        ],
+        axis=1,
+    )
+    taps = kernel[depth_tap * 1152 : depth_tap * 1152 + 1152, :]
+    return jnp.dot(cells, taps, preferred_element_type=jnp.float32)
 
 
 def inner_kernel(slab, kernel_far, part, padded, kernel, marks):
@@ -83,11 +86,11 @@
         columns_of(padded, plane, slab[plane])
     loads[1].wait()
     for plane in range(2):
-        part[plane * 256 : (plane + 1) * 256, :] = depth_term(padded, plane, kernel, 1)
+        part[plane * 256 : (plane + 1) * 256, :] = depth_term(padded, plane, 1, kernel, 1)
     loads[2].wait()
-    part[0:256, :] += depth_term(padded, 1, kernel, 2)
+    part[0:256, :] += depth_term(padded, 1, 1, kernel, 2)
     loads[0].wait()
-    part[256:512, :] += depth_term(padded, 0, kernel, 0)
+    part[256:512, :] += depth_term(padded, 0, 1, kernel, 0)
 
 
 def inner_five(slab, kernel):
@@ -113,7 +116,7 @@
     acts = []
     for plane in range(2):
         total = part[plane * 256 : (plane + 1) * 256, :]
-        total += depth_term(padded, 3 * plane, kernel, 2 * plane)
+        total += depth_term(padded, 3 * plane, 1, kernel, 2 * plane)
         act, slant = both_of(total)
         slope[plane * 256 : (plane + 1) * 256, :] = slant
         acts.append(act)
@@ -125,7 +128,17 @@
         even = tall[side, pl.ds(0, 64, stride=2), :]
         odd = tall[side, pl.ds(1, 64, stride=2), :]
         pooled.append(((even + odd) * 0.125).astype(jnp.bfloat16))
-    marks = cot[...]
+    cells = cot[...].astype(jnp.float32).reshape(128, 16)
+    same = lax.broadcasted_iota(jnp.int32, (16, 16), 0) == lax.broadcasted_iota(
+        jnp.int32, (16, 16), 1
+    )
+    unit = jnp.where(same, 1.0, 0.0)
+    marks = lax.dot_general(
+        unit.astype(jnp.bfloat16),
+        cells.astype(jnp.bfloat16),
+        NT,
+        preferred_element_type=jnp.float32,
+    ).astype(jnp.bfloat16)
     for target in range(16):
         message[target, 0:64, :] = pooled[0]
         message[target, 64:128, :] = pooled[1]
@@ -235,7 +248,7 @@
     ]
 
 
-def half_of_five(first, rows, padded, out, got=None):
+def half_of_five(first, rows, padded, out, got=None, send=None):
     for step in range(0, HALF_TAPS, 2):
         taps = [jnp.minimum(first + step + other, 26) for other in range(2)]
         total = jnp.zeros((256, 256), jnp.float32)
@@ -251,6 +264,8 @@
             if got is not None:
                 part += got[:, step + other].reshape(256, 128).astype(jnp.float32)
             out[:, step + other] = part.astype(jnp.bfloat16).reshape(16, 16, 128)
+        if send is not None:
+            send(step)
 
 
 def back_kernel(position, half, gathered, kernel, slope, padded, rows, theirs, near, tall):
@@ -269,18 +284,33 @@
     )
 
 
-def mine_kernel(half, rows, padded, got, mine):
-    half_of_five(half[0] * HALF_TAPS, rows, padded, mine, got)
+def mine_kernel(half, rows, padded, got, mine, staged, marks):
+    sends = []
+
+    def send(step):
+        pair = pl.ds(step, 2)
+        sends.append(
+            pltpu.make_async_copy(staged.at[:, pair], mine.at[:, pair], marks.at[step // 2])
+        )
+        sends[-1].start()
+
+    half_of_five(half[0] * HALF_TAPS, rows, padded, staged, got, send)
+    for copy in sends:
+        copy.wait()
 
 
 def mine_of_five(rows, padded, got, half):
     return call(
         mine_kernel,
         shape((16, HALF_TAPS, 16, 128), jnp.bfloat16),
-        [],
+        [
+            VMEM((16, HALF_TAPS, 16, 128), jnp.bfloat16),
+            pltpu.SemaphoreType.DMA((HALF_TAPS // 2,)),
+        ],
         (rows, padded, got),
         (half,),
         flops=900_000_000,
+        far_out=True,
     )
 
 
@@ -295,7 +325,7 @@
 
 
 def six_kernel(
-    position, half, gathered, kernel, cot, next_rows, mine, theirs, own, cells, grads, whole
+    position, half, gathered, kernel, next_rows, mine, theirs, own, cells, grads, whole
 ):
     rows = lax.broadcasted_iota(jnp.int32, (16, 256), 0) + position[0] * 16
     lanes = lax.broadcasted_iota(jnp.int32, (16, 256), 1)
@@ -324,7 +354,8 @@
     cell = lax.broadcasted_iota(jnp.int32, (128, 1024), 1)
     target = (cell >> 7) * 16 + ((cell % 64) >> 4) * 4 + ((cell % 8) >> 1)
     grow = jnp.where(small == target, 1.0, 0.0).astype(jnp.bfloat16)
-    upstream = jnp.dot(cot[...], grow, preferred_element_type=jnp.float32)
+    cot = gathered[position[0], 128:144, :]
+    upstream = jnp.dot(cot, grow, preferred_element_type=jnp.float32)
     high = act.astype(jnp.bfloat16)
     rest = act - high.astype(jnp.float32)
     middle = rest.astype(jnp.bfloat16)
@@ -352,7 +383,7 @@
     theirs[...] = whole[pl.ds((1 - half[0]) * HALF_TAPS, HALF_TAPS)]
 
 
-def six_own(gathered, kernel, cot_rows, position, half):
+def six_own(gathered, kernel, position, half):
     part = shape((HALF_TAPS, 16, 256), jnp.bfloat16)
     return call(
         six_kernel,
@@ -363,7 +394,7 @@
             VMEM((144, 1024), jnp.bfloat16),
             VMEM((28, 16, 256), jnp.bfloat16),
         ],
-        (gathered, kernel.reshape(27, 256, 256), cot_rows),
+        (gathered, kernel.reshape(27, 256, 256)),
         (position, half),
         flops=2_000_000_000,
     )
@@ -427,7 +458,7 @@
     half = (lax.axis_index("dp") % 2).astype(jnp.int32).reshape(1)
     low = lax.ppermute(volume, "wide", ring_perm("wide", 1))
     high = lax.ppermute(volume, "wide", ring_perm("wide", -1))
-    cot_rows = cotangent[0].reshape(128, 16).T
+    cot_rows = cotangent.reshape(32, 4, 16)
     part, inner, near_kernel = inner_five(volume, kernel_five)
     message, slope, padded = outer_five(low, high, near_kernel, part, inner, cot_rows, position)
     message, position, half, slope, padded = lax.optimization_barrier(
@@ -439,7 +470,7 @@
     )
     rows, theirs_five = back_five(gathered, kernel_six, slope, padded, position, half)
     got_five = core_swap(theirs_five)
-    next_rows, mine_six, theirs_six = six_own(gathered, kernel_six, cot_rows, position, half)
+    next_rows, mine_six, theirs_six = six_own(gathered, kernel_six, position, half)
     got_six = core_swap(theirs_six)
     pair_five = mine_of_five(rows, padded, got_five, half)
     pair_five, got_six, mine_six, next_rows = lax.optimization_barrier(

time: 70.6 us -> 70.3 us (level)
  blocking collectives: 15.3 us -> 16.3 us
  local copies, waits for them, and re-layouts: 2.47 us -> 1.67 us
    all_to_all x1, blocking collectives: 15.3 us -> 16.3 us  [exchange(): got = lax.all_to_all(flat, 'wide', split_axis=0, concat_axis=0, tiled=True)]
    another operation x1 -> x0, local copies, waits for them, and re-layouts: 0.81 us -> none  [shards(): cot_rows = cotangent[0].reshape(128, 16).T]
  transfers between devices with their start and end apart: 13 -> 13, of which waited for: 7 -> 7; matrix products, arithmetic and copies ran while one was open for 2% -> 1% of each run, Pallas kernels for 9% -> 9%
where the time goes in v6:
time: 70.3 us; the launch traced here: 70.1 us
  starting transfers between devices  26.9 us (38%)
  blocking collectives  16.3 us (23%)
  waiting for transfers between devices  12.9 us (18%)
  Pallas kernels  11.3 us (16%)
  local copies, waits for them, and re-layouts  1.67 us (2%)
  between operations  0.76 us (1%)
    all_to_all x1, blocking collectives, exchange(): got = lax.all_to_all(flat, 'wide', split_axis=0, concat_axis=0, tiled=True)  16.3 us
    pallas_call x6, Pallas kernels, call(): pl.pallas_call(body, out_shape=out_shape, in_specs=specs, out_specs=outs,...  11.3 us
    ppermute x6, waiting for transfers between devices, from_chips(): got.append(lax.ppermute(values, 'dp', pairs))  9.09 us
    ppermute x4, starting transfers between devices, core_swap(): return lax.ppermute(values, 'dp', [(i, i ^ 1) for i in range(count)])  8.73 us
    ppermute x6, starting transfers between devices, from_chips(): got.append(lax.ppermute(values, 'dp', pairs))  7.35 us
    ppermute x1, starting transfers between devices, shards(): high = lax.ppermute(volume, 'wide', ring_perm('wide', -1))  4.99 us
    all_to_all x1, starting transfers between devices, exchange(): got = lax.all_to_all(flat, 'wide', split_axis=0, concat_axis=0, tiled=True)  3.65 us
    all_to_all x1, waiting for transfers between devices, exchange(): got = lax.all_to_all(flat, 'wide', split_axis=0, concat_axis=0, tiled=True)  3.59 us
  transfers between devices with their start and end apart: 13, of which 7 were waited for; matrix products, arithmetic and copies ran while one was open for 1% of the time, Pallas kernels for 9%

profile of v6, /device:TPU:1, one launch (start us, length us, event | category | flops | bytes accessed | tf_op | source)
XLA Modules:
  0.0 70.1 jit_solution(11009201084167539405)
XLA Ops:
  0.6 2.2 %collective-permute-start = (bf16[1,2,16,16,128]{4,3,2,1,0:T(8,128)(2,1)}, bf16[1,2,16,16,128]{4,3,2,1,0:T(8,128)(2,1)S(1)}, u32[]{:S(2)}, u32[]{:S(2)}) collective-permute-start(bf16[1,2,16,16,128]{4,3,2,1,0:T(8,128)(2,1)} %param.4), channel_id=1, source_target_pairs={{0,1},{1,2},{2,3},{3,4},{4,5},{5,6},{6,7},{7,8},{8,9},{9,10},{10,1... | collective-permute-start | bytes 393224 | tf_op jit(solution)/shard_map/ppermute | solution.py:459
  2.8 5.0 %collective-permute-start.1 = (bf16[1,2,16,16,128]{4,3,2,1,0:T(8,128)(2,1)}, bf16[1,2,16,16,128]{4,3,2,1,0:T(8,128)(2,1)S(1)}, u32[]{:S(2)}, u32[]{:S(2)}) collective-permute-start(bf16[1,2,16,16,128]{4,3,2,1,0:T(8,128)(2,1)} %param.4), channel_id=1, source_target_pairs={{0,15},{1,0},{2,1},{3,2},{4,3},{5,4},{6,5},{7,6},{8,7},{9,8},{10,9... | collective-permute-start | bytes 393224 | tf_op jit(solution)/shard_map/ppermute | solution.py:460
  7.8 0.9 %copy-done.2 = bf16[1,2,16,16,128]{4,3,2,1,0:T(8,128)(2,1)S(1)} copy-done((bf16[1,2,16,16,128]{4,3,2,1,0:T(8,128)(2,1)S(1)}, bf16[1,2,16,16,128]{4,3,2,1,0:T(8,128)(2,1)}, u32[]{:S(2)}) %copy-start.2) | copy-done | bytes 131096
  8.8 2.5 %shard_map.67 = (f32[512,256]{1,0:T(8,128)S(1)}, bf16[2,288,384]{2,1,0:T(8,128)(2,1)S(1)}, bf16[3456,256]{1,0:T(8,128)(2,1)S(1)}) custom-call(bf16[2,256,128]{2,1,0:T(8,128)(2,1)S(1)} %bitcast.24, bf16[3456,256]{1,0:T(8,128)(2,1)} %bitcast.27), custom_call_target="tpu_custom_call" | custom-call | flops 600000000 | bytes 4000000 | tf_op jit(solution)/shard_map/pallas_call | solution.py:29
  11.3 0.8 %shard_map.68 = (bf16[16,144,128]{2,1,0:T(8,128)(2,1)S(1)}, f32[512,256]{1,0:T(8,128)S(1)}, bf16[4,288,384]{2,1,0:T(8,128)(2,1)S(1)}) custom-call(s32[1]{0:T(128)} %bitcast.position, bf16[2,256,128]{2,1,0:T(8,128)(2,1)S(1)} %bitcast.18, bf16[2,256,128]{2,1,0:T(8,128)(2,1)S(1)} %bitcast.19, bf16[3456,256]{1,0:T(8,128)(2,1)S(1)} %get-tuple-element.34.kernel, ...), custom_call_target="tpu_custom_call" | custom-call | flops 300000000 | bytes 4000000 | tf_op jit(solution)/shard_map/pallas_call | solution.py:29
  12.1 16.3 %all_to_all.10.gathered = bf16[16,144,128]{2,1,0:T(8,128)(2,1)S(1)} all-to-all(bf16[16,144,128]{2,1,0:T(8,128)(2,1)S(1)} %get-tuple-element.40), channel_id=1, replica_groups=mesh['dp'=8,'wide'=16] {'wide'}, dimensions={0} | all-to-all | bytes 1179648 | tf_op jit(solution)/shard_map/all_to_all | solution.py:452
  28.4 3.3 %shard_map.69 = (bf16[256,512]{1,0:T(8,128)(2,1)S(1)}, bf16[16,14,16,128]{3,2,1,0:T(8,128)(2,1)S(1)}) custom-call(s32[1]{0:T(128)} %bitcast.position, s32[1]{0:T(128)} %bitcast.6.half, bf16[16,144,128]{2,1,0:T(8,128)(2,1)S(1)} %all_to_all.10.gathered, bf16[27,256,256]{2,1,0:T(8,128)(2,1)S(1)} %bitcast.22, f32[512,256]{1,0:T(8,128)S(1)} %get-tuple-element.48.slope, ...), custom_call_target="tpu_custom_call" | custom-call | flops 3000000000 | bytes 4000000 | tf_op jit(solution)/shard_map/pallas_call | solution.py:29
  31.7 2.8 %collective-permute-start.2 = (bf16[16,14,16,128]{3,2,1,0:T(8,128)(2,1)S(1)}, bf16[16,14,16,128]{3,2,1,0:T(8,128)(2,1)S(1)}, u32[]{:S(2)}, u32[]{:S(2)}) collective-permute-start(bf16[16,14,16,128]{3,2,1,0:T(8,128)(2,1)S(1)} %get-tuple-element.51), channel_id=1, source_target_pairs={{0,16},{16,0},{32,48},{48,32},{64,80},{80,64},{96,112},{112,96},{1... | collective-permute-start | bytes 2752520 | tf_op jit(solution)/shard_map/ppermute | solution.py:431
  34.5 2.3 %shard_map.71 = (bf16[16,128]{1,0:T(8,128)(2,1)S(1)}, bf16[14,16,256]{2,1,0:T(8,128)(2,1)S(1)}, bf16[14,16,256]{2,1,0:T(8,128)(2,1)S(1)}) custom-call(s32[1]{0:T(128)} %bitcast.position, s32[1]{0:T(128)} %bitcast.6.half, bf16[16,144,128]{2,1,0:T(8,128)(2,1)S(1)} %all_to_all.10.gathered, bf16[27,256,256]{2,1,0:T(8,128)(2,1)S(1)} %bitcast.23), custom_call_target="tpu_custom_call" | custom-call | flops 2000000000 | bytes 4000000 | tf_op jit(solution)/shard_map/pallas_call | solution.py:29
  36.9 1.5 %shard_map.70 = bf16[16,14,16,128]{3,2,1,0:T(8,128)(2,1)} custom-call(s32[1]{0:T(128)} %bitcast.6.half, bf16[256,512]{1,0:T(8,128)(2,1)S(1)} %get-tuple-element.50.rows, bf16[4,288,384]{2,1,0:T(8,128)(2,1)S(1)} %get-tuple-element.49.padded, bf16[16,14,16,128]{3,2,1,0:T(8,128)(2,1)S(1)} %collective-permute-done.2.got), custom_call_target="tpu_custom_call" | custom-call | flops 900000000 | bytes 4000000 | tf_op jit(solution)/shard_map/pallas_call | solution.py:29
  38.5 3.6 %all-to-all-start.1 = ((bf16[16,224,128]{2,1,0:T(8,128)(2,1)}), bf16[16,224,128]{2,1,0:T(8,128)(2,1)S(1)}, u32[]{:S(2)}, u32[]{:S(2)}) async-start(bf16[16,224,128]{2,1,0:T(8,128)(2,1)} %bitcast.10), calls=%async_computation.1 | async-start | bytes 1835008 | tf_op jit(solution)/shard_map/all_to_all | solution.py:452
  42.2 2.5 %collective-permute-start.6 = (bf16[14,16,256]{2,1,0:T(8,128)(2,1)S(1)}, bf16[14,16,256]{2,1,0:T(8,128)(2,1)S(1)}, u32[]{:S(2)}, u32[]{:S(2)}) collective-permute-start(bf16[14,16,256]{2,1,0:T(8,128)(2,1)S(1)} %add_convert_fusion.1), channel_id=1, source_target_pairs={{0,96},{16,112},{32,0},{48,16},{64,32},{80,48},{96,64},{112,80},{1... | collective-permute-start | bytes 344072 | tf_op jit(solution)/shard_map/ppermute | solution.py:439
  45.2 0.6 collective-permute-start.4
  45.8 1.1 %collective-permute-done.6 = bf16[14,16,256]{2,1,0:T(8,128)(2,1)S(1)} collective-permute-done((bf16[14,16,256]{2,1,0:T(8,128)(2,1)S(1)}, bf16[14,16,256]{2,1,0:T(8,128)(2,1)S(1)}, u32[]{:S(2)}, u32[]{:S(2)}) %collective-permute-start.6) | collective-permute-done | bytes 114720 | tf_op jit(solution)/shard_map/ppermute | solution.py:439
  47.0 3.2 %collective-permute-done.5 = bf16[14,16,256]{2,1,0:T(8,128)(2,1)S(1)} collective-permute-done((bf16[14,16,256]{2,1,0:T(8,128)(2,1)S(1)}, bf16[14,16,256]{2,1,0:T(8,128)(2,1)S(1)}, u32[]{:S(2)}, u32[]{:S(2)}) %collective-permute-start.5) | collective-permute-done | bytes 114720 | tf_op jit(solution)/shard_map/ppermute | solution.py:439
  50.2 3.5 %collective-permute-done.4 = bf16[14,16,256]{2,1,0:T(8,128)(2,1)S(1)} collective-permute-done((bf16[14,16,256]{2,1,0:T(8,128)(2,1)S(1)}, bf16[14,16,256]{2,1,0:T(8,128)(2,1)S(1)}, u32[]{:S(2)}, u32[]{:S(2)}) %collective-permute-start.4) | collective-permute-done | bytes 114720 | tf_op jit(solution)/shard_map/ppermute | solution.py:439
  53.6 3.6 %all-to-all-done.1 = bf16[16,224,128]{2,1,0:T(8,128)(2,1)S(1)} async-done(((bf16[16,224,128]{2,1,0:T(8,128)(2,1)}), bf16[16,224,128]{2,1,0:T(8,128)(2,1)S(1)}, u32[]{:S(2)}, u32[]{:S(2)}) %all-to-all-start.1) | async-done | bytes 917536 | tf_op jit(solution)/shard_map/all_to_all | solution.py:452
  57.3 2.5 %collective-permute-start.9 = (bf16[14,16,128]{2,1,0:T(8,128)(2,1)S(1)}, bf16[14,16,128]{2,1,0:T(8,128)(2,1)S(1)}, u32[]{:S(2)}, u32[]{:S(2)}) collective-permute-start(bf16[14,16,128]{2,1,0:T(8,128)(2,1)S(1)} %reduce_sum.12), channel_id=1, source_target_pairs={{0,96},{16,112},{32,0},{48,16},{64,32},{80,48},{96,64},{112,80},{1... | collective-permute-start | bytes 172040 | tf_op jit(solution)/shard_map/ppermute | solution.py:439
  60.4 0.6 collective-permute-start.7
  61.1 2.6 %collective-permute-start.11 = (bf16[14,16,256]{2,1,0:T(8,128)(2,1)S(1)}, bf16[14,16,256]{2,1,0:T(8,128)(2,1)S(1)}, u32[]{:S(2)}, u32[]{:S(2)}) collective-permute-start(bf16[14,16,256]{2,1,0:T(8,128)(2,1)S(1)} %add_convert_fusion.mine_six), channel_id=1, source_target_pairs={{0,16},{16,0},{32,48},{48,32},{64,80},{80,64},{96,112},{112,96},{1... | collective-permute-start | bytes 344072 | tf_op jit(solution)/shard_map/ppermute | solution.py:431
  63.7 0.7 %collective-permute-done.8 = bf16[14,16,128]{2,1,0:T(8,128)(2,1)S(1)} collective-permute-done((bf16[14,16,128]{2,1,0:T(8,128)(2,1)S(1)}, bf16[14,16,128]{2,1,0:T(8,128)(2,1)S(1)}, u32[]{:S(2)}, u32[]{:S(2)}) %collective-permute-start.8) | collective-permute-done | bytes 57376 | tf_op jit(solution)/shard_map/ppermute | solution.py:439
  65.1 3.2 %collective-permute-start.10 = (bf16[14,16,128]{2,1,0:T(8,128)(2,1)S(1)}, bf16[14,16,128]{2,1,0:T(8,128)(2,1)S(1)}, u32[]{:S(2)}, u32[]{:S(2)}) collective-permute-start(bf16[14,16,128]{2,1,0:T(8,128)(2,1)S(1)} %add_convert_fusion.2.mine_five), channel_id=1, source_target_pairs={{0,16},{16,0},{32,48},{48,32},{64,80},{80,64},{96,112},{112,96},{1... | collective-permute-start | bytes 172040 | tf_op jit(solution)/shard_map/ppermute | solution.py:431
  68.3 0.7 %copy.8 = bf16[128,16]{1,0:T(8,128)(2,1)} copy(bf16[128,16]{0,1:T(8,128)(2,1)S(1)} %bitcast.21) | data formatting | bytes 8192 | tf_op jit(solution)/shard_map/transpose | solution.py:490
  69.2 0.9 %shard_map.72 = (f32[27,16,128]{2,1,0:T(8,128)}, f32[27,16,256]{2,1,0:T(8,128)}) custom-call(s32[1]{0:T(128)} %bitcast.6.half, bf16[14,16,128]{2,1,0:T(8,128)(2,1)S(1)} %add_convert_fusion.2.mine_five, bf16[14,16,128]{2,1,0:T(8,128)(2,1)S(1)} %collective-permute-done.10.other_five, bf16[14,16,256]{2,1,0:T(8,128)(2,1)S(1)} %add_convert_fusion.mine_six, ...), custom_call_target="tpu_custom_call" | custom-call | bytes 4000000 | tf_op jit(solution)/shard_map/pallas_call | solution.py:29
  (20 shorter events, 2.2 us)
Async XLA Ops:
  0.6 10.6 %copy-start = (bf16[1,8,4,4,16]{4,3,2,1,0:T(4,128)(2,1)S(1)}, bf16[1,8,4,4,16]{4,3,2,1,0:T(4,128)(2,1)}, u32[]{:S(2)}) copy-start(bf16[1,8,4,4,16]{4,3,2,1,0:T(4,128)(2,1)} %param.7) | copy-start | bytes 12292
  0.6 10.6 %collective-permute-start = (bf16[1,2,16,16,128]{4,3,2,1,0:T(8,128)(2,1)}, bf16[1,2,16,16,128]{4,3,2,1,0:T(8,128)(2,1)S(1)}, u32[]{:S(2)}, u32[]{:S(2)}) collective-permute-start(bf16[1,2,16,16,128]{4,3,2,1,0:T(8,128)(2,1)} %param.4), channel_id=1, source_target_pairs={{0,1},{1,2},{2,3},{3,4},{4,5},{5,6},{6,7},{7,8},{8,9},{9,10},{10,1... | collective-permute-start | bytes 393224 | tf_op jit(solution)/shard_map/ppermute | solution.py:459
  2.8 8.4 %collective-permute-start.1 = (bf16[1,2,16,16,128]{4,3,2,1,0:T(8,128)(2,1)}, bf16[1,2,16,16,128]{4,3,2,1,0:T(8,128)(2,1)S(1)}, u32[]{:S(2)}, u32[]{:S(2)}) collective-permute-start(bf16[1,2,16,16,128]{4,3,2,1,0:T(8,128)(2,1)} %param.4), channel_id=1, source_target_pairs={{0,15},{1,0},{2,1},{3,2},{4,3},{5,4},{6,5},{7,6},{8,7},{9,8},{10,9... | collective-permute-start | bytes 393224 | tf_op jit(solution)/shard_map/ppermute | solution.py:460
  7.8 0.9 %copy-start.2 = (bf16[1,2,16,16,128]{4,3,2,1,0:T(8,128)(2,1)S(1)}, bf16[1,2,16,16,128]{4,3,2,1,0:T(8,128)(2,1)}, u32[]{:S(2)}) copy-start(bf16[1,2,16,16,128]{4,3,2,1,0:T(8,128)(2,1)} %param.4) | copy-start | bytes 393220
  11.3 17.2 %copy-start.1 = (bf16[3,3,3,256,256]{4,3,2,1,0:T(8,128)(2,1)S(1)}, bf16[3,3,3,256,256]{4,3,2,1,0:T(8,128)(2,1)}, u32[]{:S(2)}) copy-start(bf16[3,3,3,256,256]{4,3,2,1,0:T(8,128)(2,1)} %param.6) | copy-start | bytes 10616836
  31.7 5.2 %collective-permute-start.2 = (bf16[16,14,16,128]{3,2,1,0:T(8,128)(2,1)S(1)}, bf16[16,14,16,128]{3,2,1,0:T(8,128)(2,1)S(1)}, u32[]{:S(2)}, u32[]{:S(2)}) collective-permute-start(bf16[16,14,16,128]{3,2,1,0:T(8,128)(2,1)S(1)} %get-tuple-element.51), channel_id=1, source_target_pairs={{0,16},{16,0},{32,48},{48,32},{64,80},{80,64},{96,112},{112,96},{1... | collective-permute-start | bytes 2752520 | tf_op jit(solution)/shard_map/ppermute | solution.py:431
  36.8 1.6 %collective-permute-start.3 = (bf16[14,16,256]{2,1,0:T(8,128)(2,1)S(1)}, bf16[14,16,256]{2,1,0:T(8,128)(2,1)S(1)}, u32[]{:S(2)}, u32[]{:S(2)}) collective-permute-start(bf16[14,16,256]{2,1,0:T(8,128)(2,1)S(1)} %get-tuple-element.52), channel_id=1, source_target_pairs={{0,16},{16,0},{32,48},{48,32},{64,80},{80,64},{96,112},{112,96},{1... | collective-permute-start | bytes 344072 | tf_op jit(solution)/shard_map/ppermute | solution.py:431
  38.5 18.7 %all-to-all-start.1 = ((bf16[16,224,128]{2,1,0:T(8,128)(2,1)}), bf16[16,224,128]{2,1,0:T(8,128)(2,1)S(1)}, u32[]{:S(2)}, u32[]{:S(2)}) async-start(bf16[16,224,128]{2,1,0:T(8,128)(2,1)} %bitcast.10), calls=%async_computation.1 | async-start | bytes 1835008 | tf_op jit(solution)/shard_map/all_to_all | solution.py:452
  42.2 4.8 %collective-permute-start.6 = (bf16[14,16,256]{2,1,0:T(8,128)(2,1)S(1)}, bf16[14,16,256]{2,1,0:T(8,128)(2,1)S(1)}, u32[]{:S(2)}, u32[]{:S(2)}) collective-permute-start(bf16[14,16,256]{2,1,0:T(8,128)(2,1)S(1)} %add_convert_fusion.1), channel_id=1, source_target_pairs={{0,96},{16,112},{32,0},{48,16},{64,32},{80,48},{96,64},{112,80},{1... | collective-permute-start | bytes 344072 | tf_op jit(solution)/shard_map/ppermute | solution.py:439
  44.7 5.4 %collective-permute-start.5 = (bf16[14,16,256]{2,1,0:T(8,128)(2,1)S(1)}, bf16[14,16,256]{2,1,0:T(8,128)(2,1)S(1)}, u32[]{:S(2)}, u32[]{:S(2)}) collective-permute-start(bf16[14,16,256]{2,1,0:T(8,128)(2,1)S(1)} %add_convert_fusion.1), channel_id=1, source_target_pairs={{0,64},{16,80},{32,96},{48,112},{64,0},{80,16},{96,32},{112,48},{1... | collective-permute-start | bytes 344072 | tf_op jit(solution)/shard_map/ppermute | solution.py:439
  45.2 8.4 %collective-permute-start.4 = (bf16[14,16,256]{2,1,0:T(8,128)(2,1)S(1)}, bf16[14,16,256]{2,1,0:T(8,128)(2,1)S(1)}, u32[]{:S(2)}, u32[]{:S(2)}) collective-permute-start(bf16[14,16,256]{2,1,0:T(8,128)(2,1)S(1)} %add_convert_fusion.1), channel_id=1, source_target_pairs={{0,32},{16,48},{32,64},{48,80},{64,96},{80,112},{96,0},{112,16},{1... | collective-permute-start | bytes 344072 | tf_op jit(solution)/shard_map/ppermute | solution.py:439
  57.3 6.4 %collective-permute-start.9 = (bf16[14,16,128]{2,1,0:T(8,128)(2,1)S(1)}, bf16[14,16,128]{2,1,0:T(8,128)(2,1)S(1)}, u32[]{:S(2)}, u32[]{:S(2)}) collective-permute-start(bf16[14,16,128]{2,1,0:T(8,128)(2,1)S(1)} %reduce_sum.12), channel_id=1, source_target_pairs={{0,96},{16,112},{32,0},{48,16},{64,32},{80,48},{96,64},{112,80},{1... | collective-permute-start | bytes 172040 | tf_op jit(solution)/shard_map/ppermute | solution.py:439
  59.9 4.6 %collective-permute-start.8 = (bf16[14,16,128]{2,1,0:T(8,128)(2,1)S(1)}, bf16[14,16,128]{2,1,0:T(8,128)(2,1)S(1)}, u32[]{:S(2)}, u32[]{:S(2)}) collective-permute-start(bf16[14,16,128]{2,1,0:T(8,128)(2,1)S(1)} %reduce_sum.12), channel_id=1, source_target_pairs={{0,64},{16,80},{32,96},{48,112},{64,0},{80,16},{96,32},{112,48},{1... | collective-permute-start | bytes 172040 | tf_op jit(solution)/shard_map/ppermute | solution.py:439
  60.4 4.6 %collective-permute-start.7 = (bf16[14,16,128]{2,1,0:T(8,128)(2,1)S(1)}, bf16[14,16,128]{2,1,0:T(8,128)(2,1)S(1)}, u32[]{:S(2)}, u32[]{:S(2)}) collective-permute-start(bf16[14,16,128]{2,1,0:T(8,128)(2,1)S(1)} %reduce_sum.12), channel_id=1, source_target_pairs={{0,32},{16,48},{32,64},{48,80},{64,96},{80,112},{96,0},{112,16},{1... | collective-permute-start | bytes 172040 | tf_op jit(solution)/shard_map/ppermute | solution.py:439
  61.1 8.1 %collective-permute-start.11 = (bf16[14,16,256]{2,1,0:T(8,128)(2,1)S(1)}, bf16[14,16,256]{2,1,0:T(8,128)(2,1)S(1)}, u32[]{:S(2)}, u32[]{:S(2)}) collective-permute-start(bf16[14,16,256]{2,1,0:T(8,128)(2,1)S(1)} %add_convert_fusion.mine_six), channel_id=1, source_target_pairs={{0,16},{16,0},{32,48},{48,32},{64,80},{80,64},{96,112},{112,96},{1... | collective-permute-start | bytes 344072 | tf_op jit(solution)/shard_map/ppermute | solution.py:431
  65.1 4.1 %collective-permute-start.10 = (bf16[14,16,128]{2,1,0:T(8,128)(2,1)S(1)}, bf16[14,16,128]{2,1,0:T(8,128)(2,1)S(1)}, u32[]{:S(2)}, u32[]{:S(2)}) collective-permute-start(bf16[14,16,128]{2,1,0:T(8,128)(2,1)S(1)} %add_convert_fusion.2.mine_five), channel_id=1, source_target_pairs={{0,16},{16,0},{32,48},{48,32},{64,80},{80,64},{96,112},{112,96},{1... | collective-permute-start | bytes 172040 | tf_op jit(solution)/shard_map/ppermute | solution.py:431

commit v7 on v6

--- a/solution.py
+++ b/solution.py
@@ -109,9 +109,13 @@
     )
 
 
-def outer_kernel(position, low, high, kernel, part, inner, cot, message, slope, padded, tall):
-    columns_of(padded, 0, jnp.where(position[0] == 0, jnp.zeros((256, 128), jnp.bfloat16), low[1]))
-    columns_of(padded, 3, jnp.where(position[0] == 15, jnp.zeros((256, 128), jnp.bfloat16), high[0]))
+def outer_kernel(position, odds, evens, kernel, part, inner, cot, message, slope, padded, tall):
+    even = position[0] % 2 == 0
+    blank = jnp.zeros((256, 128), jnp.bfloat16)
+    low = jnp.where(even, odds[1], evens[1])
+    high = jnp.where(even, evens[0], odds[0])
+    columns_of(padded, 0, jnp.where(position[0] == 0, blank, low))
+    columns_of(padded, 3, jnp.where(position[0] == 15, blank, high))
     padded[1:3] = inner[...]
     acts = []
     for plane in range(2):
@@ -145,7 +149,7 @@
         message[target, 128:144, :] = marks
 
 
-def outer_five(low, high, kernel, part, inner, cot_rows, position):
+def outer_five(odds, evens, kernel, part, inner, cot_rows, position):
     return call(
         outer_kernel,
         (
@@ -155,8 +159,8 @@
         ),
         [VMEM((2, 128, 128), jnp.float32)],
         (
-            low.reshape(2, 256, 128),
-            high.reshape(2, 256, 128),
+            odds.reshape(2, 256, 128),
+            evens.reshape(2, 256, 128),
             kernel,
             part,
             inner,
@@ -400,30 +404,34 @@
     )
 
 
-def halves_kernel(half, mine_five, other_five, mine_six, other_six, five, six):
+def halves_kernel(half, mine, other, out):
     for step in range(HALF_TAPS):
-        for first, part_five, part_six in (
-            (half[0] * HALF_TAPS, mine_five, mine_six),
-            ((1 - half[0]) * HALF_TAPS, other_five, other_six),
-        ):
+        for first, part in ((half[0] * HALF_TAPS, mine), ((1 - half[0]) * HALF_TAPS, other)):
             tap = jnp.minimum(first + step, 26)
-            five[tap] = part_five[step].astype(jnp.float32)
-            six[tap] = part_six[step].astype(jnp.float32)
-
-
-def both_halves(half, mine_five, other_five, mine_six, other_six):
+            out[tap] = part[step].astype(jnp.float32)
+
+
+def both_halves(half, mine, other):
     return call(
         halves_kernel,
-        (shape((27, 16, 128), jnp.float32), shape((27, 16, 256), jnp.float32)),
+        shape((27,) + mine.shape[1:], jnp.float32),
         [],
-        (mine_five, other_five, mine_six, other_six),
+        (mine, other),
         (half,),
     )
 
 
-def ring_perm(axis, step):
-    count = lax.axis_size(axis)
-    return [(i, (i + step) % count) for i in range(count)]
+def pair_perm(first):
+    volumes, count = lax.axis_size("dp"), lax.axis_size("wide")
+    pairs = []
+    for volume in range(volumes):
+        for place in range(count):
+            other = place + 1 if place % 2 == first else place - 1
+            if 0 <= other < count:
+                pairs.append((volume * count + place, volume * count + other))
+            else:
+                pairs.append((volume * count + place, (volume ^ 1) * count + place))
+    return pairs
 
 
 def core_swap(values):
@@ -456,11 +464,11 @@
 def shards(volume, kernel_five, kernel_six, cotangent):
     position = lax.axis_index("wide").astype(jnp.int32).reshape(1)
     half = (lax.axis_index("dp") % 2).astype(jnp.int32).reshape(1)
-    low = lax.ppermute(volume, "wide", ring_perm("wide", 1))
-    high = lax.ppermute(volume, "wide", ring_perm("wide", -1))
+    odds = lax.ppermute(volume, ("dp", "wide"), pair_perm(1))
+    evens = lax.ppermute(volume, ("dp", "wide"), pair_perm(0))
     cot_rows = cotangent.reshape(32, 4, 16)
     part, inner, near_kernel = inner_five(volume, kernel_five)
-    message, slope, padded = outer_five(low, high, near_kernel, part, inner, cot_rows, position)
+    message, slope, padded = outer_five(odds, evens, near_kernel, part, inner, cot_rows, position)
     message, position, half, slope, padded = lax.optimization_barrier(
         (message, position, half, slope, padded)
     )
@@ -479,15 +487,16 @@
     pair_six = total_of(mine_six, [got_six]).astype(jnp.bfloat16)
     chips_six = from_chips(pair_six)
     spread = exchange(pair_five)
-    spread, chips_six = lax.optimization_barrier((spread, chips_six))
+    total_six = total_of(pair_six, chips_six).astype(jnp.bfloat16)
+    out_six = both_halves(half, total_six, core_swap(total_six))
+    next_input = next_rows.T.reshape(1, 8, 4, 4, 16)
+    spread, out_six, next_input = lax.optimization_barrier((spread, out_six, next_input))
     depth_five = spread.astype(jnp.float32).sum(0).astype(jnp.bfloat16)
-    total_six = total_of(pair_six, chips_six).astype(jnp.bfloat16)
     total_five = total_of(depth_five, from_chips(depth_five)).astype(jnp.bfloat16)
-    other_five, other_six = core_swap(total_five), core_swap(total_six)
-    out_five, out_six = both_halves(half, total_five, other_five, total_six, other_six)
+    out_five = both_halves(half, total_five, core_swap(total_five))
     out_five = out_five.transpose(0, 2, 1).reshape(3, 3, 3, 128, 16)
     out_six = out_six.transpose(0, 2, 1).reshape(3, 3, 3, 256, 16)
-    return (next_rows.T.reshape(1, 8, 4, 4, 16), out_five, out_six)
+    return (next_input, out_five, out_six)
 
 
 def solution(mesh):

time: 70.3 us -> 68.7 us (0.977)
  starting transfers between devices: 26.9 us -> 21.3 us
  blocking collectives: 16.3 us -> 18.6 us
  waiting for transfers between devices: 12.9 us -> 14 us
    ppermute x2, starting transfers between devices: 7.19 us -> 3.5 us  [the longest x1 2 us: shards(): evens = lax.ppermute(volume, ('dp', 'wide'), pair_perm(0))]
    ppermute x6, waiting for transfers between devices: 9.09 us -> 11.8 us  [from_chips(): got.append(lax.ppermute(values, 'dp', pairs))]
    all_to_all x1, waiting for transfers between devices: 3.59 us -> 1.04 us  [exchange(): got = lax.all_to_all(flat, 'wide', split_axis=0, concat_axis=0, tiled=True)]
    all_to_all x1, blocking collectives: 16.3 us -> 18.6 us  [exchange(): got = lax.all_to_all(flat, 'wide', split_axis=0, concat_axis=0, tiled=True)]
    ppermute x4, starting transfers between devices: 8.73 us -> 6.81 us  [core_swap(): return lax.ppermute(values, 'dp', [(i, i ^ 1) for i in range(count)])]
    ppermute x4, waiting for transfers between devices: 0.18 us -> 1.14 us  [core_swap(): return lax.ppermute(values, 'dp', [(i, i ^ 1) for i in range(count)])]
    pallas_call x6 -> x7, Pallas kernels: 11.3 us -> 11.9 us  [call(): pl.pallas_call(body, out_shape=out_shape, in_specs=specs, out_specs=outs,...]
  transfers between devices with their start and end apart: 13 -> 13, of which waited for: 7 -> 9; matrix products, arithmetic and copies ran while one was open for 1% -> 1% of each run, Pallas kernels for 9% -> 10%
where the time goes in v7:
time: 68.7 us; the launch traced here: 68.5 us
  starting transfers between devices  21.3 us (31%)
  blocking collectives  18.6 us (27%)
  waiting for transfers between devices  14 us (20%)
  Pallas kernels  11.9 us (17%)
  local copies, waits for them, and re-layouts  1.67 us (2%)
  between operations  0.76 us (1%)
    all_to_all x1, blocking collectives, exchange(): got = lax.all_to_all(flat, 'wide', split_axis=0, concat_axis=0, tiled=True)  18.6 us
    pallas_call x7, Pallas kernels, call(): pl.pallas_call(body, out_shape=out_shape, in_specs=specs, out_specs=outs,...  11.9 us
    ppermute x6, waiting for transfers between devices, from_chips(): got.append(lax.ppermute(values, 'dp', pairs))  11.8 us
    ppermute x6, starting transfers between devices, from_chips(): got.append(lax.ppermute(values, 'dp', pairs))  7.35 us
    ppermute x4, starting transfers between devices, core_swap(): return lax.ppermute(values, 'dp', [(i, i ^ 1) for i in range(count)])  6.81 us
    all_to_all x1, starting transfers between devices, exchange(): got = lax.all_to_all(flat, 'wide', split_axis=0, concat_axis=0, tiled=True)  3.65 us
    ppermute x1, starting transfers between devices, shards(): evens = lax.ppermute(volume, ('dp', 'wide'), pair_perm(0))  2 us
    ppermute x1, starting transfers between devices, shards(): odds = lax.ppermute(volume, ('dp', 'wide'), pair_perm(1))  1.5 us
  transfers between devices with their start and end apart: 13, of which 9 were waited for; matrix products, arithmetic and copies ran while one was open for 1% of the time, Pallas kernels for 10%

profile of v7, /device:TPU:1, one launch (start us, length us, event | category | flops | bytes accessed | tf_op | source)
XLA Modules:
  0.0 68.5 jit_solution(9813129594897135292)
XLA Ops:
  0.6 1.5 %collective-permute-start = (bf16[1,2,16,16,128]{4,3,2,1,0:T(8,128)(2,1)}, bf16[1,2,16,16,128]{4,3,2,1,0:T(8,128)(2,1)S(1)}, u32[]{:S(2)}, u32[]{:S(2)}) collective-permute-start(bf16[1,2,16,16,128]{4,3,2,1,0:T(8,128)(2,1)} %param.4), channel_id=1, source_target_pairs={{0,16},{1,2},{2,1},{3,4},{4,3},{5,6},{6,5},{7,8},{8,7},{9,10},{10,... | collective-permute-start | bytes 393224 | tf_op jit(solution)/shard_map/ppermute | solution.py:467
  2.1 2.0 %collective-permute-start.1 = (bf16[1,2,16,16,128]{4,3,2,1,0:T(8,128)(2,1)}, bf16[1,2,16,16,128]{4,3,2,1,0:T(8,128)(2,1)S(1)}, u32[]{:S(2)}, u32[]{:S(2)}) collective-permute-start(bf16[1,2,16,16,128]{4,3,2,1,0:T(8,128)(2,1)} %param.4), channel_id=1, source_target_pairs={{0,1},{1,0},{2,3},{3,2},{4,5},{5,4},{6,7},{7,6},{8,9},{9,8},{10,11... | collective-permute-start | bytes 393224 | tf_op jit(solution)/shard_map/ppermute | solution.py:468
  4.1 0.9 %copy-done.2 = bf16[1,2,16,16,128]{4,3,2,1,0:T(8,128)(2,1)S(1)} copy-done((bf16[1,2,16,16,128]{4,3,2,1,0:T(8,128)(2,1)S(1)}, bf16[1,2,16,16,128]{4,3,2,1,0:T(8,128)(2,1)}, u32[]{:S(2)}) %copy-start.2) | copy-done | bytes 131096
  5.1 2.5 %shard_map.67 = (f32[512,256]{1,0:T(8,128)S(1)}, bf16[2,288,384]{2,1,0:T(8,128)(2,1)S(1)}, bf16[3456,256]{1,0:T(8,128)(2,1)S(1)}) custom-call(bf16[2,256,128]{2,1,0:T(8,128)(2,1)S(1)} %bitcast.24, bf16[3456,256]{1,0:T(8,128)(2,1)} %bitcast.29), custom_call_target="tpu_custom_call" | custom-call | flops 600000000 | bytes 4000000 | tf_op jit(solution)/shard_map/pallas_call | solution.py:29
  7.6 0.8 %shard_map.68 = (bf16[16,144,128]{2,1,0:T(8,128)(2,1)S(1)}, f32[512,256]{1,0:T(8,128)S(1)}, bf16[4,288,384]{2,1,0:T(8,128)(2,1)S(1)}) custom-call(s32[1]{0:T(128)} %bitcast.position, bf16[2,256,128]{2,1,0:T(8,128)(2,1)S(1)} %bitcast.18, bf16[2,256,128]{2,1,0:T(8,128)(2,1)S(1)} %bitcast.19, bf16[3456,256]{1,0:T(8,128)(2,1)S(1)} %get-tuple-element.31.kernel, ...), custom_call_target="tpu_custom_call" | custom-call | flops 300000000 | bytes 4000000 | tf_op jit(solution)/shard_map/pallas_call | solution.py:29
  8.4 18.6 %all_to_all.10.gathered = bf16[16,144,128]{2,1,0:T(8,128)(2,1)S(1)} all-to-all(bf16[16,144,128]{2,1,0:T(8,128)(2,1)S(1)} %get-tuple-element.37), channel_id=1, replica_groups=mesh['dp'=8,'wide'=16] {'wide'}, dimensions={0} | all-to-all | bytes 1179648 | tf_op jit(solution)/shard_map/all_to_all | solution.py:460
  27.0 3.3 %shard_map.69 = (bf16[256,512]{1,0:T(8,128)(2,1)S(1)}, bf16[16,14,16,128]{3,2,1,0:T(8,128)(2,1)S(1)}) custom-call(s32[1]{0:T(128)} %bitcast.position, s32[1]{0:T(128)} %bitcast.6.half, bf16[16,144,128]{2,1,0:T(8,128)(2,1)S(1)} %all_to_all.10.gathered, bf16[27,256,256]{2,1,0:T(8,128)(2,1)S(1)} %bitcast.22, f32[512,256]{1,0:T(8,128)S(1)} %get-tuple-element.45.slope, ...), custom_call_target="tpu_custom_call" | custom-call | flops 3000000000 | bytes 4000000 | tf_op jit(solution)/shard_map/pallas_call | solution.py:29
  30.3 2.8 %collective-permute-start.2 = (bf16[16,14,16,128]{3,2,1,0:T(8,128)(2,1)S(1)}, bf16[16,14,16,128]{3,2,1,0:T(8,128)(2,1)S(1)}, u32[]{:S(2)}, u32[]{:S(2)}) collective-permute-start(bf16[16,14,16,128]{3,2,1,0:T(8,128)(2,1)S(1)} %get-tuple-element.48), channel_id=1, source_target_pairs={{0,16},{16,0},{32,48},{48,32},{64,80},{80,64},{96,112},{112,96},{1... | collective-permute-start | bytes 2752520 | tf_op jit(solution)/shard_map/ppermute | solution.py:439
  33.1 2.3 %shard_map.71 = (bf16[16,128]{1,0:T(8,128)(2,1)S(1)}, bf16[14,16,256]{2,1,0:T(8,128)(2,1)S(1)}, bf16[14,16,256]{2,1,0:T(8,128)(2,1)S(1)}) custom-call(s32[1]{0:T(128)} %bitcast.position, s32[1]{0:T(128)} %bitcast.6.half, bf16[16,144,128]{2,1,0:T(8,128)(2,1)S(1)} %all_to_all.10.gathered, bf16[27,256,256]{2,1,0:T(8,128)(2,1)S(1)} %bitcast.23), custom_call_target="tpu_custom_call" | custom-call | flops 2000000000 | bytes 4000000 | tf_op jit(solution)/shard_map/pallas_call | solution.py:29
  35.5 1.5 %shard_map.70 = bf16[16,14,16,128]{3,2,1,0:T(8,128)(2,1)} custom-call(s32[1]{0:T(128)} %bitcast.6.half, bf16[256,512]{1,0:T(8,128)(2,1)S(1)} %get-tuple-element.47.rows, bf16[4,288,384]{2,1,0:T(8,128)(2,1)S(1)} %get-tuple-element.46.padded, bf16[16,14,16,128]{3,2,1,0:T(8,128)(2,1)S(1)} %collective-permute-done.2.got), custom_call_target="tpu_custom_call" | custom-call | flops 900000000 | bytes 4000000 | tf_op jit(solution)/shard_map/pallas_call | solution.py:29
  37.0 3.6 %all-to-all-start.1 = ((bf16[16,224,128]{2,1,0:T(8,128)(2,1)}), bf16[16,224,128]{2,1,0:T(8,128)(2,1)S(1)}, u32[]{:S(2)}, u32[]{:S(2)}) async-start(bf16[16,224,128]{2,1,0:T(8,128)(2,1)} %bitcast.8), calls=%async_computation.1 | async-start | bytes 1835008 | tf_op jit(solution)/shard_map/all_to_all | solution.py:460
  40.7 2.5 %collective-permute-start.6 = (bf16[14,16,256]{2,1,0:T(8,128)(2,1)S(1)}, bf16[14,16,256]{2,1,0:T(8,128)(2,1)S(1)}, u32[]{:S(2)}, u32[]{:S(2)}) collective-permute-start(bf16[14,16,256]{2,1,0:T(8,128)(2,1)S(1)} %add_convert_fusion.1), channel_id=1, source_target_pairs={{0,96},{16,112},{32,0},{48,16},{64,32},{80,48},{96,64},{112,80},{1... | collective-permute-start | bytes 344072 | tf_op jit(solution)/shard_map/ppermute | solution.py:447
  44.4 1.1 %collective-permute-done.6 = bf16[14,16,256]{2,1,0:T(8,128)(2,1)S(1)} collective-permute-done((bf16[14,16,256]{2,1,0:T(8,128)(2,1)S(1)}, bf16[14,16,256]{2,1,0:T(8,128)(2,1)S(1)}, u32[]{:S(2)}, u32[]{:S(2)}) %collective-permute-start.6) | collective-permute-done | bytes 114720 | tf_op jit(solution)/shard_map/ppermute | solution.py:447
  45.5 3.2 %collective-permute-done.5 = bf16[14,16,256]{2,1,0:T(8,128)(2,1)S(1)} collective-permute-done((bf16[14,16,256]{2,1,0:T(8,128)(2,1)S(1)}, bf16[14,16,256]{2,1,0:T(8,128)(2,1)S(1)}, u32[]{:S(2)}, u32[]{:S(2)}) %collective-permute-start.5) | collective-permute-done | bytes 114720 | tf_op jit(solution)/shard_map/ppermute | solution.py:447
  48.7 3.4 %collective-permute-done.4 = bf16[14,16,256]{2,1,0:T(8,128)(2,1)S(1)} collective-permute-done((bf16[14,16,256]{2,1,0:T(8,128)(2,1)S(1)}, bf16[14,16,256]{2,1,0:T(8,128)(2,1)S(1)}, u32[]{:S(2)}, u32[]{:S(2)}) %collective-permute-start.4) | collective-permute-done | bytes 114720 | tf_op jit(solution)/shard_map/ppermute | solution.py:447
  52.2 0.7 %collective-permute-start.7 = (bf16[14,16,256]{2,1,0:T(8,128)(2,1)S(1)}, bf16[14,16,256]{2,1,0:T(8,128)(2,1)S(1)}, u32[]{:S(2)}, u32[]{:S(2)}) collective-permute-start(bf16[14,16,256]{2,1,0:T(8,128)(2,1)S(1)} %add_convert_fusion.mine), channel_id=1, source_target_pairs={{0,16},{16,0},{32,48},{48,32},{64,80},{80,64},{96,112},{112,96},{1... | collective-permute-start | bytes 344072 | tf_op jit(solution)/shard_map/ppermute | solution.py:439
  52.9 0.7 %copy.8 = bf16[128,16]{1,0:T(8,128)(2,1)} copy(bf16[128,16]{0,1:T(8,128)(2,1)S(1)} %bitcast.21) | data formatting | bytes 8192 | tf_op jit(solution)/shard_map/transpose | solution.py:492
  53.9 0.8 %shard_map.72 = f32[27,16,256]{2,1,0:T(8,128)} custom-call(s32[1]{0:T(128)} %bitcast.6.half, bf16[14,16,256]{2,1,0:T(8,128)(2,1)S(1)} %add_convert_fusion.mine, bf16[14,16,256]{2,1,0:T(8,128)(2,1)S(1)} %collective-permute-done.7.other), custom_call_target="tpu_custom_call" | custom-call | bytes 4000000 | tf_op jit(solution)/shard_map/pallas_call | solution.py:29
  54.7 1.0 %all-to-all-done.1 = bf16[16,224,128]{2,1,0:T(8,128)(2,1)S(1)} async-done(((bf16[16,224,128]{2,1,0:T(8,128)(2,1)}), bf16[16,224,128]{2,1,0:T(8,128)(2,1)S(1)}, u32[]{:S(2)}, u32[]{:S(2)}) %all-to-all-start.1) | async-done | bytes 917536 | tf_op jit(solution)/shard_map/all_to_all | solution.py:460
  55.9 2.6 %collective-permute-start.10 = (bf16[14,16,128]{2,1,0:T(8,128)(2,1)S(1)}, bf16[14,16,128]{2,1,0:T(8,128)(2,1)S(1)}, u32[]{:S(2)}, u32[]{:S(2)}) collective-permute-start(bf16[14,16,128]{2,1,0:T(8,128)(2,1)S(1)} %reduce_sum.12), channel_id=1, source_target_pairs={{0,96},{16,112},{32,0},{48,16},{64,32},{80,48},{96,64},{112,80},{1... | collective-permute-start | bytes 172040 | tf_op jit(solution)/shard_map/ppermute | solution.py:447
  59.7 3.3 %collective-permute-done.9 = bf16[14,16,128]{2,1,0:T(8,128)(2,1)S(1)} collective-permute-done((bf16[14,16,128]{2,1,0:T(8,128)(2,1)S(1)}, bf16[14,16,128]{2,1,0:T(8,128)(2,1)S(1)}, u32[]{:S(2)}, u32[]{:S(2)}) %collective-permute-start.9) | collective-permute-done | bytes 57376 | tf_op jit(solution)/shard_map/ppermute | solution.py:447
  63.6 3.2 %collective-permute-start.11 = (bf16[14,16,128]{2,1,0:T(8,128)(2,1)S(1)}, bf16[14,16,128]{2,1,0:T(8,128)(2,1)S(1)}, u32[]{:S(2)}, u32[]{:S(2)}) collective-permute-start(bf16[14,16,128]{2,1,0:T(8,128)(2,1)S(1)} %add_convert_fusion.2.mine), channel_id=1, source_target_pairs={{0,16},{16,0},{32,48},{48,32},{64,80},{80,64},{96,112},{112,96},{1... | collective-permute-start | bytes 172040 | tf_op jit(solution)/shard_map/ppermute | solution.py:439
  66.8 0.9 %collective-permute-done.11.other = bf16[14,16,128]{2,1,0:T(8,128)(2,1)S(1)} collective-permute-done((bf16[14,16,128]{2,1,0:T(8,128)(2,1)S(1)}, bf16[14,16,128]{2,1,0:T(8,128)(2,1)S(1)}, u32[]{:S(2)}, u32[]{:S(2)}) %collective-permute-start.11) | collective-permute-done | bytes 57376 | tf_op jit(solution)/shard_map/ppermute | solution.py:439
  67.7 0.7 %shard_map.73 = f32[27,16,128]{2,1,0:T(8,128)} custom-call(s32[1]{0:T(128)} %bitcast.6.half, bf16[14,16,128]{2,1,0:T(8,128)(2,1)S(1)} %add_convert_fusion.2.mine, bf16[14,16,128]{2,1,0:T(8,128)(2,1)S(1)} %collective-permute-done.11.other), custom_call_target="tpu_custom_call" | custom-call | bytes 4000000 | tf_op jit(solution)/shard_map/pallas_call | solution.py:29
  (21 shorter events, 3.6 us)
Async XLA Ops:
  0.6 6.9 %copy-start = (bf16[1,8,4,4,16]{4,3,2,1,0:T(4,128)(2,1)S(1)}, bf16[1,8,4,4,16]{4,3,2,1,0:T(4,128)(2,1)}, u32[]{:S(2)}) copy-start(bf16[1,8,4,4,16]{4,3,2,1,0:T(4,128)(2,1)} %param.7) | copy-start | bytes 12292
  0.6 6.9 %collective-permute-start = (bf16[1,2,16,16,128]{4,3,2,1,0:T(8,128)(2,1)}, bf16[1,2,16,16,128]{4,3,2,1,0:T(8,128)(2,1)S(1)}, u32[]{:S(2)}, u32[]{:S(2)}) collective-permute-start(bf16[1,2,16,16,128]{4,3,2,1,0:T(8,128)(2,1)} %param.4), channel_id=1, source_target_pairs={{0,16},{1,2},{2,1},{3,4},{4,3},{5,6},{6,5},{7,8},{8,7},{9,10},{10,... | collective-permute-start | bytes 393224 | tf_op jit(solution)/shard_map/ppermute | solution.py:467
  2.1 5.4 %collective-permute-start.1 = (bf16[1,2,16,16,128]{4,3,2,1,0:T(8,128)(2,1)}, bf16[1,2,16,16,128]{4,3,2,1,0:T(8,128)(2,1)S(1)}, u32[]{:S(2)}, u32[]{:S(2)}) collective-permute-start(bf16[1,2,16,16,128]{4,3,2,1,0:T(8,128)(2,1)} %param.4), channel_id=1, source_target_pairs={{0,1},{1,0},{2,3},{3,2},{4,5},{5,4},{6,7},{7,6},{8,9},{9,8},{10,11... | collective-permute-start | bytes 393224 | tf_op jit(solution)/shard_map/ppermute | solution.py:468
  4.1 0.9 %copy-start.2 = (bf16[1,2,16,16,128]{4,3,2,1,0:T(8,128)(2,1)S(1)}, bf16[1,2,16,16,128]{4,3,2,1,0:T(8,128)(2,1)}, u32[]{:S(2)}) copy-start(bf16[1,2,16,16,128]{4,3,2,1,0:T(8,128)(2,1)} %param.4) | copy-start | bytes 393220
  7.6 19.4 %copy-start.1 = (bf16[3,3,3,256,256]{4,3,2,1,0:T(8,128)(2,1)S(1)}, bf16[3,3,3,256,256]{4,3,2,1,0:T(8,128)(2,1)}, u32[]{:S(2)}) copy-start(bf16[3,3,3,256,256]{4,3,2,1,0:T(8,128)(2,1)} %param.6) | copy-start | bytes 10616836
  30.3 5.2 %collective-permute-start.2 = (bf16[16,14,16,128]{3,2,1,0:T(8,128)(2,1)S(1)}, bf16[16,14,16,128]{3,2,1,0:T(8,128)(2,1)S(1)}, u32[]{:S(2)}, u32[]{:S(2)}) collective-permute-start(bf16[16,14,16,128]{3,2,1,0:T(8,128)(2,1)S(1)} %get-tuple-element.48), channel_id=1, source_target_pairs={{0,16},{16,0},{32,48},{48,32},{64,80},{80,64},{96,112},{112,96},{1... | collective-permute-start | bytes 2752520 | tf_op jit(solution)/shard_map/ppermute | solution.py:439
  35.4 1.6 %collective-permute-start.3 = (bf16[14,16,256]{2,1,0:T(8,128)(2,1)S(1)}, bf16[14,16,256]{2,1,0:T(8,128)(2,1)S(1)}, u32[]{:S(2)}, u32[]{:S(2)}) collective-permute-start(bf16[14,16,256]{2,1,0:T(8,128)(2,1)S(1)} %get-tuple-element.49), channel_id=1, source_target_pairs={{0,16},{16,0},{32,48},{48,32},{64,80},{80,64},{96,112},{112,96},{1... | collective-permute-start | bytes 344072 | tf_op jit(solution)/shard_map/ppermute | solution.py:439
  37.0 18.7 %all-to-all-start.1 = ((bf16[16,224,128]{2,1,0:T(8,128)(2,1)}), bf16[16,224,128]{2,1,0:T(8,128)(2,1)S(1)}, u32[]{:S(2)}, u32[]{:S(2)}) async-start(bf16[16,224,128]{2,1,0:T(8,128)(2,1)} %bitcast.8), calls=%async_computation.1 | async-start | bytes 1835008 | tf_op jit(solution)/shard_map/all_to_all | solution.py:460
  40.7 4.8 %collective-permute-start.6 = (bf16[14,16,256]{2,1,0:T(8,128)(2,1)S(1)}, bf16[14,16,256]{2,1,0:T(8,128)(2,1)S(1)}, u32[]{:S(2)}, u32[]{:S(2)}) collective-permute-start(bf16[14,16,256]{2,1,0:T(8,128)(2,1)S(1)} %add_convert_fusion.1), channel_id=1, source_target_pairs={{0,96},{16,112},{32,0},{48,16},{64,32},{80,48},{96,64},{112,80},{1... | collective-permute-start | bytes 344072 | tf_op jit(solution)/shard_map/ppermute | solution.py:447
  43.3 5.5 %collective-permute-start.5 = (bf16[14,16,256]{2,1,0:T(8,128)(2,1)S(1)}, bf16[14,16,256]{2,1,0:T(8,128)(2,1)S(1)}, u32[]{:S(2)}, u32[]{:S(2)}) collective-permute-start(bf16[14,16,256]{2,1,0:T(8,128)(2,1)S(1)} %add_convert_fusion.1), channel_id=1, source_target_pairs={{0,64},{16,80},{32,96},{48,112},{64,0},{80,16},{96,32},{112,48},{1... | collective-permute-start | bytes 344072 | tf_op jit(solution)/shard_map/ppermute | solution.py:447
  43.8 8.4 %collective-permute-start.4 = (bf16[14,16,256]{2,1,0:T(8,128)(2,1)S(1)}, bf16[14,16,256]{2,1,0:T(8,128)(2,1)S(1)}, u32[]{:S(2)}, u32[]{:S(2)}) collective-permute-start(bf16[14,16,256]{2,1,0:T(8,128)(2,1)S(1)} %add_convert_fusion.1), channel_id=1, source_target_pairs={{0,32},{16,48},{32,64},{48,80},{64,96},{80,112},{96,0},{112,16},{1... | collective-permute-start | bytes 344072 | tf_op jit(solution)/shard_map/ppermute | solution.py:447
  52.2 1.7 %collective-permute-start.7 = (bf16[14,16,256]{2,1,0:T(8,128)(2,1)S(1)}, bf16[14,16,256]{2,1,0:T(8,128)(2,1)S(1)}, u32[]{:S(2)}, u32[]{:S(2)}) collective-permute-start(bf16[14,16,256]{2,1,0:T(8,128)(2,1)S(1)} %add_convert_fusion.mine), channel_id=1, source_target_pairs={{0,16},{16,0},{32,48},{48,32},{64,80},{80,64},{96,112},{112,96},{1... | collective-permute-start | bytes 344072 | tf_op jit(solution)/shard_map/ppermute | solution.py:439
  55.9 3.8 %collective-permute-start.10 = (bf16[14,16,128]{2,1,0:T(8,128)(2,1)S(1)}, bf16[14,16,128]{2,1,0:T(8,128)(2,1)S(1)}, u32[]{:S(2)}, u32[]{:S(2)}) collective-permute-start(bf16[14,16,128]{2,1,0:T(8,128)(2,1)S(1)} %reduce_sum.12), channel_id=1, source_target_pairs={{0,96},{16,112},{32,0},{48,16},{64,32},{80,48},{96,64},{112,80},{1... | collective-permute-start | bytes 172040 | tf_op jit(solution)/shard_map/ppermute | solution.py:447
  58.4 4.6 %collective-permute-start.9 = (bf16[14,16,128]{2,1,0:T(8,128)(2,1)S(1)}, bf16[14,16,128]{2,1,0:T(8,128)(2,1)S(1)}, u32[]{:S(2)}, u32[]{:S(2)}) collective-permute-start(bf16[14,16,128]{2,1,0:T(8,128)(2,1)S(1)} %reduce_sum.12), channel_id=1, source_target_pairs={{0,64},{16,80},{32,96},{48,112},{64,0},{80,16},{96,32},{112,48},{1... | collective-permute-start | bytes 172040 | tf_op jit(solution)/shard_map/ppermute | solution.py:447
  59.0 4.6 %collective-permute-start.8 = (bf16[14,16,128]{2,1,0:T(8,128)(2,1)S(1)}, bf16[14,16,128]{2,1,0:T(8,128)(2,1)S(1)}, u32[]{:S(2)}, u32[]{:S(2)}) collective-permute-start(bf16[14,16,128]{2,1,0:T(8,128)(2,1)S(1)} %reduce_sum.12), channel_id=1, source_target_pairs={{0,32},{16,48},{32,64},{48,80},{64,96},{80,112},{96,0},{112,16},{1... | collective-permute-start | bytes 172040 | tf_op jit(solution)/shard_map/ppermute | solution.py:447
  63.6 4.1 %collective-permute-start.11 = (bf16[14,16,128]{2,1,0:T(8,128)(2,1)S(1)}, bf16[14,16,128]{2,1,0:T(8,128)(2,1)S(1)}, u32[]{:S(2)}, u32[]{:S(2)}) collective-permute-start(bf16[14,16,128]{2,1,0:T(8,128)(2,1)S(1)} %add_convert_fusion.2.mine), channel_id=1, source_target_pairs={{0,16},{16,0},{32,48},{48,32},{64,80},{80,64},{96,112},{112,96},{1... | collective-permute-start | bytes 172040 | tf_op jit(solution)/shard_map/ppermute | solution.py:439

commit v8 on v7

--- a/solution.py
+++ b/solution.py
@@ -74,6 +74,19 @@
     return jnp.dot(cells, taps, preferred_element_type=jnp.float32)
 
 
+def rims_kernel(position, slab, for_odds, for_evens, near):
+    even = position[0] % 2 == 0
+    near[...] = slab[...]
+    for_odds[...] = jnp.where(even, slab[0], slab[1])
+    for_evens[...] = jnp.where(even, slab[1], slab[0])
+
+
+def rims_of(slab, position):
+    rim = shape((256, 128), jnp.bfloat16)
+    near = shape((2, 256, 128), jnp.bfloat16)
+    return call(rims_kernel, (rim, rim, near), [], (slab.reshape(2, 256, 128),), (position,))
+
+
 def inner_kernel(slab, kernel_far, part, padded, kernel, marks):
     loads = {}
     for depth_tap in (1, 2, 0):
@@ -112,8 +125,8 @@
 def outer_kernel(position, odds, evens, kernel, part, inner, cot, message, slope, padded, tall):
     even = position[0] % 2 == 0
     blank = jnp.zeros((256, 128), jnp.bfloat16)
-    low = jnp.where(even, odds[1], evens[1])
-    high = jnp.where(even, evens[0], odds[0])
+    low = jnp.where(even, odds[...], evens[...])
+    high = jnp.where(even, evens[...], odds[...])
     columns_of(padded, 0, jnp.where(position[0] == 0, blank, low))
     columns_of(padded, 3, jnp.where(position[0] == 15, blank, high))
     padded[1:3] = inner[...]
@@ -159,8 +172,8 @@
         ),
         [VMEM((2, 128, 128), jnp.float32)],
         (
-            odds.reshape(2, 256, 128),
-            evens.reshape(2, 256, 128),
+            odds,
+            evens,
             kernel,
             part,
             inner,
@@ -441,18 +454,14 @@
 
 def from_chips(values):
     count = lax.axis_size("dp")
-    got = []
-    for step in range(1, count // 2):
-        pairs = [(i, (i + 2 * step) % count) for i in range(count)]
-        got.append(lax.ppermute(values, "dp", pairs))
-    return got
-
-
-def total_of(values, others):
-    total = values.astype(jnp.float32)
-    for other in others:
-        total = total + other.astype(jnp.float32)
-    return total
+    return [
+        lax.ppermute(values, "dp", [(i, i ^ step) for i in range(count)]) for step in (2, 6, 4)
+    ]
+
+
+def sum_of_chips(values, others):
+    beside, across, ahead = [other.astype(jnp.float32) for other in others]
+    return ((values.astype(jnp.float32) + beside) + (across + ahead)).astype(jnp.bfloat16)
 
 
 def exchange(values):
@@ -464,10 +473,11 @@
 def shards(volume, kernel_five, kernel_six, cotangent):
     position = lax.axis_index("wide").astype(jnp.int32).reshape(1)
     half = (lax.axis_index("dp") % 2).astype(jnp.int32).reshape(1)
-    odds = lax.ppermute(volume, ("dp", "wide"), pair_perm(1))
-    evens = lax.ppermute(volume, ("dp", "wide"), pair_perm(0))
+    for_odds, for_evens, near_slab = rims_of(volume, position)
+    odds = lax.ppermute(for_odds, ("dp", "wide"), pair_perm(1))
+    evens = lax.ppermute(for_evens, ("dp", "wide"), pair_perm(0))
     cot_rows = cotangent.reshape(32, 4, 16)
-    part, inner, near_kernel = inner_five(volume, kernel_five)
+    part, inner, near_kernel = inner_five(near_slab, kernel_five)
     message, slope, padded = outer_five(odds, evens, near_kernel, part, inner, cot_rows, position)
     message, position, half, slope, padded = lax.optimization_barrier(
         (message, position, half, slope, padded)
@@ -484,15 +494,15 @@
     pair_five, got_six, mine_six, next_rows = lax.optimization_barrier(
         (pair_five, got_six, mine_six, next_rows)
     )
-    pair_six = total_of(mine_six, [got_six]).astype(jnp.bfloat16)
+    pair_six = (mine_six.astype(jnp.float32) + got_six.astype(jnp.float32)).astype(jnp.bfloat16)
     chips_six = from_chips(pair_six)
     spread = exchange(pair_five)
-    total_six = total_of(pair_six, chips_six).astype(jnp.bfloat16)
+    total_six = sum_of_chips(pair_six, chips_six)
     out_six = both_halves(half, total_six, core_swap(total_six))
     next_input = next_rows.T.reshape(1, 8, 4, 4, 16)
     spread, out_six, next_input = lax.optimization_barrier((spread, out_six, next_input))
     depth_five = spread.astype(jnp.float32).sum(0).astype(jnp.bfloat16)
-    total_five = total_of(depth_five, from_chips(depth_five)).astype(jnp.bfloat16)
+    total_five = sum_of_chips(depth_five, from_chips(depth_five))
     out_five = both_halves(half, total_five, core_swap(total_five))
     out_five = out_five.transpose(0, 2, 1).reshape(3, 3, 3, 128, 16)
     out_six = out_six.transpose(0, 2, 1).reshape(3, 3, 3, 256, 16)

time: 68.7 us -> 67.5 us (0.983)
  waiting for transfers between devices: 14 us -> 12.8 us
  blocking collectives: 18.6 us -> 17.7 us
  starting transfers between devices: 21.3 us -> 22.2 us
    ppermute x8, waiting for transfers between devices: 11.8 us -> 8.19 us  [the longest x6 8.19 us: from_chips(): lax.ppermute(values, 'dp', [(i, i ^ step) for i in range(count)])]
    all_to_all x1, waiting for transfers between devices: 1.04 us -> 3.42 us  [exchange(): got = lax.all_to_all(flat, 'wide', split_axis=0, concat_axis=0, tiled=True)]
    all_to_all x1, blocking collectives: 18.6 us -> 17.7 us  [exchange(): got = lax.all_to_all(flat, 'wide', split_axis=0, concat_axis=0, tiled=True)]
    ppermute x4, starting transfers between devices: 6.81 us -> 7.68 us  [core_swap(): return lax.ppermute(values, 'dp', [(i, i ^ 1) for i in range(count)])]
    pallas_call x7 -> x8, Pallas kernels: 11.9 us -> 12 us  [call(): pl.pallas_call(body, out_shape=out_shape, in_specs=specs, out_specs=outs,...]
  transfers between devices with their start and end apart: 13 -> 13, of which waited for: 9 -> 7; matrix products, arithmetic and copies ran while one was open for 1% -> 1% of each run, Pallas kernels for 10% -> 11%
where the time goes in v8:
time: 67.5 us; the launch traced here: 67.3 us
  starting transfers between devices  22.2 us (33%)
  blocking collectives  17.7 us (26%)
  waiting for transfers between devices  12.8 us (19%)
  Pallas kernels  12 us (18%)
  local copies, waits for them, and re-layouts  1.63 us (2%)
  between operations  0.77 us (1%)
    all_to_all x1, blocking collectives, exchange(): got = lax.all_to_all(flat, 'wide', split_axis=0, concat_axis=0, tiled=True)  17.7 us
    pallas_call x8, Pallas kernels, call(): pl.pallas_call(body, out_shape=out_shape, in_specs=specs, out_specs=outs,...  12 us
    ppermute x6, waiting for transfers between devices, from_chips(): lax.ppermute(values, 'dp', [(i, i ^ step) for i in range(count)])  8.19 us
    ppermute x4, starting transfers between devices, core_swap(): return lax.ppermute(values, 'dp', [(i, i ^ 1) for i in range(count)])  7.68 us
    ppermute x6, starting transfers between devices, from_chips(): lax.ppermute(values, 'dp', [(i, i ^ step) for i in range(count)])  7.4 us
    all_to_all x1, starting transfers between devices, exchange(): got = lax.all_to_all(flat, 'wide', split_axis=0, concat_axis=0, tiled=True)  3.65 us
    all_to_all x1, waiting for transfers between devices, exchange(): got = lax.all_to_all(flat, 'wide', split_axis=0, concat_axis=0, tiled=True)  3.42 us
    ppermute x1, starting transfers between devices, shards(): evens = lax.ppermute(for_evens, ('dp', 'wide'), pair_perm(0))  2 us
  transfers between devices with their start and end apart: 13, of which 7 were waited for; matrix products, arithmetic and copies ran while one was open for 1% of the time, Pallas kernels for 11%

profile of v8, /device:TPU:1, one launch (start us, length us, event | category | flops | bytes accessed | tf_op | source)
XLA Modules:
  0.0 67.3 jit_solution(17685248478823883580)
XLA Ops:
  0.6 0.9 %copy-done = bf16[1,2,16,16,128]{4,3,2,1,0:T(8,128)(2,1)S(1)} copy-done((bf16[1,2,16,16,128]{4,3,2,1,0:T(8,128)(2,1)S(1)}, bf16[1,2,16,16,128]{4,3,2,1,0:T(8,128)(2,1)}, u32[]{:S(2)}) %copy-start) | copy-done | bytes 131096
  1.6 1.5 %collective-permute-start = (bf16[256,128]{1,0:T(8,128)(2,1)S(1)}, bf16[256,128]{1,0:T(8,128)(2,1)S(1)}, u32[]{:S(2)}, u32[]{:S(2)}) collective-permute-start(bf16[256,128]{1,0:T(8,128)(2,1)S(1)} %get-tuple-element.34), channel_id=1, source_target_pairs={{0,16},{1,2},{2,1},{3,4},{4,3},{5,6},{6,5},{7,8},{8,7},{9,10},{10,... | collective-permute-start | bytes 196616 | tf_op jit(solution)/shard_map/ppermute | solution.py:477
  3.1 2.0 %collective-permute-start.1 = (bf16[256,128]{1,0:T(8,128)(2,1)S(1)}, bf16[256,128]{1,0:T(8,128)(2,1)S(1)}, u32[]{:S(2)}, u32[]{:S(2)}) collective-permute-start(bf16[256,128]{1,0:T(8,128)(2,1)S(1)} %get-tuple-element.35), channel_id=1, source_target_pairs={{0,1},{1,0},{2,3},{3,2},{4,5},{5,4},{6,7},{7,6},{8,9},{9,8},{10,11... | collective-permute-start | bytes 196616 | tf_op jit(solution)/shard_map/ppermute | solution.py:478
  5.1 2.5 %shard_map.68 = (f32[512,256]{1,0:T(8,128)S(1)}, bf16[2,288,384]{2,1,0:T(8,128)(2,1)S(1)}, bf16[3456,256]{1,0:T(8,128)(2,1)S(1)}) custom-call(bf16[2,256,128]{2,1,0:T(8,128)(2,1)S(1)} %get-tuple-element.36.slab, bf16[3456,256]{1,0:T(8,128)(2,1)} %bitcast.25), custom_call_target="tpu_custom_call" | custom-call | flops 600000000 | bytes 4000000 | tf_op jit(solution)/shard_map/pallas_call | solution.py:29
  7.6 0.8 %shard_map.69 = (bf16[16,144,128]{2,1,0:T(8,128)(2,1)S(1)}, f32[512,256]{1,0:T(8,128)S(1)}, bf16[4,288,384]{2,1,0:T(8,128)(2,1)S(1)}) custom-call(s32[1]{0:T(128)} %bitcast.position, bf16[256,128]{1,0:T(8,128)(2,1)S(1)} %collective-permute-done.odds, bf16[256,128]{1,0:T(8,128)(2,1)S(1)} %collective-permute-done.1.evens, ...), custom_call_target="tpu_custom_call" | custom-call | flops 300000000 | bytes 4000000 | tf_op jit(solution)/shard_map/pallas_call | solution.py:29
  8.4 17.7 %all_to_all.10.gathered = bf16[16,144,128]{2,1,0:T(8,128)(2,1)S(1)} all-to-all(bf16[16,144,128]{2,1,0:T(8,128)(2,1)S(1)} %get-tuple-element.43), channel_id=1, replica_groups=mesh['dp'=8,'wide'=16] {'wide'}, dimensions={0} | all-to-all | bytes 1179648 | tf_op jit(solution)/shard_map/all_to_all | solution.py:469
  26.1 3.3 %shard_map.70 = (bf16[256,512]{1,0:T(8,128)(2,1)S(1)}, bf16[16,14,16,128]{3,2,1,0:T(8,128)(2,1)S(1)}) custom-call(s32[1]{0:T(128)} %bitcast.position, s32[1]{0:T(128)} %bitcast.4.half, bf16[16,144,128]{2,1,0:T(8,128)(2,1)S(1)} %all_to_all.10.gathered, bf16[27,256,256]{2,1,0:T(8,128)(2,1)S(1)} %bitcast.19, f32[512,256]{1,0:T(8,128)S(1)} %get-tuple-element.51.slope, ...), custom_call_target="tpu_custom_call" | custom-call | flops 3000000000 | bytes 4000000 | tf_op jit(solution)/shard_map/pallas_call | solution.py:29
  29.4 3.1 %collective-permute-start.2 = (bf16[16,14,16,128]{3,2,1,0:T(8,128)(2,1)S(1)}, bf16[16,14,16,128]{3,2,1,0:T(8,128)(2,1)S(1)}, u32[]{:S(2)}, u32[]{:S(2)}) collective-permute-start(bf16[16,14,16,128]{3,2,1,0:T(8,128)(2,1)S(1)} %get-tuple-element.54), channel_id=1, source_target_pairs={{0,16},{16,0},{32,48},{48,32},{64,80},{80,64},{96,112},{112,96},{1... | collective-permute-start | bytes 2752520 | tf_op jit(solution)/shard_map/ppermute | solution.py:452
  32.5 2.3 %shard_map.72 = (bf16[16,128]{1,0:T(8,128)(2,1)S(1)}, bf16[14,16,256]{2,1,0:T(8,128)(2,1)S(1)}, bf16[14,16,256]{2,1,0:T(8,128)(2,1)S(1)}) custom-call(s32[1]{0:T(128)} %bitcast.position, s32[1]{0:T(128)} %bitcast.4.half, bf16[16,144,128]{2,1,0:T(8,128)(2,1)S(1)} %all_to_all.10.gathered, bf16[27,256,256]{2,1,0:T(8,128)(2,1)S(1)} %bitcast.20), custom_call_target="tpu_custom_call" | custom-call | flops 2000000000 | bytes 4000000 | tf_op jit(solution)/shard_map/pallas_call | solution.py:29
  35.0 1.5 %shard_map.71 = bf16[16,14,16,128]{3,2,1,0:T(8,128)(2,1)} custom-call(s32[1]{0:T(128)} %bitcast.4.half, bf16[256,512]{1,0:T(8,128)(2,1)S(1)} %get-tuple-element.53.rows, bf16[4,288,384]{2,1,0:T(8,128)(2,1)S(1)} %get-tuple-element.52.padded, bf16[16,14,16,128]{3,2,1,0:T(8,128)(2,1)S(1)} %collective-permute-done.2.got), custom_call_target="tpu_custom_call" | custom-call | flops 900000000 | bytes 4000000 | tf_op jit(solution)/shard_map/pallas_call | solution.py:29
  36.5 3.6 %all-to-all-start.1 = ((bf16[16,224,128]{2,1,0:T(8,128)(2,1)}), bf16[16,224,128]{2,1,0:T(8,128)(2,1)S(1)}, u32[]{:S(2)}, u32[]{:S(2)}) async-start(bf16[16,224,128]{2,1,0:T(8,128)(2,1)} %bitcast.6), calls=%async_computation.1 | async-start | bytes 1835008 | tf_op jit(solution)/shard_map/all_to_all | solution.py:469
  40.2 2.8 %collective-permute-start.6 = (bf16[14,16,256]{2,1,0:T(8,128)(2,1)S(1)}, bf16[14,16,256]{2,1,0:T(8,128)(2,1)S(1)}, u32[]{:S(2)}, u32[]{:S(2)}) collective-permute-start(bf16[14,16,256]{2,1,0:T(8,128)(2,1)S(1)} %add_convert_fusion.1), channel_id=1, source_target_pairs={{0,64},{16,80},{32,96},{48,112},{64,0},{80,16},{96,32},{112,48},{1... | collective-permute-start | bytes 344072 | tf_op jit(solution)/shard_map/ppermute | solution.py:458
  43.0 0.9 %collective-permute-start.5 = (bf16[14,16,256]{2,1,0:T(8,128)(2,1)S(1)}, bf16[14,16,256]{2,1,0:T(8,128)(2,1)S(1)}, u32[]{:S(2)}, u32[]{:S(2)}) collective-permute-start(bf16[14,16,256]{2,1,0:T(8,128)(2,1)S(1)} %add_convert_fusion.1), channel_id=1, source_target_pairs={{0,96},{16,112},{32,64},{48,80},{64,32},{80,48},{96,0},{112,16},{1... | collective-permute-start | bytes 344072 | tf_op jit(solution)/shard_map/ppermute | solution.py:458
  43.9 2.2 %collective-permute-done.6 = bf16[14,16,256]{2,1,0:T(8,128)(2,1)S(1)} collective-permute-done((bf16[14,16,256]{2,1,0:T(8,128)(2,1)S(1)}, bf16[14,16,256]{2,1,0:T(8,128)(2,1)S(1)}, u32[]{:S(2)}, u32[]{:S(2)}) %collective-permute-start.6) | collective-permute-done | bytes 114720 | tf_op jit(solution)/shard_map/ppermute | solution.py:458
  46.0 2.3 %collective-permute-done.5 = bf16[14,16,256]{2,1,0:T(8,128)(2,1)S(1)} collective-permute-done((bf16[14,16,256]{2,1,0:T(8,128)(2,1)S(1)}, bf16[14,16,256]{2,1,0:T(8,128)(2,1)S(1)}, u32[]{:S(2)}, u32[]{:S(2)}) %collective-permute-start.5) | collective-permute-done | bytes 114720 | tf_op jit(solution)/shard_map/ppermute | solution.py:458
  48.5 1.6 %collective-permute-start.7 = (bf16[14,16,256]{2,1,0:T(8,128)(2,1)S(1)}, bf16[14,16,256]{2,1,0:T(8,128)(2,1)S(1)}, u32[]{:S(2)}, u32[]{:S(2)}) collective-permute-start(bf16[14,16,256]{2,1,0:T(8,128)(2,1)S(1)} %add_convert_fusion.mine), channel_id=1, source_target_pairs={{0,16},{16,0},{32,48},{48,32},{64,80},{80,64},{96,112},{112,96},{1... | collective-permute-start | bytes 344072 | tf_op jit(solution)/shard_map/ppermute | solution.py:452
  51.0 0.8 %shard_map.73 = f32[27,16,256]{2,1,0:T(8,128)} custom-call(s32[1]{0:T(128)} %bitcast.4.half, bf16[14,16,256]{2,1,0:T(8,128)(2,1)S(1)} %add_convert_fusion.mine, bf16[14,16,256]{2,1,0:T(8,128)(2,1)S(1)} %collective-permute-done.7.other), custom_call_target="tpu_custom_call" | custom-call | bytes 4000000 | tf_op jit(solution)/shard_map/pallas_call | solution.py:29
  51.8 3.4 %all-to-all-done.1 = bf16[16,224,128]{2,1,0:T(8,128)(2,1)S(1)} async-done(((bf16[16,224,128]{2,1,0:T(8,128)(2,1)}), bf16[16,224,128]{2,1,0:T(8,128)(2,1)S(1)}, u32[]{:S(2)}, u32[]{:S(2)}) %all-to-all-start.1) | async-done | bytes 917536 | tf_op jit(solution)/shard_map/all_to_all | solution.py:469
  55.3 2.8 %collective-permute-start.10 = (bf16[14,16,128]{2,1,0:T(8,128)(2,1)S(1)}, bf16[14,16,128]{2,1,0:T(8,128)(2,1)S(1)}, u32[]{:S(2)}, u32[]{:S(2)}) collective-permute-start(bf16[14,16,128]{2,1,0:T(8,128)(2,1)S(1)} %reduce_sum.12), channel_id=1, source_target_pairs={{0,64},{16,80},{32,96},{48,112},{64,0},{80,16},{96,32},{112,48},{1... | collective-permute-start | bytes 172040 | tf_op jit(solution)/shard_map/ppermute | solution.py:458
  58.2 0.9 %collective-permute-start.9 = (bf16[14,16,128]{2,1,0:T(8,128)(2,1)S(1)}, bf16[14,16,128]{2,1,0:T(8,128)(2,1)S(1)}, u32[]{:S(2)}, u32[]{:S(2)}) collective-permute-start(bf16[14,16,128]{2,1,0:T(8,128)(2,1)S(1)} %reduce_sum.12), channel_id=1, source_target_pairs={{0,96},{16,112},{32,64},{48,80},{64,32},{80,48},{96,0},{112,16},{1... | collective-permute-start | bytes 172040 | tf_op jit(solution)/shard_map/ppermute | solution.py:458
  59.0 0.9 %collective-permute-done.10 = bf16[14,16,128]{2,1,0:T(8,128)(2,1)S(1)} collective-permute-done((bf16[14,16,128]{2,1,0:T(8,128)(2,1)S(1)}, bf16[14,16,128]{2,1,0:T(8,128)(2,1)S(1)}, u32[]{:S(2)}, u32[]{:S(2)}) %collective-permute-start.10) | collective-permute-done | bytes 57376 | tf_op jit(solution)/shard_map/ppermute | solution.py:458
  60.0 2.8 %collective-permute-done.9 = bf16[14,16,128]{2,1,0:T(8,128)(2,1)S(1)} collective-permute-done((bf16[14,16,128]{2,1,0:T(8,128)(2,1)S(1)}, bf16[14,16,128]{2,1,0:T(8,128)(2,1)S(1)}, u32[]{:S(2)}, u32[]{:S(2)}) %collective-permute-start.9) | collective-permute-done | bytes 57376 | tf_op jit(solution)/shard_map/ppermute | solution.py:458
  62.8 2.9 %collective-permute-start.11 = (bf16[14,16,128]{2,1,0:T(8,128)(2,1)S(1)}, bf16[14,16,128]{2,1,0:T(8,128)(2,1)S(1)}, u32[]{:S(2)}, u32[]{:S(2)}) collective-permute-start(bf16[14,16,128]{2,1,0:T(8,128)(2,1)S(1)} %add_convert_fusion.2.mine), channel_id=1, source_target_pairs={{0,16},{16,0},{32,48},{48,32},{64,80},{80,64},{96,112},{112,96},{1... | collective-permute-start | bytes 172040 | tf_op jit(solution)/shard_map/ppermute | solution.py:452
  65.7 0.9 %collective-permute-done.11.other = bf16[14,16,128]{2,1,0:T(8,128)(2,1)S(1)} collective-permute-done((bf16[14,16,128]{2,1,0:T(8,128)(2,1)S(1)}, bf16[14,16,128]{2,1,0:T(8,128)(2,1)S(1)}, u32[]{:S(2)}, u32[]{:S(2)}) %collective-permute-start.11) | collective-permute-done | bytes 57376 | tf_op jit(solution)/shard_map/ppermute | solution.py:452
  (22 shorter events, 2.1 us)
Async XLA Ops:
  0.6 0.9 %copy-start = (bf16[1,2,16,16,128]{4,3,2,1,0:T(8,128)(2,1)S(1)}, bf16[1,2,16,16,128]{4,3,2,1,0:T(8,128)(2,1)}, u32[]{:S(2)}) copy-start(bf16[1,2,16,16,128]{4,3,2,1,0:T(8,128)(2,1)} %param.4) | copy-start | bytes 393220
  1.5 6.0 %copy-start.1 = (bf16[1,8,4,4,16]{4,3,2,1,0:T(4,128)(2,1)S(1)}, bf16[1,8,4,4,16]{4,3,2,1,0:T(4,128)(2,1)}, u32[]{:S(2)}) copy-start(bf16[1,8,4,4,16]{4,3,2,1,0:T(4,128)(2,1)} %param.7) | copy-start | bytes 12292
  1.6 6.0 %collective-permute-start = (bf16[256,128]{1,0:T(8,128)(2,1)S(1)}, bf16[256,128]{1,0:T(8,128)(2,1)S(1)}, u32[]{:S(2)}, u32[]{:S(2)}) collective-permute-start(bf16[256,128]{1,0:T(8,128)(2,1)S(1)} %get-tuple-element.34), channel_id=1, source_target_pairs={{0,16},{1,2},{2,1},{3,4},{4,3},{5,6},{6,5},{7,8},{8,7},{9,10},{10,... | collective-permute-start | bytes 196616 | tf_op jit(solution)/shard_map/ppermute | solution.py:477
  3.1 4.5 %collective-permute-start.1 = (bf16[256,128]{1,0:T(8,128)(2,1)S(1)}, bf16[256,128]{1,0:T(8,128)(2,1)S(1)}, u32[]{:S(2)}, u32[]{:S(2)}) collective-permute-start(bf16[256,128]{1,0:T(8,128)(2,1)S(1)} %get-tuple-element.35), channel_id=1, source_target_pairs={{0,1},{1,0},{2,3},{3,2},{4,5},{5,4},{6,7},{7,6},{8,9},{9,8},{10,11... | collective-permute-start | bytes 196616 | tf_op jit(solution)/shard_map/ppermute | solution.py:478
  7.6 18.5 %copy-start.2 = (bf16[3,3,3,256,256]{4,3,2,1,0:T(8,128)(2,1)S(1)}, bf16[3,3,3,256,256]{4,3,2,1,0:T(8,128)(2,1)}, u32[]{:S(2)}) copy-start(bf16[3,3,3,256,256]{4,3,2,1,0:T(8,128)(2,1)} %param.6) | copy-start | bytes 10616836
  29.4 5.5 %collective-permute-start.2 = (bf16[16,14,16,128]{3,2,1,0:T(8,128)(2,1)S(1)}, bf16[16,14,16,128]{3,2,1,0:T(8,128)(2,1)S(1)}, u32[]{:S(2)}, u32[]{:S(2)}) collective-permute-start(bf16[16,14,16,128]{3,2,1,0:T(8,128)(2,1)S(1)} %get-tuple-element.54), channel_id=1, source_target_pairs={{0,16},{16,0},{32,48},{48,32},{64,80},{80,64},{96,112},{112,96},{1... | collective-permute-start | bytes 2752520 | tf_op jit(solution)/shard_map/ppermute | solution.py:452
  34.9 1.6 %collective-permute-start.3 = (bf16[14,16,256]{2,1,0:T(8,128)(2,1)S(1)}, bf16[14,16,256]{2,1,0:T(8,128)(2,1)S(1)}, u32[]{:S(2)}, u32[]{:S(2)}) collective-permute-start(bf16[14,16,256]{2,1,0:T(8,128)(2,1)S(1)} %get-tuple-element.55), channel_id=1, source_target_pairs={{0,16},{16,0},{32,48},{48,32},{64,80},{80,64},{96,112},{112,96},{1... | collective-permute-start | bytes 344072 | tf_op jit(solution)/shard_map/ppermute | solution.py:452
  36.5 18.7 %all-to-all-start.1 = ((bf16[16,224,128]{2,1,0:T(8,128)(2,1)}), bf16[16,224,128]{2,1,0:T(8,128)(2,1)S(1)}, u32[]{:S(2)}, u32[]{:S(2)}) async-start(bf16[16,224,128]{2,1,0:T(8,128)(2,1)} %bitcast.6), calls=%async_computation.1 | async-start | bytes 1835008 | tf_op jit(solution)/shard_map/all_to_all | solution.py:469
  40.2 5.9 %collective-permute-start.6 = (bf16[14,16,256]{2,1,0:T(8,128)(2,1)S(1)}, bf16[14,16,256]{2,1,0:T(8,128)(2,1)S(1)}, u32[]{:S(2)}, u32[]{:S(2)}) collective-permute-start(bf16[14,16,256]{2,1,0:T(8,128)(2,1)S(1)} %add_convert_fusion.1), channel_id=1, source_target_pairs={{0,64},{16,80},{32,96},{48,112},{64,0},{80,16},{96,32},{112,48},{1... | collective-permute-start | bytes 344072 | tf_op jit(solution)/shard_map/ppermute | solution.py:458
  43.0 5.3 %collective-permute-start.5 = (bf16[14,16,256]{2,1,0:T(8,128)(2,1)S(1)}, bf16[14,16,256]{2,1,0:T(8,128)(2,1)S(1)}, u32[]{:S(2)}, u32[]{:S(2)}) collective-permute-start(bf16[14,16,256]{2,1,0:T(8,128)(2,1)S(1)} %add_convert_fusion.1), channel_id=1, source_target_pairs={{0,96},{16,112},{32,64},{48,80},{64,32},{80,48},{96,0},{112,16},{1... | collective-permute-start | bytes 344072 | tf_op jit(solution)/shard_map/ppermute | solution.py:458
  43.9 4.5 %collective-permute-start.4 = (bf16[14,16,256]{2,1,0:T(8,128)(2,1)S(1)}, bf16[14,16,256]{2,1,0:T(8,128)(2,1)S(1)}, u32[]{:S(2)}, u32[]{:S(2)}) collective-permute-start(bf16[14,16,256]{2,1,0:T(8,128)(2,1)S(1)} %add_convert_fusion.1), channel_id=1, source_target_pairs={{0,32},{16,48},{32,0},{48,16},{64,96},{80,112},{96,64},{112,80},{1... | collective-permute-start | bytes 344072 | tf_op jit(solution)/shard_map/ppermute | solution.py:458
  48.5 2.5 %collective-permute-start.7 = (bf16[14,16,256]{2,1,0:T(8,128)(2,1)S(1)}, bf16[14,16,256]{2,1,0:T(8,128)(2,1)S(1)}, u32[]{:S(2)}, u32[]{:S(2)}) collective-permute-start(bf16[14,16,256]{2,1,0:T(8,128)(2,1)S(1)} %add_convert_fusion.mine), channel_id=1, source_target_pairs={{0,16},{16,0},{32,48},{48,32},{64,80},{80,64},{96,112},{112,96},{1... | collective-permute-start | bytes 344072 | tf_op jit(solution)/shard_map/ppermute | solution.py:452
  55.3 4.6 %collective-permute-start.10 = (bf16[14,16,128]{2,1,0:T(8,128)(2,1)S(1)}, bf16[14,16,128]{2,1,0:T(8,128)(2,1)S(1)}, u32[]{:S(2)}, u32[]{:S(2)}) collective-permute-start(bf16[14,16,128]{2,1,0:T(8,128)(2,1)S(1)} %reduce_sum.12), channel_id=1, source_target_pairs={{0,64},{16,80},{32,96},{48,112},{64,0},{80,16},{96,32},{112,48},{1... | collective-permute-start | bytes 172040 | tf_op jit(solution)/shard_map/ppermute | solution.py:458
  58.2 4.5 %collective-permute-start.9 = (bf16[14,16,128]{2,1,0:T(8,128)(2,1)S(1)}, bf16[14,16,128]{2,1,0:T(8,128)(2,1)S(1)}, u32[]{:S(2)}, u32[]{:S(2)}) collective-permute-start(bf16[14,16,128]{2,1,0:T(8,128)(2,1)S(1)} %reduce_sum.12), channel_id=1, source_target_pairs={{0,96},{16,112},{32,64},{48,80},{64,32},{80,48},{96,0},{112,16},{1... | collective-permute-start | bytes 172040 | tf_op jit(solution)/shard_map/ppermute | solution.py:458
  59.0 3.7 %collective-permute-start.8 = (bf16[14,16,128]{2,1,0:T(8,128)(2,1)S(1)}, bf16[14,16,128]{2,1,0:T(8,128)(2,1)S(1)}, u32[]{:S(2)}, u32[]{:S(2)}) collective-permute-start(bf16[14,16,128]{2,1,0:T(8,128)(2,1)S(1)} %reduce_sum.12), channel_id=1, source_target_pairs={{0,32},{16,48},{32,0},{48,16},{64,96},{80,112},{96,64},{112,80},{1... | collective-permute-start | bytes 172040 | tf_op jit(solution)/shard_map/ppermute | solution.py:458
  62.8 3.8 %collective-permute-start.11 = (bf16[14,16,128]{2,1,0:T(8,128)(2,1)S(1)}, bf16[14,16,128]{2,1,0:T(8,128)(2,1)S(1)}, u32[]{:S(2)}, u32[]{:S(2)}) collective-permute-start(bf16[14,16,128]{2,1,0:T(8,128)(2,1)S(1)} %add_convert_fusion.2.mine), channel_id=1, source_target_pairs={{0,16},{16,0},{32,48},{48,32},{64,80},{80,64},{96,112},{112,96},{1... | collective-permute-start | bytes 172040 | tf_op jit(solution)/shard_map/ppermute | solution.py:452

commit v9 on v8

--- a/solution.py
+++ b/solution.py
@@ -184,7 +184,7 @@
     )
 
 
-def six_to_five(position, gathered, kernel, slope, rows_out, near, tall):
+def six_to_five(position, gathered, kernel, slope, rows_out, own, near, tall):
     for plane in range(5):
         where = position[0] + (plane - 2)
         inside = (where >= 0) & (where < 16)
@@ -235,14 +235,20 @@
                 lane = (row_tap * 3 + col_tap) * 256
                 near[depth_tap, :, lane : lane + 256] = cells.astype(jnp.bfloat16)
 
+    filters = lax.broadcasted_iota(jnp.int32, (16, 256), 0) + position[0] * 16
+    lanes = lax.broadcasted_iota(jnp.int32, (16, 256), 1)
+    pick = jnp.where(filters == lanes, 1.0, 0.0).astype(jnp.bfloat16)
+
     def depth_of(depth_tap, total):
         for tap in range(9):
-            total += lax.dot_general(
-                near[depth_tap, :, tap * 256 : tap * 256 + 256],
+            both = lax.dot_general(
+                jnp.concatenate([near[depth_tap, :, tap * 256 : tap * 256 + 256], pick], axis=0),
                 kernel[depth_tap * 9 + tap],
                 NT,
                 preferred_element_type=jnp.float32,
             )
+            total += both[:64]
+            own[depth_tap * 9 + tap] = both[64:].astype(jnp.bfloat16)
         return total
 
     grad_pooled = lax.fori_loop(0, 3, depth_of, jnp.zeros((64, 256), jnp.float32))
@@ -285,15 +291,21 @@
             send(step)
 
 
-def back_kernel(position, half, gathered, kernel, slope, padded, rows, theirs, near, tall):
-    six_to_five(position, gathered, kernel, slope, rows, near, tall)
+def back_kernel(
+    position, half, gathered, kernel, slope, padded, rows, theirs, own, near, tall
+):
+    six_to_five(position, gathered, kernel, slope, rows, own, near, tall)
     half_of_five((1 - half[0]) * HALF_TAPS, rows, padded, theirs)
 
 
 def back_five(gathered, kernel, slope, padded, position, half):
     return call(
         back_kernel,
-        (shape((256, 512), jnp.bfloat16), shape((16, HALF_TAPS, 16, 128), jnp.bfloat16)),
+        (
+            shape((256, 512), jnp.bfloat16),
+            shape((16, HALF_TAPS, 16, 128), jnp.bfloat16),
+            shape((27, 16, 256), jnp.bfloat16),
+        ),
         [VMEM((5, 64, 2304), jnp.bfloat16), VMEM((2, 128, 128), jnp.float32)],
         (gathered, kernel.reshape(27, 256, 256), slope, padded),
         (position, half),
@@ -342,14 +354,8 @@
 
 
 def six_kernel(
-    position, half, gathered, kernel, next_rows, mine, theirs, own, cells, grads, whole
+    position, half, gathered, own, next_rows, mine, theirs, cells, grads, whole
 ):
-    rows = lax.broadcasted_iota(jnp.int32, (16, 256), 0) + position[0] * 16
-    lanes = lax.broadcasted_iota(jnp.int32, (16, 256), 1)
-    pick = jnp.where(rows == lanes, 1.0, 0.0).astype(jnp.bfloat16)
-    for tap in range(27):
-        chosen = lax.dot_general(pick, kernel[tap], NT, preferred_element_type=jnp.float32)
-        own[tap] = chosen.astype(jnp.bfloat16)
     blank = jnp.zeros((64, 256), jnp.bfloat16)
     cells[0:64, :] = blank
     cells[1088:1152, :] = blank
@@ -400,18 +406,17 @@
     theirs[...] = whole[pl.ds((1 - half[0]) * HALF_TAPS, HALF_TAPS)]
 
 
-def six_own(gathered, kernel, position, half):
+def six_own(gathered, own, position, half):
     part = shape((HALF_TAPS, 16, 256), jnp.bfloat16)
     return call(
         six_kernel,
         (shape((16, 128), jnp.bfloat16), part, part),
         [
-            VMEM((27, 16, 256), jnp.bfloat16),
             VMEM((1152, 256), jnp.bfloat16),
             VMEM((144, 1024), jnp.bfloat16),
             VMEM((28, 16, 256), jnp.bfloat16),
         ],
-        (gathered, kernel.reshape(27, 256, 256)),
+        (gathered, own),
         (position, half),
         flops=2_000_000_000,
     )
@@ -486,9 +491,9 @@
     gathered, position, half, slope, padded = lax.optimization_barrier(
         (gathered, position, half, slope, padded)
     )
-    rows, theirs_five = back_five(gathered, kernel_six, slope, padded, position, half)
+    rows, theirs_five, own = back_five(gathered, kernel_six, slope, padded, position, half)
     got_five = core_swap(theirs_five)
-    next_rows, mine_six, theirs_six = six_own(gathered, kernel_six, position, half)
+    next_rows, mine_six, theirs_six = six_own(gathered, own, position, half)
     got_six = core_swap(theirs_six)
     pair_five = mine_of_five(rows, padded, got_five, half)
     pair_five, got_six, mine_six, next_rows = lax.optimization_barrier(

time: 67.5 us -> 67.3 us (level)
  Pallas kernels: 12 us -> 11.1 us
  waiting for transfers between devices: 12.8 us -> 13.5 us
    pallas_call x8, Pallas kernels: 12 us -> 11.1 us  [call(): pl.pallas_call(body, out_shape=out_shape, in_specs=specs, out_specs=outs,...]
  transfers between devices with their start and end apart: 13 -> 13, of which waited for: 7 -> 9; matrix products, arithmetic and copies ran while one was open for 1% -> 1% of each run, Pallas kernels for 11% -> 9%
where the time goes in v9:
time: 67.3 us; the launch traced here: 67 us
  starting transfers between devices  22.1 us (33%)
  blocking collectives  17.7 us (26%)
  waiting for transfers between devices  13.5 us (20%)
  Pallas kernels  11.1 us (16%)
  local copies, waits for them, and re-layouts  1.63 us (2%)
  between operations  0.76 us (1%)
    all_to_all x1, blocking collectives, exchange(): got = lax.all_to_all(flat, 'wide', split_axis=0, concat_axis=0, tiled=True)  17.7 us
    pallas_call x8, Pallas kernels, call(): pl.pallas_call(body, out_shape=out_shape, in_specs=specs, out_specs=outs,...  11.1 us
    ppermute x6, waiting for transfers between devices, from_chips(): lax.ppermute(values, 'dp', [(i, i ^ step) for i in range(count)])  8.3 us
    ppermute x4, starting transfers between devices, core_swap(): return lax.ppermute(values, 'dp', [(i, i ^ 1) for i in range(count)])  7.55 us
    ppermute x6, starting transfers between devices, from_chips(): lax.ppermute(values, 'dp', [(i, i ^ step) for i in range(count)])  7.37 us
    all_to_all x1, starting transfers between devices, exchange(): got = lax.all_to_all(flat, 'wide', split_axis=0, concat_axis=0, tiled=True)  3.65 us
    all_to_all x1, waiting for transfers between devices, exchange(): got = lax.all_to_all(flat, 'wide', split_axis=0, concat_axis=0, tiled=True)  3.55 us
    ppermute x1, starting transfers between devices, shards(): evens = lax.ppermute(for_evens, ('dp', 'wide'), pair_perm(0))  2 us
  transfers between devices with their start and end apart: 13, of which 9 were waited for; matrix products, arithmetic and copies ran while one was open for 1% of the time, Pallas kernels for 9%

profile of v9, /device:TPU:1, one launch (start us, length us, event | category | flops | bytes accessed | tf_op | source)
XLA Modules:
  0.0 67.0 jit_solution(15751462994730727805)
XLA Ops:
  0.6 0.9 %copy-done = bf16[1,2,16,16,128]{4,3,2,1,0:T(8,128)(2,1)S(1)} copy-done((bf16[1,2,16,16,128]{4,3,2,1,0:T(8,128)(2,1)S(1)}, bf16[1,2,16,16,128]{4,3,2,1,0:T(8,128)(2,1)}, u32[]{:S(2)}) %copy-start) | copy-done | bytes 131096
  1.6 1.5 %collective-permute-start = (bf16[256,128]{1,0:T(8,128)(2,1)S(1)}, bf16[256,128]{1,0:T(8,128)(2,1)S(1)}, u32[]{:S(2)}, u32[]{:S(2)}) collective-permute-start(bf16[256,128]{1,0:T(8,128)(2,1)S(1)} %get-tuple-element.35), channel_id=1, source_target_pairs={{0,16},{1,2},{2,1},{3,4},{4,3},{5,6},{6,5},{7,8},{8,7},{9,10},{10,... | collective-permute-start | bytes 196616 | tf_op jit(solution)/shard_map/ppermute | solution.py:482
  3.1 2.0 %collective-permute-start.1 = (bf16[256,128]{1,0:T(8,128)(2,1)S(1)}, bf16[256,128]{1,0:T(8,128)(2,1)S(1)}, u32[]{:S(2)}, u32[]{:S(2)}) collective-permute-start(bf16[256,128]{1,0:T(8,128)(2,1)S(1)} %get-tuple-element.36), channel_id=1, source_target_pairs={{0,1},{1,0},{2,3},{3,2},{4,5},{5,4},{6,7},{7,6},{8,9},{9,8},{10,11... | collective-permute-start | bytes 196616 | tf_op jit(solution)/shard_map/ppermute | solution.py:483
  5.1 2.5 %shard_map.68 = (f32[512,256]{1,0:T(8,128)S(1)}, bf16[2,288,384]{2,1,0:T(8,128)(2,1)S(1)}, bf16[3456,256]{1,0:T(8,128)(2,1)S(1)}) custom-call(bf16[2,256,128]{2,1,0:T(8,128)(2,1)S(1)} %get-tuple-element.37.slab, bf16[3456,256]{1,0:T(8,128)(2,1)} %bitcast.24), custom_call_target="tpu_custom_call" | custom-call | flops 600000000 | bytes 4000000 | tf_op jit(solution)/shard_map/pallas_call | solution.py:29
  7.6 0.8 %shard_map.69 = (bf16[16,144,128]{2,1,0:T(8,128)(2,1)S(1)}, f32[512,256]{1,0:T(8,128)S(1)}, bf16[4,288,384]{2,1,0:T(8,128)(2,1)S(1)}) custom-call(s32[1]{0:T(128)} %bitcast.position, bf16[256,128]{1,0:T(8,128)(2,1)S(1)} %collective-permute-done.odds, bf16[256,128]{1,0:T(8,128)(2,1)S(1)} %collective-permute-done.1.evens, ...), custom_call_target="tpu_custom_call" | custom-call | flops 300000000 | bytes 4000000 | tf_op jit(solution)/shard_map/pallas_call | solution.py:29
  8.4 17.7 %all_to_all.10.gathered = bf16[16,144,128]{2,1,0:T(8,128)(2,1)S(1)} all-to-all(bf16[16,144,128]{2,1,0:T(8,128)(2,1)S(1)} %get-tuple-element.44), channel_id=1, replica_groups=mesh['dp'=8,'wide'=16] {'wide'}, dimensions={0} | all-to-all | bytes 1179648 | tf_op jit(solution)/shard_map/all_to_all | solution.py:474
  26.1 3.3 %shard_map.70 = (bf16[256,512]{1,0:T(8,128)(2,1)S(1)}, bf16[16,14,16,128]{3,2,1,0:T(8,128)(2,1)S(1)}, bf16[27,16,256]{2,1,0:T(8,128)(2,1)S(1)}) custom-call(s32[1]{0:T(128)} %bitcast.position, s32[1]{0:T(128)} %bitcast.4.half, bf16[16,144,128]{2,1,0:T(8,128)(2,1)S(1)} %all_to_all.10.gathered, bf16[27,256,256]{2,1,0:T(8,128)(2,1)S(1)} %bitcast.19, ...), custom_call_target="tpu_custom_call" | custom-call | flops 3000000000 | bytes 4000000 | tf_op jit(solution)/shard_map/pallas_call | solution.py:29
  29.4 3.1 %collective-permute-start.2 = (bf16[16,14,16,128]{3,2,1,0:T(8,128)(2,1)S(1)}, bf16[16,14,16,128]{3,2,1,0:T(8,128)(2,1)S(1)}, u32[]{:S(2)}, u32[]{:S(2)}) collective-permute-start(bf16[16,14,16,128]{3,2,1,0:T(8,128)(2,1)S(1)} %get-tuple-element.55), channel_id=1, source_target_pairs={{0,16},{16,0},{32,48},{48,32},{64,80},{80,64},{96,112},{112,96},{1... | collective-permute-start | bytes 2752520 | tf_op jit(solution)/shard_map/ppermute | solution.py:457
  32.5 1.5 %shard_map.72 = (bf16[16,128]{1,0:T(8,128)(2,1)S(1)}, bf16[14,16,256]{2,1,0:T(8,128)(2,1)S(1)}, bf16[14,16,256]{2,1,0:T(8,128)(2,1)S(1)}) custom-call(s32[1]{0:T(128)} %bitcast.position, s32[1]{0:T(128)} %bitcast.4.half, bf16[16,144,128]{2,1,0:T(8,128)(2,1)S(1)} %all_to_all.10.gathered, bf16[27,16,256]{2,1,0:T(8,128)(2,1)S(1)} %get-tuple-element.56.own), custom_call_target="tpu_custom_call" | custom-call | flops 2000000000 | bytes 4000000 | tf_op jit(solution)/shard_map/pallas_call | solution.py:29
  34.6 1.5 %shard_map.71 = bf16[16,14,16,128]{3,2,1,0:T(8,128)(2,1)} custom-call(s32[1]{0:T(128)} %bitcast.4.half, bf16[256,512]{1,0:T(8,128)(2,1)S(1)} %get-tuple-element.54.rows, bf16[4,288,384]{2,1,0:T(8,128)(2,1)S(1)} %get-tuple-element.53.padded, bf16[16,14,16,128]{3,2,1,0:T(8,128)(2,1)S(1)} %collective-permute-done.2.got), custom_call_target="tpu_custom_call" | custom-call | flops 900000000 | bytes 4000000 | tf_op jit(solution)/shard_map/pallas_call | solution.py:29
  36.1 3.6 %all-to-all-start.1 = ((bf16[16,224,128]{2,1,0:T(8,128)(2,1)}), bf16[16,224,128]{2,1,0:T(8,128)(2,1)S(1)}, u32[]{:S(2)}, u32[]{:S(2)}) async-start(bf16[16,224,128]{2,1,0:T(8,128)(2,1)} %bitcast.6), calls=%async_computation.1 | async-start | bytes 1835008 | tf_op jit(solution)/shard_map/all_to_all | solution.py:474
  39.8 2.8 %collective-permute-start.6 = (bf16[14,16,256]{2,1,0:T(8,128)(2,1)S(1)}, bf16[14,16,256]{2,1,0:T(8,128)(2,1)S(1)}, u32[]{:S(2)}, u32[]{:S(2)}) collective-permute-start(bf16[14,16,256]{2,1,0:T(8,128)(2,1)S(1)} %add_convert_fusion.1), channel_id=1, source_target_pairs={{0,64},{16,80},{32,96},{48,112},{64,0},{80,16},{96,32},{112,48},{1... | collective-permute-start | bytes 344072 | tf_op jit(solution)/shard_map/ppermute | solution.py:463
  42.7 0.9 %collective-permute-start.5 = (bf16[14,16,256]{2,1,0:T(8,128)(2,1)S(1)}, bf16[14,16,256]{2,1,0:T(8,128)(2,1)S(1)}, u32[]{:S(2)}, u32[]{:S(2)}) collective-permute-start(bf16[14,16,256]{2,1,0:T(8,128)(2,1)S(1)} %add_convert_fusion.1), channel_id=1, source_target_pairs={{0,96},{16,112},{32,64},{48,80},{64,32},{80,48},{96,0},{112,16},{1... | collective-permute-start | bytes 344072 | tf_op jit(solution)/shard_map/ppermute | solution.py:463
  43.5 2.3 %collective-permute-done.6 = bf16[14,16,256]{2,1,0:T(8,128)(2,1)S(1)} collective-permute-done((bf16[14,16,256]{2,1,0:T(8,128)(2,1)S(1)}, bf16[14,16,256]{2,1,0:T(8,128)(2,1)S(1)}, u32[]{:S(2)}, u32[]{:S(2)}) %collective-permute-start.6) | collective-permute-done | bytes 114720 | tf_op jit(solution)/shard_map/ppermute | solution.py:463
  45.8 2.2 %collective-permute-done.5 = bf16[14,16,256]{2,1,0:T(8,128)(2,1)S(1)} collective-permute-done((bf16[14,16,256]{2,1,0:T(8,128)(2,1)S(1)}, bf16[14,16,256]{2,1,0:T(8,128)(2,1)S(1)}, u32[]{:S(2)}, u32[]{:S(2)}) %collective-permute-start.5) | collective-permute-done | bytes 114720 | tf_op jit(solution)/shard_map/ppermute | solution.py:463
  48.2 1.5 %collective-permute-start.7 = (bf16[14,16,256]{2,1,0:T(8,128)(2,1)S(1)}, bf16[14,16,256]{2,1,0:T(8,128)(2,1)S(1)}, u32[]{:S(2)}, u32[]{:S(2)}) collective-permute-start(bf16[14,16,256]{2,1,0:T(8,128)(2,1)S(1)} %add_convert_fusion.mine), channel_id=1, source_target_pairs={{0,16},{16,0},{32,48},{48,32},{64,80},{80,64},{96,112},{112,96},{1... | collective-permute-start | bytes 344072 | tf_op jit(solution)/shard_map/ppermute | solution.py:457
  50.6 0.8 %shard_map.73 = f32[27,16,256]{2,1,0:T(8,128)} custom-call(s32[1]{0:T(128)} %bitcast.4.half, bf16[14,16,256]{2,1,0:T(8,128)(2,1)S(1)} %add_convert_fusion.mine, bf16[14,16,256]{2,1,0:T(8,128)(2,1)S(1)} %collective-permute-done.7.other), custom_call_target="tpu_custom_call" | custom-call | bytes 4000000 | tf_op jit(solution)/shard_map/pallas_call | solution.py:29
  51.4 3.5 %all-to-all-done.1 = bf16[16,224,128]{2,1,0:T(8,128)(2,1)S(1)} async-done(((bf16[16,224,128]{2,1,0:T(8,128)(2,1)}), bf16[16,224,128]{2,1,0:T(8,128)(2,1)S(1)}, u32[]{:S(2)}, u32[]{:S(2)}) %all-to-all-start.1) | async-done | bytes 917536 | tf_op jit(solution)/shard_map/all_to_all | solution.py:474
  55.1 2.8 %collective-permute-start.10 = (bf16[14,16,128]{2,1,0:T(8,128)(2,1)S(1)}, bf16[14,16,128]{2,1,0:T(8,128)(2,1)S(1)}, u32[]{:S(2)}, u32[]{:S(2)}) collective-permute-start(bf16[14,16,128]{2,1,0:T(8,128)(2,1)S(1)} %reduce_sum.12), channel_id=1, source_target_pairs={{0,64},{16,80},{32,96},{48,112},{64,0},{80,16},{96,32},{112,48},{1... | collective-permute-start | bytes 172040 | tf_op jit(solution)/shard_map/ppermute | solution.py:463
  57.9 0.9 %collective-permute-start.9 = (bf16[14,16,128]{2,1,0:T(8,128)(2,1)S(1)}, bf16[14,16,128]{2,1,0:T(8,128)(2,1)S(1)}, u32[]{:S(2)}, u32[]{:S(2)}) collective-permute-start(bf16[14,16,128]{2,1,0:T(8,128)(2,1)S(1)} %reduce_sum.12), channel_id=1, source_target_pairs={{0,96},{16,112},{32,64},{48,80},{64,32},{80,48},{96,0},{112,16},{1... | collective-permute-start | bytes 172040 | tf_op jit(solution)/shard_map/ppermute | solution.py:463
  58.8 0.9 %collective-permute-done.10 = bf16[14,16,128]{2,1,0:T(8,128)(2,1)S(1)} collective-permute-done((bf16[14,16,128]{2,1,0:T(8,128)(2,1)S(1)}, bf16[14,16,128]{2,1,0:T(8,128)(2,1)S(1)}, u32[]{:S(2)}, u32[]{:S(2)}) %collective-permute-start.10) | collective-permute-done | bytes 57376 | tf_op jit(solution)/shard_map/ppermute | solution.py:463
  59.7 2.7 %collective-permute-done.9 = bf16[14,16,128]{2,1,0:T(8,128)(2,1)S(1)} collective-permute-done((bf16[14,16,128]{2,1,0:T(8,128)(2,1)S(1)}, bf16[14,16,128]{2,1,0:T(8,128)(2,1)S(1)}, u32[]{:S(2)}, u32[]{:S(2)}) %collective-permute-start.9) | collective-permute-done | bytes 57376 | tf_op jit(solution)/shard_map/ppermute | solution.py:463
  62.5 2.9 %collective-permute-start.11 = (bf16[14,16,128]{2,1,0:T(8,128)(2,1)S(1)}, bf16[14,16,128]{2,1,0:T(8,128)(2,1)S(1)}, u32[]{:S(2)}, u32[]{:S(2)}) collective-permute-start(bf16[14,16,128]{2,1,0:T(8,128)(2,1)S(1)} %add_convert_fusion.2.mine), channel_id=1, source_target_pairs={{0,16},{16,0},{32,48},{48,32},{64,80},{80,64},{96,112},{112,96},{1... | collective-permute-start | bytes 172040 | tf_op jit(solution)/shard_map/ppermute | solution.py:457
  65.4 0.9 %collective-permute-done.11.other = bf16[14,16,128]{2,1,0:T(8,128)(2,1)S(1)} collective-permute-done((bf16[14,16,128]{2,1,0:T(8,128)(2,1)S(1)}, bf16[14,16,128]{2,1,0:T(8,128)(2,1)S(1)}, u32[]{:S(2)}, u32[]{:S(2)}) %collective-permute-start.11) | collective-permute-done | bytes 57376 | tf_op jit(solution)/shard_map/ppermute | solution.py:457
  (22 shorter events, 2.7 us)
Async XLA Ops:
  0.6 0.9 %copy-start = (bf16[1,2,16,16,128]{4,3,2,1,0:T(8,128)(2,1)S(1)}, bf16[1,2,16,16,128]{4,3,2,1,0:T(8,128)(2,1)}, u32[]{:S(2)}) copy-start(bf16[1,2,16,16,128]{4,3,2,1,0:T(8,128)(2,1)} %param.4) | copy-start | bytes 393220
  1.5 6.0 %copy-start.1 = (bf16[1,8,4,4,16]{4,3,2,1,0:T(4,128)(2,1)S(1)}, bf16[1,8,4,4,16]{4,3,2,1,0:T(4,128)(2,1)}, u32[]{:S(2)}) copy-start(bf16[1,8,4,4,16]{4,3,2,1,0:T(4,128)(2,1)} %param.7) | copy-start | bytes 12292
  1.6 6.0 %collective-permute-start = (bf16[256,128]{1,0:T(8,128)(2,1)S(1)}, bf16[256,128]{1,0:T(8,128)(2,1)S(1)}, u32[]{:S(2)}, u32[]{:S(2)}) collective-permute-start(bf16[256,128]{1,0:T(8,128)(2,1)S(1)} %get-tuple-element.35), channel_id=1, source_target_pairs={{0,16},{1,2},{2,1},{3,4},{4,3},{5,6},{6,5},{7,8},{8,7},{9,10},{10,... | collective-permute-start | bytes 196616 | tf_op jit(solution)/shard_map/ppermute | solution.py:482
  3.1 4.5 %collective-permute-start.1 = (bf16[256,128]{1,0:T(8,128)(2,1)S(1)}, bf16[256,128]{1,0:T(8,128)(2,1)S(1)}, u32[]{:S(2)}, u32[]{:S(2)}) collective-permute-start(bf16[256,128]{1,0:T(8,128)(2,1)S(1)} %get-tuple-element.36), channel_id=1, source_target_pairs={{0,1},{1,0},{2,3},{3,2},{4,5},{5,4},{6,7},{7,6},{8,9},{9,8},{10,11... | collective-permute-start | bytes 196616 | tf_op jit(solution)/shard_map/ppermute | solution.py:483
  7.6 18.5 %copy-start.2 = (bf16[3,3,3,256,256]{4,3,2,1,0:T(8,128)(2,1)S(1)}, bf16[3,3,3,256,256]{4,3,2,1,0:T(8,128)(2,1)}, u32[]{:S(2)}) copy-start(bf16[3,3,3,256,256]{4,3,2,1,0:T(8,128)(2,1)} %param.6) | copy-start | bytes 10616836
  29.4 5.2 %collective-permute-start.2 = (bf16[16,14,16,128]{3,2,1,0:T(8,128)(2,1)S(1)}, bf16[16,14,16,128]{3,2,1,0:T(8,128)(2,1)S(1)}, u32[]{:S(2)}, u32[]{:S(2)}) collective-permute-start(bf16[16,14,16,128]{3,2,1,0:T(8,128)(2,1)S(1)} %get-tuple-element.55), channel_id=1, source_target_pairs={{0,16},{16,0},{32,48},{48,32},{64,80},{80,64},{96,112},{112,96},{1... | collective-permute-start | bytes 2752520 | tf_op jit(solution)/shard_map/ppermute | solution.py:457
  34.1 2.1 %collective-permute-start.3 = (bf16[14,16,256]{2,1,0:T(8,128)(2,1)S(1)}, bf16[14,16,256]{2,1,0:T(8,128)(2,1)S(1)}, u32[]{:S(2)}, u32[]{:S(2)}) collective-permute-start(bf16[14,16,256]{2,1,0:T(8,128)(2,1)S(1)} %get-tuple-element.57), channel_id=1, source_target_pairs={{0,16},{16,0},{32,48},{48,32},{64,80},{80,64},{96,112},{112,96},{1... | collective-permute-start | bytes 344072 | tf_op jit(solution)/shard_map/ppermute | solution.py:457
  36.1 18.9 %all-to-all-start.1 = ((bf16[16,224,128]{2,1,0:T(8,128)(2,1)}), bf16[16,224,128]{2,1,0:T(8,128)(2,1)S(1)}, u32[]{:S(2)}, u32[]{:S(2)}) async-start(bf16[16,224,128]{2,1,0:T(8,128)(2,1)} %bitcast.6), calls=%async_computation.1 | async-start | bytes 1835008 | tf_op jit(solution)/shard_map/all_to_all | solution.py:474
  39.8 5.9 %collective-permute-start.6 = (bf16[14,16,256]{2,1,0:T(8,128)(2,1)S(1)}, bf16[14,16,256]{2,1,0:T(8,128)(2,1)S(1)}, u32[]{:S(2)}, u32[]{:S(2)}) collective-permute-start(bf16[14,16,256]{2,1,0:T(8,128)(2,1)S(1)} %add_convert_fusion.1), channel_id=1, source_target_pairs={{0,64},{16,80},{32,96},{48,112},{64,0},{80,16},{96,32},{112,48},{1... | collective-permute-start | bytes 344072 | tf_op jit(solution)/shard_map/ppermute | solution.py:463
  42.7 5.4 %collective-permute-start.5 = (bf16[14,16,256]{2,1,0:T(8,128)(2,1)S(1)}, bf16[14,16,256]{2,1,0:T(8,128)(2,1)S(1)}, u32[]{:S(2)}, u32[]{:S(2)}) collective-permute-start(bf16[14,16,256]{2,1,0:T(8,128)(2,1)S(1)} %add_convert_fusion.1), channel_id=1, source_target_pairs={{0,96},{16,112},{32,64},{48,80},{64,32},{80,48},{96,0},{112,16},{1... | collective-permute-start | bytes 344072 | tf_op jit(solution)/shard_map/ppermute | solution.py:463
  43.5 4.6 %collective-permute-start.4 = (bf16[14,16,256]{2,1,0:T(8,128)(2,1)S(1)}, bf16[14,16,256]{2,1,0:T(8,128)(2,1)S(1)}, u32[]{:S(2)}, u32[]{:S(2)}) collective-permute-start(bf16[14,16,256]{2,1,0:T(8,128)(2,1)S(1)} %add_convert_fusion.1), channel_id=1, source_target_pairs={{0,32},{16,48},{32,0},{48,16},{64,96},{80,112},{96,64},{112,80},{1... | collective-permute-start | bytes 344072 | tf_op jit(solution)/shard_map/ppermute | solution.py:463
  48.2 2.4 %collective-permute-start.7 = (bf16[14,16,256]{2,1,0:T(8,128)(2,1)S(1)}, bf16[14,16,256]{2,1,0:T(8,128)(2,1)S(1)}, u32[]{:S(2)}, u32[]{:S(2)}) collective-permute-start(bf16[14,16,256]{2,1,0:T(8,128)(2,1)S(1)} %add_convert_fusion.mine), channel_id=1, source_target_pairs={{0,16},{16,0},{32,48},{48,32},{64,80},{80,64},{96,112},{112,96},{1... | collective-permute-start | bytes 344072 | tf_op jit(solution)/shard_map/ppermute | solution.py:457
  55.1 4.6 %collective-permute-start.10 = (bf16[14,16,128]{2,1,0:T(8,128)(2,1)S(1)}, bf16[14,16,128]{2,1,0:T(8,128)(2,1)S(1)}, u32[]{:S(2)}, u32[]{:S(2)}) collective-permute-start(bf16[14,16,128]{2,1,0:T(8,128)(2,1)S(1)} %reduce_sum.12), channel_id=1, source_target_pairs={{0,64},{16,80},{32,96},{48,112},{64,0},{80,16},{96,32},{112,48},{1... | collective-permute-start | bytes 172040 | tf_op jit(solution)/shard_map/ppermute | solution.py:463
  57.9 4.5 %collective-permute-start.9 = (bf16[14,16,128]{2,1,0:T(8,128)(2,1)S(1)}, bf16[14,16,128]{2,1,0:T(8,128)(2,1)S(1)}, u32[]{:S(2)}, u32[]{:S(2)}) collective-permute-start(bf16[14,16,128]{2,1,0:T(8,128)(2,1)S(1)} %reduce_sum.12), channel_id=1, source_target_pairs={{0,96},{16,112},{32,64},{48,80},{64,32},{80,48},{96,0},{112,16},{1... | collective-permute-start | bytes 172040 | tf_op jit(solution)/shard_map/ppermute | solution.py:463
  58.8 3.7 %collective-permute-start.8 = (bf16[14,16,128]{2,1,0:T(8,128)(2,1)S(1)}, bf16[14,16,128]{2,1,0:T(8,128)(2,1)S(1)}, u32[]{:S(2)}, u32[]{:S(2)}) collective-permute-start(bf16[14,16,128]{2,1,0:T(8,128)(2,1)S(1)} %reduce_sum.12), channel_id=1, source_target_pairs={{0,32},{16,48},{32,0},{48,16},{64,96},{80,112},{96,64},{112,80},{1... | collective-permute-start | bytes 172040 | tf_op jit(solution)/shard_map/ppermute | solution.py:463
  62.5 3.8 %collective-permute-start.11 = (bf16[14,16,128]{2,1,0:T(8,128)(2,1)S(1)}, bf16[14,16,128]{2,1,0:T(8,128)(2,1)S(1)}, u32[]{:S(2)}, u32[]{:S(2)}) collective-permute-start(bf16[14,16,128]{2,1,0:T(8,128)(2,1)S(1)} %add_convert_fusion.2.mine), channel_id=1, source_target_pairs={{0,16},{16,0},{32,48},{48,32},{64,80},{80,64},{96,112},{112,96},{1... | collective-permute-start | bytes 172040 | tf_op jit(solution)/shard_map/ppermute | solution.py:457

commit v10 on v9

--- a/solution.py
+++ b/solution.py
@@ -84,41 +84,25 @@
 def rims_of(slab, position):
     rim = shape((256, 128), jnp.bfloat16)
     near = shape((2, 256, 128), jnp.bfloat16)
-    return call(rims_kernel, (rim, rim, near), [], (slab.reshape(2, 256, 128),), (position,))
-
-
-def inner_kernel(slab, kernel_far, part, padded, kernel, marks):
-    loads = {}
-    for depth_tap in (1, 2, 0):
-        rows = pl.ds(depth_tap * 1152, 1152)
-        loads[depth_tap] = pltpu.make_async_copy(
-            kernel_far.at[rows], kernel.at[rows], marks.at[depth_tap]
-        )
-        loads[depth_tap].start()
+    return call(rims_kernel, (rim, rim, near), [], (slab.reshape(2, 256, 128),), (position,), flops=6_000_000_000)
+
+
+def inner_kernel(slab, kernel, part, padded):
     for plane in range(2):
         columns_of(padded, plane, slab[plane])
-    loads[1].wait()
     for plane in range(2):
-        part[plane * 256 : (plane + 1) * 256, :] = depth_term(padded, plane, 1, kernel, 1)
-    loads[2].wait()
-    part[0:256, :] += depth_term(padded, 1, 1, kernel, 2)
-    loads[0].wait()
-    part[256:512, :] += depth_term(padded, 0, 1, kernel, 0)
+        total = depth_term(padded, plane, 1, kernel, 1)
+        total += depth_term(padded, 1 - plane, 1, kernel, 2 - 2 * plane)
+        part[plane * 256 : (plane + 1) * 256, :] = total
 
 
 def inner_five(slab, kernel):
     return call(
         inner_kernel,
-        (
-            shape((512, 256), jnp.float32),
-            shape((2, 288, 384), jnp.bfloat16),
-            shape((3456, 256), jnp.bfloat16),
-        ),
-        [pltpu.SemaphoreType.DMA((3,))],
-        (slab.reshape(2, 256, 128), kernel.reshape(3456, 256)),
+        (shape((512, 256), jnp.float32), shape((2, 288, 384), jnp.bfloat16)),
+        [],
+        (slab, kernel.reshape(3456, 256)),
         flops=600_000_000,
-        limit=51,
-        far=(1,),
     )
 
 
@@ -482,8 +466,8 @@
     odds = lax.ppermute(for_odds, ("dp", "wide"), pair_perm(1))
     evens = lax.ppermute(for_evens, ("dp", "wide"), pair_perm(0))
     cot_rows = cotangent.reshape(32, 4, 16)
-    part, inner, near_kernel = inner_five(near_slab, kernel_five)
-    message, slope, padded = outer_five(odds, evens, near_kernel, part, inner, cot_rows, position)
+    part, inner = inner_five(near_slab, kernel_five)
+    message, slope, padded = outer_five(odds, evens, kernel_five.reshape(3456, 256), part, inner, cot_rows, position)
     message, position, half, slope, padded = lax.optimization_barrier(
         (message, position, half, slope, padded)
     )

time: 67.3 us -> 67.1 us (level)
  Pallas kernels: 11.1 us -> 9.53 us
  blocking collectives: 17.7 us -> 18.4 us
  waiting for transfers between devices: 13.5 us -> 14.2 us
    pallas_call x8, Pallas kernels: 11.1 us -> 9.53 us  [call(): pl.pallas_call(body, out_shape=out_shape, in_specs=specs, out_specs=outs,...]
    ppermute x1, waiting for transfers between devices: 0.01 us -> 0.77 us  [shards(): evens = lax.ppermute(for_evens, ('dp', 'wide'), pair_perm(0))]
    all_to_all x1, blocking collectives: 17.7 us -> 18.4 us  [exchange(): got = lax.all_to_all(flat, 'wide', split_axis=0, concat_axis=0, tiled=True)]
  transfers between devices with their start and end apart: 13 -> 13, of which waited for: 9 -> 10; matrix products, arithmetic and copies ran while one was open for 1% -> 1% of each run, Pallas kernels for 9% -> 7%
where the time goes in v10:
time: 67.1 us; the launch traced here: 66.9 us
  starting transfers between devices  22.1 us (33%)
  blocking collectives  18.4 us (27%)
  waiting for transfers between devices  14.2 us (21%)
  Pallas kernels  9.53 us (14%)
  local copies, waits for them, and re-layouts  1.63 us (2%)
  between operations  0.74 us (1%)
    all_to_all x1, blocking collectives, exchange(): got = lax.all_to_all(flat, 'wide', split_axis=0, concat_axis=0, tiled=True)  18.4 us
    pallas_call x8, Pallas kernels, call(): pl.pallas_call(body, out_shape=out_shape, in_specs=specs, out_specs=outs,...  9.53 us
    ppermute x6, waiting for transfers between devices, from_chips(): lax.ppermute(values, 'dp', [(i, i ^ step) for i in range(count)])  8.29 us
    ppermute x4, starting transfers between devices, core_swap(): return lax.ppermute(values, 'dp', [(i, i ^ 1) for i in range(count)])  7.55 us
    ppermute x6, starting transfers between devices, from_chips(): lax.ppermute(values, 'dp', [(i, i ^ step) for i in range(count)])  7.37 us
    all_to_all x1, starting transfers between devices, exchange(): got = lax.all_to_all(flat, 'wide', split_axis=0, concat_axis=0, tiled=True)  3.65 us
    all_to_all x1, waiting for transfers between devices, exchange(): got = lax.all_to_all(flat, 'wide', split_axis=0, concat_axis=0, tiled=True)  3.55 us
    ppermute x1, starting transfers between devices, shards(): evens = lax.ppermute(for_evens, ('dp', 'wide'), pair_perm(0))  2 us
  transfers between devices with their start and end apart: 13, of which 10 were waited for; matrix products, arithmetic and copies ran while one was open for 1% of the time, Pallas kernels for 7%

profile of v10, /device:TPU:1, one launch (start us, length us, event | category | flops | bytes accessed | tf_op | source)
XLA Modules:
  0.0 66.9 jit_solution(7109809658406555342)
XLA Ops:
  0.6 0.9 %copy-done.3 = bf16[1,2,16,16,128]{4,3,2,1,0:T(8,128)(2,1)S(1)} copy-done((bf16[1,2,16,16,128]{4,3,2,1,0:T(8,128)(2,1)S(1)}, bf16[1,2,16,16,128]{4,3,2,1,0:T(8,128)(2,1)}, u32[]{:S(2)}) %copy-start.3) | copy-done | bytes 131096
  1.6 1.5 %collective-permute-start = (bf16[256,128]{1,0:T(8,128)(2,1)S(1)}, bf16[256,128]{1,0:T(8,128)(2,1)S(1)}, u32[]{:S(2)}, u32[]{:S(2)}) collective-permute-start(bf16[256,128]{1,0:T(8,128)(2,1)S(1)} %get-tuple-element.34), channel_id=1, source_target_pairs={{0,16},{1,2},{2,1},{3,4},{4,3},{5,6},{6,5},{7,8},{8,7},{9,10},{10,... | collective-permute-start | bytes 196616 | tf_op jit(solution)/shard_map/ppermute | solution.py:466
  3.1 2.0 %collective-permute-start.1 = (bf16[256,128]{1,0:T(8,128)(2,1)S(1)}, bf16[256,128]{1,0:T(8,128)(2,1)S(1)}, u32[]{:S(2)}, u32[]{:S(2)}) collective-permute-start(bf16[256,128]{1,0:T(8,128)(2,1)S(1)} %get-tuple-element.35), channel_id=1, source_target_pairs={{0,1},{1,0},{2,3},{3,2},{4,5},{5,4},{6,7},{7,6},{8,9},{9,8},{10,11... | collective-permute-start | bytes 196616 | tf_op jit(solution)/shard_map/ppermute | solution.py:467
  5.1 0.9 %shard_map.68 = (f32[512,256]{1,0:T(8,128)S(1)}, bf16[2,288,384]{2,1,0:T(8,128)(2,1)S(1)}) custom-call(bf16[2,256,128]{2,1,0:T(8,128)(2,1)S(1)} %get-tuple-element.36.slab, bf16[3456,256]{1,0:T(8,128)(2,1)S(1)} %bitcast.16), custom_call_target="tpu_custom_call" | custom-call | flops 600000000 | bytes 4000000 | tf_op jit(solution)/shard_map/pallas_call | solution.py:29
  6.8 0.8 %shard_map.69 = (bf16[16,144,128]{2,1,0:T(8,128)(2,1)S(1)}, f32[512,256]{1,0:T(8,128)S(1)}, bf16[4,288,384]{2,1,0:T(8,128)(2,1)S(1)}) custom-call(s32[1]{0:T(128)} %bitcast.position, bf16[256,128]{1,0:T(8,128)(2,1)S(1)} %collective-permute-done.odds, bf16[256,128]{1,0:T(8,128)(2,1)S(1)} %collective-permute-done.1.evens, bf16[3456,256]{1,0:T(8,128)(2,1)S(1)} %bitcast.17, ...), custom_call_target="tpu_custom_call" | custom-call | flops 300000000 | bytes 4000000 | tf_op jit(solution)/shard_map/pallas_call | solution.py:29
  7.6 18.4 %all_to_all.10.gathered = bf16[16,144,128]{2,1,0:T(8,128)(2,1)S(1)} all-to-all(bf16[16,144,128]{2,1,0:T(8,128)(2,1)S(1)} %get-tuple-element.42), channel_id=1, replica_groups=mesh['dp'=8,'wide'=16] {'wide'}, dimensions={0} | all-to-all | bytes 1179648 | tf_op jit(solution)/shard_map/all_to_all | solution.py:458
  26.0 3.3 %shard_map.70 = (bf16[256,512]{1,0:T(8,128)(2,1)S(1)}, bf16[16,14,16,128]{3,2,1,0:T(8,128)(2,1)S(1)}, bf16[27,16,256]{2,1,0:T(8,128)(2,1)S(1)}) custom-call(s32[1]{0:T(128)} %bitcast.position, s32[1]{0:T(128)} %bitcast.4.half, bf16[16,144,128]{2,1,0:T(8,128)(2,1)S(1)} %all_to_all.10.gathered, bf16[27,256,256]{2,1,0:T(8,128)(2,1)S(1)} %bitcast.20, ...), custom_call_target="tpu_custom_call" | custom-call | flops 3000000000 | bytes 4000000 | tf_op jit(solution)/shard_map/pallas_call | solution.py:29
  29.3 3.1 %collective-permute-start.2 = (bf16[16,14,16,128]{3,2,1,0:T(8,128)(2,1)S(1)}, bf16[16,14,16,128]{3,2,1,0:T(8,128)(2,1)S(1)}, u32[]{:S(2)}, u32[]{:S(2)}) collective-permute-start(bf16[16,14,16,128]{3,2,1,0:T(8,128)(2,1)S(1)} %get-tuple-element.53), channel_id=1, source_target_pairs={{0,16},{16,0},{32,48},{48,32},{64,80},{80,64},{96,112},{112,96},{1... | collective-permute-start | bytes 2752520 | tf_op jit(solution)/shard_map/ppermute | solution.py:441
  32.4 1.5 %shard_map.72 = (bf16[16,128]{1,0:T(8,128)(2,1)S(1)}, bf16[14,16,256]{2,1,0:T(8,128)(2,1)S(1)}, bf16[14,16,256]{2,1,0:T(8,128)(2,1)S(1)}) custom-call(s32[1]{0:T(128)} %bitcast.position, s32[1]{0:T(128)} %bitcast.4.half, bf16[16,144,128]{2,1,0:T(8,128)(2,1)S(1)} %all_to_all.10.gathered, bf16[27,16,256]{2,1,0:T(8,128)(2,1)S(1)} %get-tuple-element.54.own), custom_call_target="tpu_custom_call" | custom-call | flops 2000000000 | bytes 4000000 | tf_op jit(solution)/shard_map/pallas_call | solution.py:29
  34.5 1.5 %shard_map.71 = bf16[16,14,16,128]{3,2,1,0:T(8,128)(2,1)} custom-call(s32[1]{0:T(128)} %bitcast.4.half, bf16[256,512]{1,0:T(8,128)(2,1)S(1)} %get-tuple-element.52.rows, bf16[4,288,384]{2,1,0:T(8,128)(2,1)S(1)} %get-tuple-element.51.padded, bf16[16,14,16,128]{3,2,1,0:T(8,128)(2,1)S(1)} %collective-permute-done.2.got), custom_call_target="tpu_custom_call" | custom-call | flops 900000000 | bytes 4000000 | tf_op jit(solution)/shard_map/pallas_call | solution.py:29
  36.0 3.6 %all-to-all-start.1 = ((bf16[16,224,128]{2,1,0:T(8,128)(2,1)}), bf16[16,224,128]{2,1,0:T(8,128)(2,1)S(1)}, u32[]{:S(2)}, u32[]{:S(2)}) async-start(bf16[16,224,128]{2,1,0:T(8,128)(2,1)} %bitcast.6), calls=%async_computation.1 | async-start | bytes 1835008 | tf_op jit(solution)/shard_map/all_to_all | solution.py:458
  39.7 2.8 %collective-permute-start.6 = (bf16[14,16,256]{2,1,0:T(8,128)(2,1)S(1)}, bf16[14,16,256]{2,1,0:T(8,128)(2,1)S(1)}, u32[]{:S(2)}, u32[]{:S(2)}) collective-permute-start(bf16[14,16,256]{2,1,0:T(8,128)(2,1)S(1)} %add_convert_fusion.1), channel_id=1, source_target_pairs={{0,64},{16,80},{32,96},{48,112},{64,0},{80,16},{96,32},{112,48},{1... | collective-permute-start | bytes 344072 | tf_op jit(solution)/shard_map/ppermute | solution.py:447
  42.5 0.9 %collective-permute-start.5 = (bf16[14,16,256]{2,1,0:T(8,128)(2,1)S(1)}, bf16[14,16,256]{2,1,0:T(8,128)(2,1)S(1)}, u32[]{:S(2)}, u32[]{:S(2)}) collective-permute-start(bf16[14,16,256]{2,1,0:T(8,128)(2,1)S(1)} %add_convert_fusion.1), channel_id=1, source_target_pairs={{0,96},{16,112},{32,64},{48,80},{64,32},{80,48},{96,0},{112,16},{1... | collective-permute-start | bytes 344072 | tf_op jit(solution)/shard_map/ppermute | solution.py:447
  43.4 2.3 %collective-permute-done.6 = bf16[14,16,256]{2,1,0:T(8,128)(2,1)S(1)} collective-permute-done((bf16[14,16,256]{2,1,0:T(8,128)(2,1)S(1)}, bf16[14,16,256]{2,1,0:T(8,128)(2,1)S(1)}, u32[]{:S(2)}, u32[]{:S(2)}) %collective-permute-start.6) | collective-permute-done | bytes 114720 | tf_op jit(solution)/shard_map/ppermute | solution.py:447
  45.7 2.2 %collective-permute-done.5 = bf16[14,16,256]{2,1,0:T(8,128)(2,1)S(1)} collective-permute-done((bf16[14,16,256]{2,1,0:T(8,128)(2,1)S(1)}, bf16[14,16,256]{2,1,0:T(8,128)(2,1)S(1)}, u32[]{:S(2)}, u32[]{:S(2)}) %collective-permute-start.5) | collective-permute-done | bytes 114720 | tf_op jit(solution)/shard_map/ppermute | solution.py:447
  48.1 1.5 %collective-permute-start.7 = (bf16[14,16,256]{2,1,0:T(8,128)(2,1)S(1)}, bf16[14,16,256]{2,1,0:T(8,128)(2,1)S(1)}, u32[]{:S(2)}, u32[]{:S(2)}) collective-permute-start(bf16[14,16,256]{2,1,0:T(8,128)(2,1)S(1)} %add_convert_fusion.mine), channel_id=1, source_target_pairs={{0,16},{16,0},{32,48},{48,32},{64,80},{80,64},{96,112},{112,96},{1... | collective-permute-start | bytes 344072 | tf_op jit(solution)/shard_map/ppermute | solution.py:441
  50.5 0.8 %shard_map.73 = f32[27,16,256]{2,1,0:T(8,128)} custom-call(s32[1]{0:T(128)} %bitcast.4.half, bf16[14,16,256]{2,1,0:T(8,128)(2,1)S(1)} %add_convert_fusion.mine, bf16[14,16,256]{2,1,0:T(8,128)(2,1)S(1)} %collective-permute-done.7.other), custom_call_target="tpu_custom_call" | custom-call | bytes 4000000 | tf_op jit(solution)/shard_map/pallas_call | solution.py:29
  51.3 3.5 %all-to-all-done.1 = bf16[16,224,128]{2,1,0:T(8,128)(2,1)S(1)} async-done(((bf16[16,224,128]{2,1,0:T(8,128)(2,1)}), bf16[16,224,128]{2,1,0:T(8,128)(2,1)S(1)}, u32[]{:S(2)}, u32[]{:S(2)}) %all-to-all-start.1) | async-done | bytes 917536 | tf_op jit(solution)/shard_map/all_to_all | solution.py:458
  55.0 2.8 %collective-permute-start.10 = (bf16[14,16,128]{2,1,0:T(8,128)(2,1)S(1)}, bf16[14,16,128]{2,1,0:T(8,128)(2,1)S(1)}, u32[]{:S(2)}, u32[]{:S(2)}) collective-permute-start(bf16[14,16,128]{2,1,0:T(8,128)(2,1)S(1)} %reduce_sum.12), channel_id=1, source_target_pairs={{0,64},{16,80},{32,96},{48,112},{64,0},{80,16},{96,32},{112,48},{1... | collective-permute-start | bytes 172040 | tf_op jit(solution)/shard_map/ppermute | solution.py:447
  57.8 0.9 %collective-permute-start.9 = (bf16[14,16,128]{2,1,0:T(8,128)(2,1)S(1)}, bf16[14,16,128]{2,1,0:T(8,128)(2,1)S(1)}, u32[]{:S(2)}, u32[]{:S(2)}) collective-permute-start(bf16[14,16,128]{2,1,0:T(8,128)(2,1)S(1)} %reduce_sum.12), channel_id=1, source_target_pairs={{0,96},{16,112},{32,64},{48,80},{64,32},{80,48},{96,0},{112,16},{1... | collective-permute-start | bytes 172040 | tf_op jit(solution)/shard_map/ppermute | solution.py:447
  58.7 0.9 %collective-permute-done.10 = bf16[14,16,128]{2,1,0:T(8,128)(2,1)S(1)} collective-permute-done((bf16[14,16,128]{2,1,0:T(8,128)(2,1)S(1)}, bf16[14,16,128]{2,1,0:T(8,128)(2,1)S(1)}, u32[]{:S(2)}, u32[]{:S(2)}) %collective-permute-start.10) | collective-permute-done | bytes 57376 | tf_op jit(solution)/shard_map/ppermute | solution.py:447
  59.6 2.7 %collective-permute-done.9 = bf16[14,16,128]{2,1,0:T(8,128)(2,1)S(1)} collective-permute-done((bf16[14,16,128]{2,1,0:T(8,128)(2,1)S(1)}, bf16[14,16,128]{2,1,0:T(8,128)(2,1)S(1)}, u32[]{:S(2)}, u32[]{:S(2)}) %collective-permute-start.9) | collective-permute-done | bytes 57376 | tf_op jit(solution)/shard_map/ppermute | solution.py:447
  62.4 2.9 %collective-permute-start.11 = (bf16[14,16,128]{2,1,0:T(8,128)(2,1)S(1)}, bf16[14,16,128]{2,1,0:T(8,128)(2,1)S(1)}, u32[]{:S(2)}, u32[]{:S(2)}) collective-permute-start(bf16[14,16,128]{2,1,0:T(8,128)(2,1)S(1)} %add_convert_fusion.2.mine), channel_id=1, source_target_pairs={{0,16},{16,0},{32,48},{48,32},{64,80},{80,64},{96,112},{112,96},{1... | collective-permute-start | bytes 172040 | tf_op jit(solution)/shard_map/ppermute | solution.py:441
  65.3 0.9 %collective-permute-done.11.other = bf16[14,16,128]{2,1,0:T(8,128)(2,1)S(1)} collective-permute-done((bf16[14,16,128]{2,1,0:T(8,128)(2,1)S(1)}, bf16[14,16,128]{2,1,0:T(8,128)(2,1)S(1)}, u32[]{:S(2)}, u32[]{:S(2)}) %collective-permute-start.11) | collective-permute-done | bytes 57376 | tf_op jit(solution)/shard_map/ppermute | solution.py:441
  (24 shorter events, 3.5 us)
Async XLA Ops:
  0.6 0.9 %copy-start.3 = (bf16[1,2,16,16,128]{4,3,2,1,0:T(8,128)(2,1)S(1)}, bf16[1,2,16,16,128]{4,3,2,1,0:T(8,128)(2,1)}, u32[]{:S(2)}) copy-start(bf16[1,2,16,16,128]{4,3,2,1,0:T(8,128)(2,1)} %param.4) | copy-start | bytes 393220
  1.5 3.6 %copy-start = (bf16[3,3,3,128,256]{4,3,2,1,0:T(8,128)(2,1)S(1)}, bf16[3,3,3,128,256]{4,3,2,1,0:T(8,128)(2,1)}, u32[]{:S(2)}) copy-start(bf16[3,3,3,128,256]{4,3,2,1,0:T(8,128)(2,1)} %param.5) | copy-start | bytes 5308420
  1.5 5.2 %copy-start.1 = (bf16[1,8,4,4,16]{4,3,2,1,0:T(4,128)(2,1)S(1)}, bf16[1,8,4,4,16]{4,3,2,1,0:T(4,128)(2,1)}, u32[]{:S(2)}) copy-start(bf16[1,8,4,4,16]{4,3,2,1,0:T(4,128)(2,1)} %param.7) | copy-start | bytes 12292
  1.6 4.4 %collective-permute-start = (bf16[256,128]{1,0:T(8,128)(2,1)S(1)}, bf16[256,128]{1,0:T(8,128)(2,1)S(1)}, u32[]{:S(2)}, u32[]{:S(2)}) collective-permute-start(bf16[256,128]{1,0:T(8,128)(2,1)S(1)} %get-tuple-element.34), channel_id=1, source_target_pairs={{0,16},{1,2},{2,1},{3,4},{4,3},{5,6},{6,5},{7,8},{8,7},{9,10},{10,... | collective-permute-start | bytes 196616 | tf_op jit(solution)/shard_map/ppermute | solution.py:466
  3.1 3.7 %collective-permute-start.1 = (bf16[256,128]{1,0:T(8,128)(2,1)S(1)}, bf16[256,128]{1,0:T(8,128)(2,1)S(1)}, u32[]{:S(2)}, u32[]{:S(2)}) collective-permute-start(bf16[256,128]{1,0:T(8,128)(2,1)S(1)} %get-tuple-element.35), channel_id=1, source_target_pairs={{0,1},{1,0},{2,3},{3,2},{4,5},{5,4},{6,7},{7,6},{8,9},{9,8},{10,11... | collective-permute-start | bytes 196616 | tf_op jit(solution)/shard_map/ppermute | solution.py:467
  5.1 20.9 %copy-start.2 = (bf16[3,3,3,256,256]{4,3,2,1,0:T(8,128)(2,1)S(1)}, bf16[3,3,3,256,256]{4,3,2,1,0:T(8,128)(2,1)}, u32[]{:S(2)}) copy-start(bf16[3,3,3,256,256]{4,3,2,1,0:T(8,128)(2,1)} %param.6) | copy-start | bytes 10616836
  29.3 5.2 %collective-permute-start.2 = (bf16[16,14,16,128]{3,2,1,0:T(8,128)(2,1)S(1)}, bf16[16,14,16,128]{3,2,1,0:T(8,128)(2,1)S(1)}, u32[]{:S(2)}, u32[]{:S(2)}) collective-permute-start(bf16[16,14,16,128]{3,2,1,0:T(8,128)(2,1)S(1)} %get-tuple-element.53), channel_id=1, source_target_pairs={{0,16},{16,0},{32,48},{48,32},{64,80},{80,64},{96,112},{112,96},{1... | collective-permute-start | bytes 2752520 | tf_op jit(solution)/shard_map/ppermute | solution.py:441
  33.9 2.1 %collective-permute-start.3 = (bf16[14,16,256]{2,1,0:T(8,128)(2,1)S(1)}, bf16[14,16,256]{2,1,0:T(8,128)(2,1)S(1)}, u32[]{:S(2)}, u32[]{:S(2)}) collective-permute-start(bf16[14,16,256]{2,1,0:T(8,128)(2,1)S(1)} %get-tuple-element.55), channel_id=1, source_target_pairs={{0,16},{16,0},{32,48},{48,32},{64,80},{80,64},{96,112},{112,96},{1... | collective-permute-start | bytes 344072 | tf_op jit(solution)/shard_map/ppermute | solution.py:441
  36.0 18.9 %all-to-all-start.1 = ((bf16[16,224,128]{2,1,0:T(8,128)(2,1)}), bf16[16,224,128]{2,1,0:T(8,128)(2,1)S(1)}, u32[]{:S(2)}, u32[]{:S(2)}) async-start(bf16[16,224,128]{2,1,0:T(8,128)(2,1)} %bitcast.6), calls=%async_computation.1 | async-start | bytes 1835008 | tf_op jit(solution)/shard_map/all_to_all | solution.py:458
  39.7 5.9 %collective-permute-start.6 = (bf16[14,16,256]{2,1,0:T(8,128)(2,1)S(1)}, bf16[14,16,256]{2,1,0:T(8,128)(2,1)S(1)}, u32[]{:S(2)}, u32[]{:S(2)}) collective-permute-start(bf16[14,16,256]{2,1,0:T(8,128)(2,1)S(1)} %add_convert_fusion.1), channel_id=1, source_target_pairs={{0,64},{16,80},{32,96},{48,112},{64,0},{80,16},{96,32},{112,48},{1... | collective-permute-start | bytes 344072 | tf_op jit(solution)/shard_map/ppermute | solution.py:447
  42.5 5.4 %collective-permute-start.5 = (bf16[14,16,256]{2,1,0:T(8,128)(2,1)S(1)}, bf16[14,16,256]{2,1,0:T(8,128)(2,1)S(1)}, u32[]{:S(2)}, u32[]{:S(2)}) collective-permute-start(bf16[14,16,256]{2,1,0:T(8,128)(2,1)S(1)} %add_convert_fusion.1), channel_id=1, source_target_pairs={{0,96},{16,112},{32,64},{48,80},{64,32},{80,48},{96,0},{112,16},{1... | collective-permute-start | bytes 344072 | tf_op jit(solution)/shard_map/ppermute | solution.py:447
  43.4 4.6 %collective-permute-start.4 = (bf16[14,16,256]{2,1,0:T(8,128)(2,1)S(1)}, bf16[14,16,256]{2,1,0:T(8,128)(2,1)S(1)}, u32[]{:S(2)}, u32[]{:S(2)}) collective-permute-start(bf16[14,16,256]{2,1,0:T(8,128)(2,1)S(1)} %add_convert_fusion.1), channel_id=1, source_target_pairs={{0,32},{16,48},{32,0},{48,16},{64,96},{80,112},{96,64},{112,80},{1... | collective-permute-start | bytes 344072 | tf_op jit(solution)/shard_map/ppermute | solution.py:447
  48.1 2.4 %collective-permute-start.7 = (bf16[14,16,256]{2,1,0:T(8,128)(2,1)S(1)}, bf16[14,16,256]{2,1,0:T(8,128)(2,1)S(1)}, u32[]{:S(2)}, u32[]{:S(2)}) collective-permute-start(bf16[14,16,256]{2,1,0:T(8,128)(2,1)S(1)} %add_convert_fusion.mine), channel_id=1, source_target_pairs={{0,16},{16,0},{32,48},{48,32},{64,80},{80,64},{96,112},{112,96},{1... | collective-permute-start | bytes 344072 | tf_op jit(solution)/shard_map/ppermute | solution.py:441
  55.0 4.6 %collective-permute-start.10 = (bf16[14,16,128]{2,1,0:T(8,128)(2,1)S(1)}, bf16[14,16,128]{2,1,0:T(8,128)(2,1)S(1)}, u32[]{:S(2)}, u32[]{:S(2)}) collective-permute-start(bf16[14,16,128]{2,1,0:T(8,128)(2,1)S(1)} %reduce_sum.12), channel_id=1, source_target_pairs={{0,64},{16,80},{32,96},{48,112},{64,0},{80,16},{96,32},{112,48},{1... | collective-permute-start | bytes 172040 | tf_op jit(solution)/shard_map/ppermute | solution.py:447
  57.8 4.6 %collective-permute-start.9 = (bf16[14,16,128]{2,1,0:T(8,128)(2,1)S(1)}, bf16[14,16,128]{2,1,0:T(8,128)(2,1)S(1)}, u32[]{:S(2)}, u32[]{:S(2)}) collective-permute-start(bf16[14,16,128]{2,1,0:T(8,128)(2,1)S(1)} %reduce_sum.12), channel_id=1, source_target_pairs={{0,96},{16,112},{32,64},{48,80},{64,32},{80,48},{96,0},{112,16},{1... | collective-permute-start | bytes 172040 | tf_op jit(solution)/shard_map/ppermute | solution.py:447
  58.7 3.7 %collective-permute-start.8 = (bf16[14,16,128]{2,1,0:T(8,128)(2,1)S(1)}, bf16[14,16,128]{2,1,0:T(8,128)(2,1)S(1)}, u32[]{:S(2)}, u32[]{:S(2)}) collective-permute-start(bf16[14,16,128]{2,1,0:T(8,128)(2,1)S(1)} %reduce_sum.12), channel_id=1, source_target_pairs={{0,32},{16,48},{32,0},{48,16},{64,96},{80,112},{96,64},{112,80},{1... | collective-permute-start | bytes 172040 | tf_op jit(solution)/shard_map/ppermute | solution.py:447
  62.4 3.8 %collective-permute-start.11 = (bf16[14,16,128]{2,1,0:T(8,128)(2,1)S(1)}, bf16[14,16,128]{2,1,0:T(8,128)(2,1)S(1)}, u32[]{:S(2)}, u32[]{:S(2)}) collective-permute-start(bf16[14,16,128]{2,1,0:T(8,128)(2,1)S(1)} %add_convert_fusion.2.mine), channel_id=1, source_target_pairs={{0,16},{16,0},{32,48},{48,32},{64,80},{80,64},{96,112},{112,96},{1... | collective-permute-start | bytes 172040 | tf_op jit(solution)/shard_map/ppermute | solution.py:441

commit v11 on v10

--- a/solution.py
+++ b/solution.py
@@ -255,7 +255,7 @@
     ]
 
 
-def half_of_five(first, rows, padded, out, got=None, send=None):
+def half_of_five(first, rows, padded, out):
     for step in range(0, HALF_TAPS, 2):
         taps = [jnp.minimum(first + step + other, 26) for other in range(2)]
         total = jnp.zeros((256, 256), jnp.float32)
@@ -268,11 +268,7 @@
             )
         for other in range(2):
             part = total[:, other * 128 : (other + 1) * 128]
-            if got is not None:
-                part += got[:, step + other].reshape(256, 128).astype(jnp.float32)
-            out[:, step + other] = part.astype(jnp.bfloat16).reshape(16, 16, 128)
-        if send is not None:
-            send(step)
+            out[:, step + other] = part.astype(out.dtype).reshape(16, 16, 128)
 
 
 def back_kernel(
@@ -297,32 +293,38 @@
     )
 
 
-def mine_kernel(half, rows, padded, got, mine, staged, marks):
+def mine_kernel(half, rows, padded, mine):
+    half_of_five(half[0] * HALF_TAPS, rows, padded, mine)
+
+
+def mine_of_five(rows, padded, half):
+    return call(
+        mine_kernel,
+        shape((16, HALF_TAPS, 16, 128), jnp.float32),
+        [],
+        (rows, padded),
+        (half,),
+        flops=900_000_000,
+    )
+
+
+def pair_kernel(mine, got, out, staged, marks):
     sends = []
-
-    def send(step):
-        pair = pl.ds(step, 2)
-        sends.append(
-            pltpu.make_async_copy(staged.at[:, pair], mine.at[:, pair], marks.at[step // 2])
-        )
+    for group in range(4):
+        part = pl.ds(group * 4, 4)
+        staged[part] = (mine[part] + got[part].astype(jnp.float32)).astype(jnp.bfloat16)
+        sends.append(pltpu.make_async_copy(staged.at[part], out.at[part], marks.at[group]))
         sends[-1].start()
-
-    half_of_five(half[0] * HALF_TAPS, rows, padded, staged, got, send)
     for copy in sends:
         copy.wait()
 
 
-def mine_of_five(rows, padded, got, half):
-    return call(
-        mine_kernel,
-        shape((16, HALF_TAPS, 16, 128), jnp.bfloat16),
-        [
-            VMEM((16, HALF_TAPS, 16, 128), jnp.bfloat16),
-            pltpu.SemaphoreType.DMA((HALF_TAPS // 2,)),
-        ],
-        (rows, padded, got),
-        (half,),
-        flops=900_000_000,
+def pair_of_five(mine, got):
+    return call(
+        pair_kernel,
+        shape(got.shape, jnp.bfloat16),
+        [VMEM(got.shape, jnp.bfloat16), pltpu.SemaphoreType.DMA((4,))],
+        (mine, got),
         far_out=True,
     )
 
@@ -478,18 +480,22 @@
     rows, theirs_five, own = back_five(gathered, kernel_six, slope, padded, position, half)
     got_five = core_swap(theirs_five)
     next_rows, mine_six, theirs_six = six_own(gathered, own, position, half)
+    mine_five = mine_of_five(rows, padded, half)
+    got_five, mine_five, theirs_six, mine_six, next_rows = lax.optimization_barrier(
+        (got_five, mine_five, theirs_six, mine_six, next_rows)
+    )
+    pair_five = pair_of_five(mine_five, got_five)
+    pair_five, theirs_six, mine_six, next_rows = lax.optimization_barrier(
+        (pair_five, theirs_six, mine_six, next_rows)
+    )
     got_six = core_swap(theirs_six)
-    pair_five = mine_of_five(rows, padded, got_five, half)
-    pair_five, got_six, mine_six, next_rows = lax.optimization_barrier(
-        (pair_five, got_six, mine_six, next_rows)
-    )
     pair_six = (mine_six.astype(jnp.float32) + got_six.astype(jnp.float32)).astype(jnp.bfloat16)
     chips_six = from_chips(pair_six)
     spread = exchange(pair_five)
     total_six = sum_of_chips(pair_six, chips_six)
     out_six = both_halves(half, total_six, core_swap(total_six))
     next_input = next_rows.T.reshape(1, 8, 4, 4, 16)
-    spread, out_six, next_input = lax.optimization_barrier((spread, out_six, next_input))
+    spread, out_six = lax.optimization_barrier((spread, out_six))
     depth_five = spread.astype(jnp.float32).sum(0).astype(jnp.bfloat16)
     total_five = sum_of_chips(depth_five, from_chips(depth_five))
     out_five = both_halves(half, total_five, core_swap(total_five))

time: 67.1 us -> 67 us (level)
    all_to_all x1, waiting for transfers between devices: 3.55 us -> 2.46 us  [exchange(): got = lax.all_to_all(flat, 'wide', split_axis=0, concat_axis=0, tiled=True)]
    pallas_call x8 -> x9, Pallas kernels: 9.53 us -> 9.72 us  [call(): pl.pallas_call(body, out_shape=out_shape, in_specs=specs, out_specs=outs,...]
  transfers between devices with their start and end apart: 13 -> 13, of which waited for: 10 -> 11; matrix products, arithmetic and copies ran while one was open for 1% -> 1% of each run, Pallas kernels for 7% -> 6%
where the time goes in v11:
time: 67 us; the launch traced here: 66.8 us
  starting transfers between devices  22.1 us (33%)
  blocking collectives  18.5 us (28%)
  waiting for transfers between devices  13.7 us (20%)
  Pallas kernels  9.72 us (15%)
  local copies, waits for them, and re-layouts  1.63 us (2%)
  between operations  0.75 us (1%)
    all_to_all x1, blocking collectives, exchange(): got = lax.all_to_all(flat, 'wide', split_axis=0, concat_axis=0, tiled=True)  18.5 us
    pallas_call x9, Pallas kernels, call(): pl.pallas_call(body, out_shape=out_shape, in_specs=specs, out_specs=outs,...  9.72 us
    ppermute x6, waiting for transfers between devices, from_chips(): lax.ppermute(values, 'dp', [(i, i ^ step) for i in range(count)])  8.3 us
    ppermute x4, starting transfers between devices, core_swap(): return lax.ppermute(values, 'dp', [(i, i ^ 1) for i in range(count)])  7.61 us
    ppermute x6, starting transfers between devices, from_chips(): lax.ppermute(values, 'dp', [(i, i ^ step) for i in range(count)])  7.35 us
    all_to_all x1, starting transfers between devices, exchange(): got = lax.all_to_all(flat, 'wide', split_axis=0, concat_axis=0, tiled=True)  3.65 us
    all_to_all x1, waiting for transfers between devices, exchange(): got = lax.all_to_all(flat, 'wide', split_axis=0, concat_axis=0, tiled=True)  2.46 us
    ppermute x4, waiting for transfers between devices, core_swap(): return lax.ppermute(values, 'dp', [(i, i ^ 1) for i in range(count)])  2.19 us
  transfers between devices with their start and end apart: 13, of which 11 were waited for; matrix products, arithmetic and copies ran while one was open for 1% of the time, Pallas kernels for 6%

profile of v11, /device:TPU:1, one launch (start us, length us, event | category | flops | bytes accessed | tf_op | source)
XLA Modules:
  0.0 66.8 jit_solution(5174017823375566299)
XLA Ops:
  0.6 0.9 %copy-done.3 = bf16[1,2,16,16,128]{4,3,2,1,0:T(8,128)(2,1)S(1)} copy-done((bf16[1,2,16,16,128]{4,3,2,1,0:T(8,128)(2,1)S(1)}, bf16[1,2,16,16,128]{4,3,2,1,0:T(8,128)(2,1)}, u32[]{:S(2)}) %copy-start.3) | copy-done | bytes 131096
  1.6 1.5 %collective-permute-start = (bf16[256,128]{1,0:T(8,128)(2,1)S(1)}, bf16[256,128]{1,0:T(8,128)(2,1)S(1)}, u32[]{:S(2)}, u32[]{:S(2)}) collective-permute-start(bf16[256,128]{1,0:T(8,128)(2,1)S(1)} %get-tuple-element.38), channel_id=1, source_target_pairs={{0,16},{1,2},{2,1},{3,4},{4,3},{5,6},{6,5},{7,8},{8,7},{9,10},{10,... | collective-permute-start | bytes 196616 | tf_op jit(solution)/shard_map/ppermute | solution.py:468
  3.1 2.0 %collective-permute-start.1 = (bf16[256,128]{1,0:T(8,128)(2,1)S(1)}, bf16[256,128]{1,0:T(8,128)(2,1)S(1)}, u32[]{:S(2)}, u32[]{:S(2)}) collective-permute-start(bf16[256,128]{1,0:T(8,128)(2,1)S(1)} %get-tuple-element.39), channel_id=1, source_target_pairs={{0,1},{1,0},{2,3},{3,2},{4,5},{5,4},{6,7},{7,6},{8,9},{9,8},{10,11... | collective-permute-start | bytes 196616 | tf_op jit(solution)/shard_map/ppermute | solution.py:469
  5.1 0.8 %shard_map.68 = (f32[512,256]{1,0:T(8,128)S(1)}, bf16[2,288,384]{2,1,0:T(8,128)(2,1)S(1)}) custom-call(bf16[2,256,128]{2,1,0:T(8,128)(2,1)S(1)} %get-tuple-element.40.slab, bf16[3456,256]{1,0:T(8,128)(2,1)S(1)} %bitcast.16), custom_call_target="tpu_custom_call" | custom-call | flops 600000000 | bytes 4000000 | tf_op jit(solution)/shard_map/pallas_call | solution.py:29
  7.6 18.5 %all_to_all.10.gathered = bf16[16,144,128]{2,1,0:T(8,128)(2,1)S(1)} all-to-all(bf16[16,144,128]{2,1,0:T(8,128)(2,1)S(1)} %get-tuple-element.46), channel_id=1, replica_groups=mesh['dp'=8,'wide'=16] {'wide'}, dimensions={0} | all-to-all | bytes 1179648 | tf_op jit(solution)/shard_map/all_to_all | solution.py:460
  26.1 3.3 %shard_map.70 = (bf16[256,512]{1,0:T(8,128)(2,1)S(1)}, bf16[16,14,16,128]{3,2,1,0:T(8,128)(2,1)S(1)}, bf16[27,16,256]{2,1,0:T(8,128)(2,1)S(1)}) custom-call(s32[1]{0:T(128)} %bitcast.position, s32[1]{0:T(128)} %bitcast.4.half, bf16[16,144,128]{2,1,0:T(8,128)(2,1)S(1)} %all_to_all.10.gathered, bf16[27,256,256]{2,1,0:T(8,128)(2,1)S(1)} %bitcast.20, ...), custom_call_target="tpu_custom_call" | custom-call | flops 3000000000 | bytes 4000000 | tf_op jit(solution)/shard_map/pallas_call | solution.py:29
  29.4 3.1 %collective-permute-start.2 = (bf16[16,14,16,128]{3,2,1,0:T(8,128)(2,1)S(1)}, bf16[16,14,16,128]{3,2,1,0:T(8,128)(2,1)S(1)}, u32[]{:S(2)}, u32[]{:S(2)}) collective-permute-start(bf16[16,14,16,128]{3,2,1,0:T(8,128)(2,1)S(1)} %get-tuple-element.56), channel_id=1, source_target_pairs={{0,16},{16,0},{32,48},{48,32},{64,80},{80,64},{96,112},{112,96},{1... | collective-permute-start | bytes 2752520 | tf_op jit(solution)/shard_map/ppermute | solution.py:443
  33.2 1.5 %shard_map.72 = (bf16[16,128]{1,0:T(8,128)(2,1)S(1)}, bf16[14,16,256]{2,1,0:T(8,128)(2,1)S(1)}, bf16[14,16,256]{2,1,0:T(8,128)(2,1)S(1)}) custom-call(s32[1]{0:T(128)} %bitcast.position, s32[1]{0:T(128)} %bitcast.4.half, bf16[16,144,128]{2,1,0:T(8,128)(2,1)S(1)} %all_to_all.10.gathered, bf16[27,16,256]{2,1,0:T(8,128)(2,1)S(1)} %get-tuple-element.58.own), custom_call_target="tpu_custom_call" | custom-call | flops 2000000000 | bytes 4000000 | tf_op jit(solution)/shard_map/pallas_call | solution.py:29
  34.8 1.0 %shard_map.73 = bf16[16,14,16,128]{3,2,1,0:T(8,128)(2,1)} custom-call(f32[16,14,16,128]{3,2,1,0:T(8,128)S(1)} %shard_map.71.mine, bf16[16,14,16,128]{3,2,1,0:T(8,128)(2,1)S(1)} %collective-permute-done.2.got), custom_call_target="tpu_custom_call" | custom-call | bytes 4000000 | tf_op jit(solution)/shard_map/pallas_call | solution.py:29
  35.8 3.6 %all-to-all-start.1 = ((bf16[16,224,128]{2,1,0:T(8,128)(2,1)}), bf16[16,224,128]{2,1,0:T(8,128)(2,1)S(1)}, u32[]{:S(2)}, u32[]{:S(2)}) async-start(bf16[16,224,128]{2,1,0:T(8,128)(2,1)} %bitcast.8), calls=%async_computation.1 | async-start | bytes 1835008 | tf_op jit(solution)/shard_map/all_to_all | solution.py:460
  39.8 1.1 %collective-permute-done.3 = bf16[14,16,256]{2,1,0:T(8,128)(2,1)S(1)} collective-permute-done((bf16[14,16,256]{2,1,0:T(8,128)(2,1)S(1)}, bf16[14,16,256]{2,1,0:T(8,128)(2,1)S(1)}, u32[]{:S(2)}, u32[]{:S(2)}) %collective-permute-start.3) | collective-permute-done | bytes 114720 | tf_op jit(solution)/shard_map/ppermute | solution.py:443
  40.9 2.8 %collective-permute-start.6 = (bf16[14,16,256]{2,1,0:T(8,128)(2,1)S(1)}, bf16[14,16,256]{2,1,0:T(8,128)(2,1)S(1)}, u32[]{:S(2)}, u32[]{:S(2)}) collective-permute-start(bf16[14,16,256]{2,1,0:T(8,128)(2,1)S(1)} %add_convert_fusion.1), channel_id=1, source_target_pairs={{0,64},{16,80},{32,96},{48,112},{64,0},{80,16},{96,32},{112,48},{1... | collective-permute-start | bytes 344072 | tf_op jit(solution)/shard_map/ppermute | solution.py:449
  43.7 0.9 %collective-permute-start.5 = (bf16[14,16,256]{2,1,0:T(8,128)(2,1)S(1)}, bf16[14,16,256]{2,1,0:T(8,128)(2,1)S(1)}, u32[]{:S(2)}, u32[]{:S(2)}) collective-permute-start(bf16[14,16,256]{2,1,0:T(8,128)(2,1)S(1)} %add_convert_fusion.1), channel_id=1, source_target_pairs={{0,96},{16,112},{32,64},{48,80},{64,32},{80,48},{96,0},{112,16},{1... | collective-permute-start | bytes 344072 | tf_op jit(solution)/shard_map/ppermute | solution.py:449
  44.5 2.4 %collective-permute-done.6 = bf16[14,16,256]{2,1,0:T(8,128)(2,1)S(1)} collective-permute-done((bf16[14,16,256]{2,1,0:T(8,128)(2,1)S(1)}, bf16[14,16,256]{2,1,0:T(8,128)(2,1)S(1)}, u32[]{:S(2)}, u32[]{:S(2)}) %collective-permute-start.6) | collective-permute-done | bytes 114720 | tf_op jit(solution)/shard_map/ppermute | solution.py:449
  46.9 2.1 %collective-permute-done.5 = bf16[14,16,256]{2,1,0:T(8,128)(2,1)S(1)} collective-permute-done((bf16[14,16,256]{2,1,0:T(8,128)(2,1)S(1)}, bf16[14,16,256]{2,1,0:T(8,128)(2,1)S(1)}, u32[]{:S(2)}, u32[]{:S(2)}) %collective-permute-start.5) | collective-permute-done | bytes 114720 | tf_op jit(solution)/shard_map/ppermute | solution.py:449
  49.3 1.4 %collective-permute-start.7 = (bf16[14,16,256]{2,1,0:T(8,128)(2,1)S(1)}, bf16[14,16,256]{2,1,0:T(8,128)(2,1)S(1)}, u32[]{:S(2)}, u32[]{:S(2)}) collective-permute-start(bf16[14,16,256]{2,1,0:T(8,128)(2,1)S(1)} %add_convert_fusion.mine), channel_id=1, source_target_pairs={{0,16},{16,0},{32,48},{48,32},{64,80},{80,64},{96,112},{112,96},{1... | collective-permute-start | bytes 344072 | tf_op jit(solution)/shard_map/ppermute | solution.py:443
  50.7 1.0 %collective-permute-done.7.other = bf16[14,16,256]{2,1,0:T(8,128)(2,1)S(1)} collective-permute-done((bf16[14,16,256]{2,1,0:T(8,128)(2,1)S(1)}, bf16[14,16,256]{2,1,0:T(8,128)(2,1)S(1)}, u32[]{:S(2)}, u32[]{:S(2)}) %collective-permute-start.7) | collective-permute-done | bytes 114720 | tf_op jit(solution)/shard_map/ppermute | solution.py:443
  51.7 0.8 %shard_map.74 = f32[27,16,256]{2,1,0:T(8,128)} custom-call(s32[1]{0:T(128)} %bitcast.4.half, bf16[14,16,256]{2,1,0:T(8,128)(2,1)S(1)} %add_convert_fusion.mine, bf16[14,16,256]{2,1,0:T(8,128)(2,1)S(1)} %collective-permute-done.7.other), custom_call_target="tpu_custom_call" | custom-call | bytes 4000000 | tf_op jit(solution)/shard_map/pallas_call | solution.py:29
  52.5 2.5 %all-to-all-done.1 = bf16[16,224,128]{2,1,0:T(8,128)(2,1)S(1)} async-done(((bf16[16,224,128]{2,1,0:T(8,128)(2,1)}), bf16[16,224,128]{2,1,0:T(8,128)(2,1)S(1)}, u32[]{:S(2)}, u32[]{:S(2)}) %all-to-all-start.1) | async-done | bytes 917536 | tf_op jit(solution)/shard_map/all_to_all | solution.py:460
  55.1 2.8 %collective-permute-start.10 = (bf16[14,16,128]{2,1,0:T(8,128)(2,1)S(1)}, bf16[14,16,128]{2,1,0:T(8,128)(2,1)S(1)}, u32[]{:S(2)}, u32[]{:S(2)}) collective-permute-start(bf16[14,16,128]{2,1,0:T(8,128)(2,1)S(1)} %reduce_sum.12), channel_id=1, source_target_pairs={{0,64},{16,80},{32,96},{48,112},{64,0},{80,16},{96,32},{112,48},{1... | collective-permute-start | bytes 172040 | tf_op jit(solution)/shard_map/ppermute | solution.py:449
  57.9 0.9 %collective-permute-start.9 = (bf16[14,16,128]{2,1,0:T(8,128)(2,1)S(1)}, bf16[14,16,128]{2,1,0:T(8,128)(2,1)S(1)}, u32[]{:S(2)}, u32[]{:S(2)}) collective-permute-start(bf16[14,16,128]{2,1,0:T(8,128)(2,1)S(1)} %reduce_sum.12), channel_id=1, source_target_pairs={{0,96},{16,112},{32,64},{48,80},{64,32},{80,48},{96,0},{112,16},{1... | collective-permute-start | bytes 172040 | tf_op jit(solution)/shard_map/ppermute | solution.py:449
  58.7 0.9 %collective-permute-done.10 = bf16[14,16,128]{2,1,0:T(8,128)(2,1)S(1)} collective-permute-done((bf16[14,16,128]{2,1,0:T(8,128)(2,1)S(1)}, bf16[14,16,128]{2,1,0:T(8,128)(2,1)S(1)}, u32[]{:S(2)}, u32[]{:S(2)}) %collective-permute-start.10) | collective-permute-done | bytes 57376 | tf_op jit(solution)/shard_map/ppermute | solution.py:449
  59.7 2.5 %collective-permute-done.9 = bf16[14,16,128]{2,1,0:T(8,128)(2,1)S(1)} collective-permute-done((bf16[14,16,128]{2,1,0:T(8,128)(2,1)S(1)}, bf16[14,16,128]{2,1,0:T(8,128)(2,1)S(1)}, u32[]{:S(2)}, u32[]{:S(2)}) %collective-permute-start.9) | collective-permute-done | bytes 57376 | tf_op jit(solution)/shard_map/ppermute | solution.py:449
  62.3 2.8 %collective-permute-start.11 = (bf16[14,16,128]{2,1,0:T(8,128)(2,1)S(1)}, bf16[14,16,128]{2,1,0:T(8,128)(2,1)S(1)}, u32[]{:S(2)}, u32[]{:S(2)}) collective-permute-start(bf16[14,16,128]{2,1,0:T(8,128)(2,1)S(1)} %add_convert_fusion.2.mine), channel_id=1, source_target_pairs={{0,16},{16,0},{32,48},{48,32},{64,80},{80,64},{96,112},{112,96},{1... | collective-permute-start | bytes 172040 | tf_op jit(solution)/shard_map/ppermute | solution.py:443
  (25 shorter events, 4.9 us)
Async XLA Ops:
  0.6 0.9 %copy-start.3 = (bf16[1,2,16,16,128]{4,3,2,1,0:T(8,128)(2,1)S(1)}, bf16[1,2,16,16,128]{4,3,2,1,0:T(8,128)(2,1)}, u32[]{:S(2)}) copy-start(bf16[1,2,16,16,128]{4,3,2,1,0:T(8,128)(2,1)} %param.4) | copy-start | bytes 393220
  1.5 3.6 %copy-start = (bf16[3,3,3,128,256]{4,3,2,1,0:T(8,128)(2,1)S(1)}, bf16[3,3,3,128,256]{4,3,2,1,0:T(8,128)(2,1)}, u32[]{:S(2)}) copy-start(bf16[3,3,3,128,256]{4,3,2,1,0:T(8,128)(2,1)} %param.5) | copy-start | bytes 5308420
  1.6 5.2 %copy-start.1 = (bf16[1,8,4,4,16]{4,3,2,1,0:T(4,128)(2,1)S(1)}, bf16[1,8,4,4,16]{4,3,2,1,0:T(4,128)(2,1)}, u32[]{:S(2)}) copy-start(bf16[1,8,4,4,16]{4,3,2,1,0:T(4,128)(2,1)} %param.7) | copy-start | bytes 12292
  1.6 4.4 %collective-permute-start = (bf16[256,128]{1,0:T(8,128)(2,1)S(1)}, bf16[256,128]{1,0:T(8,128)(2,1)S(1)}, u32[]{:S(2)}, u32[]{:S(2)}) collective-permute-start(bf16[256,128]{1,0:T(8,128)(2,1)S(1)} %get-tuple-element.38), channel_id=1, source_target_pairs={{0,16},{1,2},{2,1},{3,4},{4,3},{5,6},{6,5},{7,8},{8,7},{9,10},{10,... | collective-permute-start | bytes 196616 | tf_op jit(solution)/shard_map/ppermute | solution.py:468
  3.1 3.7 %collective-permute-start.1 = (bf16[256,128]{1,0:T(8,128)(2,1)S(1)}, bf16[256,128]{1,0:T(8,128)(2,1)S(1)}, u32[]{:S(2)}, u32[]{:S(2)}) collective-permute-start(bf16[256,128]{1,0:T(8,128)(2,1)S(1)} %get-tuple-element.39), channel_id=1, source_target_pairs={{0,1},{1,0},{2,3},{3,2},{4,5},{5,4},{6,7},{7,6},{8,9},{9,8},{10,11... | collective-permute-start | bytes 196616 | tf_op jit(solution)/shard_map/ppermute | solution.py:469
  6.8 19.4 %copy-start.2 = (bf16[3,3,3,256,256]{4,3,2,1,0:T(8,128)(2,1)S(1)}, bf16[3,3,3,256,256]{4,3,2,1,0:T(8,128)(2,1)}, u32[]{:S(2)}) copy-start(bf16[3,3,3,256,256]{4,3,2,1,0:T(8,128)(2,1)} %param.6) | copy-start | bytes 10616836
  29.4 5.3 %collective-permute-start.2 = (bf16[16,14,16,128]{3,2,1,0:T(8,128)(2,1)S(1)}, bf16[16,14,16,128]{3,2,1,0:T(8,128)(2,1)S(1)}, u32[]{:S(2)}, u32[]{:S(2)}) collective-permute-start(bf16[16,14,16,128]{3,2,1,0:T(8,128)(2,1)S(1)} %get-tuple-element.56), channel_id=1, source_target_pairs={{0,16},{16,0},{32,48},{48,32},{64,80},{80,64},{96,112},{112,96},{1... | collective-permute-start | bytes 2752520 | tf_op jit(solution)/shard_map/ppermute | solution.py:443
  35.8 19.2 %all-to-all-start.1 = ((bf16[16,224,128]{2,1,0:T(8,128)(2,1)}), bf16[16,224,128]{2,1,0:T(8,128)(2,1)S(1)}, u32[]{:S(2)}, u32[]{:S(2)}) async-start(bf16[16,224,128]{2,1,0:T(8,128)(2,1)} %bitcast.8), calls=%async_computation.1 | async-start | bytes 1835008 | tf_op jit(solution)/shard_map/all_to_all | solution.py:460
  39.4 1.4 %collective-permute-start.3 = (bf16[14,16,256]{2,1,0:T(8,128)(2,1)S(1)}, bf16[14,16,256]{2,1,0:T(8,128)(2,1)S(1)}, u32[]{:S(2)}, u32[]{:S(2)}) collective-permute-start(bf16[14,16,256]{2,1,0:T(8,128)(2,1)S(1)} %get-tuple-element.70), channel_id=1, source_target_pairs={{0,16},{16,0},{32,48},{48,32},{64,80},{80,64},{96,112},{112,96},{1... | collective-permute-start | bytes 344072 | tf_op jit(solution)/shard_map/ppermute | solution.py:443
  40.9 6.1 %collective-permute-start.6 = (bf16[14,16,256]{2,1,0:T(8,128)(2,1)S(1)}, bf16[14,16,256]{2,1,0:T(8,128)(2,1)S(1)}, u32[]{:S(2)}, u32[]{:S(2)}) collective-permute-start(bf16[14,16,256]{2,1,0:T(8,128)(2,1)S(1)} %add_convert_fusion.1), channel_id=1, source_target_pairs={{0,64},{16,80},{32,96},{48,112},{64,0},{80,16},{96,32},{112,48},{1... | collective-permute-start | bytes 344072 | tf_op jit(solution)/shard_map/ppermute | solution.py:449
  43.7 5.4 %collective-permute-start.5 = (bf16[14,16,256]{2,1,0:T(8,128)(2,1)S(1)}, bf16[14,16,256]{2,1,0:T(8,128)(2,1)S(1)}, u32[]{:S(2)}, u32[]{:S(2)}) collective-permute-start(bf16[14,16,256]{2,1,0:T(8,128)(2,1)S(1)} %add_convert_fusion.1), channel_id=1, source_target_pairs={{0,96},{16,112},{32,64},{48,80},{64,32},{80,48},{96,0},{112,16},{1... | collective-permute-start | bytes 344072 | tf_op jit(solution)/shard_map/ppermute | solution.py:449
  44.5 4.7 %collective-permute-start.4 = (bf16[14,16,256]{2,1,0:T(8,128)(2,1)S(1)}, bf16[14,16,256]{2,1,0:T(8,128)(2,1)S(1)}, u32[]{:S(2)}, u32[]{:S(2)}) collective-permute-start(bf16[14,16,256]{2,1,0:T(8,128)(2,1)S(1)} %add_convert_fusion.1), channel_id=1, source_target_pairs={{0,32},{16,48},{32,0},{48,16},{64,96},{80,112},{96,64},{112,80},{1... | collective-permute-start | bytes 344072 | tf_op jit(solution)/shard_map/ppermute | solution.py:449
  49.3 2.3 %collective-permute-start.7 = (bf16[14,16,256]{2,1,0:T(8,128)(2,1)S(1)}, bf16[14,16,256]{2,1,0:T(8,128)(2,1)S(1)}, u32[]{:S(2)}, u32[]{:S(2)}) collective-permute-start(bf16[14,16,256]{2,1,0:T(8,128)(2,1)S(1)} %add_convert_fusion.mine), channel_id=1, source_target_pairs={{0,16},{16,0},{32,48},{48,32},{64,80},{80,64},{96,112},{112,96},{1... | collective-permute-start | bytes 344072 | tf_op jit(solution)/shard_map/ppermute | solution.py:443
  55.1 4.6 %collective-permute-start.10 = (bf16[14,16,128]{2,1,0:T(8,128)(2,1)S(1)}, bf16[14,16,128]{2,1,0:T(8,128)(2,1)S(1)}, u32[]{:S(2)}, u32[]{:S(2)}) collective-permute-start(bf16[14,16,128]{2,1,0:T(8,128)(2,1)S(1)} %reduce_sum.12), channel_id=1, source_target_pairs={{0,64},{16,80},{32,96},{48,112},{64,0},{80,16},{96,32},{112,48},{1... | collective-permute-start | bytes 172040 | tf_op jit(solution)/shard_map/ppermute | solution.py:449
  57.9 4.3 %collective-permute-start.9 = (bf16[14,16,128]{2,1,0:T(8,128)(2,1)S(1)}, bf16[14,16,128]{2,1,0:T(8,128)(2,1)S(1)}, u32[]{:S(2)}, u32[]{:S(2)}) collective-permute-start(bf16[14,16,128]{2,1,0:T(8,128)(2,1)S(1)} %reduce_sum.12), channel_id=1, source_target_pairs={{0,96},{16,112},{32,64},{48,80},{64,32},{80,48},{96,0},{112,16},{1... | collective-permute-start | bytes 172040 | tf_op jit(solution)/shard_map/ppermute | solution.py:449
  58.7 3.6 %collective-permute-start.8 = (bf16[14,16,128]{2,1,0:T(8,128)(2,1)S(1)}, bf16[14,16,128]{2,1,0:T(8,128)(2,1)S(1)}, u32[]{:S(2)}, u32[]{:S(2)}) collective-permute-start(bf16[14,16,128]{2,1,0:T(8,128)(2,1)S(1)} %reduce_sum.12), channel_id=1, source_target_pairs={{0,32},{16,48},{32,0},{48,16},{64,96},{80,112},{96,64},{112,80},{1... | collective-permute-start | bytes 172040 | tf_op jit(solution)/shard_map/ppermute | solution.py:449
  62.3 3.7 %collective-permute-start.11 = (bf16[14,16,128]{2,1,0:T(8,128)(2,1)S(1)}, bf16[14,16,128]{2,1,0:T(8,128)(2,1)S(1)}, u32[]{:S(2)}, u32[]{:S(2)}) collective-permute-start(bf16[14,16,128]{2,1,0:T(8,128)(2,1)S(1)} %add_convert_fusion.2.mine), channel_id=1, source_target_pairs={{0,16},{16,0},{32,48},{48,32},{64,80},{80,64},{96,112},{112,96},{1... | collective-permute-start | bytes 172040 | tf_op jit(solution)/shard_map/ppermute | solution.py:443
